TPU v7x, 32 devices: a whole 2x2x4 slice. The times are simulated.
32 devices in a mesh: groups: 2 (over y), req: 4 (over x, core), tp: 4 (over z).
Axes of the slice: x: 2, y: 2, z: 4, core: 2. Of those that a mesh axis runs over, the one named last changes fastest.
Arguments:
- tokens: bfloat16 [4096, 8192], P(('groups', 'req'), 'tp'), parts along dimension 0, may hold values from -6 to 6
- norm_gain: bfloat16 [8192], replicated, may hold values from 0.25 to 1.75
- w_query: bfloat16 [8192, 4096], P(None, 'tp'), may hold values from -0.0625 to 0.0625
- key_weight: bfloat16 [8192, 1024], P(None, 'tp'), may hold values from -0.0625 to 0.0625
- value_weight: bfloat16 [8192, 1024], P(None, 'tp'), may hold values from -0.0625 to 0.0625
- lengths: int32 [8], P('groups'), parts along dimension 0, may hold values from 1 to 512, 1024 in all
- plan: int32 [32], P('groups'), parts along dimension 0, may hold values from 0 to 15, as said below
Outputs:
- attended: bfloat16 [4096, 4096], P(('groups', 'req'), 'tp'), parts along dimension 0
- cache: bfloat16 [2, 4096, 1024], P(None, ('groups', 'req'), 'tp'), parts along dimension 1
There are 2 independent parts, one for each index of `groups`. A program takes and returns all parts, laid end to end along the dimension named above; an argument that names none is the same for every part. Nothing has to cross between parts.
Inputs may be any that keep to these rules, and one draw needn't show every extreme that they name: lengths: the longest request is exactly 512. plan is a permutation of the spans 0 to 15; span g is request g // 4 at positions (g % 4) * 128 onward; slot k belongs to worker k // 4; the 4 spans of one request go to 4 different workers.
All inputs are finite; a program needn't handle non-finite values.
Results may differ from a plain program's by a relative error of at most 0.008.
Values may be sent and summed in bfloat16 or wider, within the bound.
No kernel may reach another device: no remote copies, remote signals or barrier semaphores. Data moves between devices by JAX's collectives and lax.ppermute only.
A program may use at most 128 MiB of HBM per device.

v0:
```python
import math

import jax
import jax.numpy as jnp
from jax import lax
from jax.sharding import PartitionSpec as P

HEAD_SIZE = 128
SPAN = 128


def rotate(values, positions, width):
    shaped = values.reshape(values.shape[0], -1, width)
    halfway = width // 2
    frequency = jnp.exp(
        -(jnp.arange(halfway).astype(jnp.float32) * 2.0 / width) * math.log(500000.0)
    )
    angles = positions.astype(jnp.float32)[:, None] * frequency[None, :]
    cosines = jnp.cos(angles)[:, None, :]
    sinusoid = jnp.sin(angles)[:, None, :]
    lower_half = shaped[..., :halfway]
    upper_half = shaped[..., halfway:]
    turned = jnp.concatenate(
        [
            lower_half * cosines - upper_half * sinusoid,
            upper_half * cosines + lower_half * sinusoid,
        ],
        -1,
    )
    return turned.reshape(values.shape)


def attend_span(queries, key_rows, value_rows, first_pos, length):
    count = queries.shape[0]
    key_value_heads = key_rows.shape[1] // HEAD_SIZE
    per_group = queries.shape[1] // HEAD_SIZE // key_value_heads
    query_view = queries.reshape(count, key_value_heads, per_group, HEAD_SIZE)
    key_view = key_rows.reshape(-1, key_value_heads, HEAD_SIZE)
    value_view = value_rows.reshape(-1, key_value_heads, HEAD_SIZE)
    scores = jnp.einsum(
        "ckgd,lkd->kgcl", query_view, key_view, preferred_element_type=jnp.float32
    ) / math.sqrt(HEAD_SIZE)
    query_pos = first_pos + jnp.arange(count)
    key_pos = jnp.arange(key_view.shape[0])
    allowed = (key_pos[None, :] <= query_pos[:, None]) & (key_pos[None, :] < length)
    scores = jnp.where(allowed, scores, -1e30)
    weights = jax.nn.softmax(scores, axis=-1).astype(jnp.bfloat16)
    mixed = jnp.einsum("kgcl,lkd->ckgd", weights, value_view, preferred_element_type=jnp.float32)
    mixed = jnp.where((query_pos < length)[:, None, None, None], mixed, 0.0)
    return mixed.reshape(count, -1).astype(jnp.bfloat16)


def local(tokens, norm_gain, w_query, key_weight, value_weight, lengths, plan):
    gathered = lax.all_gather(tokens, "tp", axis=1, tiled=True)
    wide = gathered.astype(jnp.float32)
    scale = lax.rsqrt(jnp.mean(wide * wide, axis=-1, keepdims=True) + 1e-05)
    normed = (wide * scale * norm_gain.astype(jnp.float32)).astype(jnp.bfloat16)
    slots = tokens.shape[0]
    per_home = slots // SPAN
    home_index = lax.axis_index("req")
    length = lengths[home_index]
    positions = jnp.arange(slots)
    live = (positions < length)[:, None]
    queries = rotate(
        jnp.dot(normed, w_query, preferred_element_type=jnp.float32), positions, HEAD_SIZE
    ).astype(jnp.bfloat16)
    key_rows = jnp.where(
        live,
        rotate(
            jnp.dot(normed, key_weight, preferred_element_type=jnp.float32), positions, HEAD_SIZE
        ),
        0.0,
    ).astype(jnp.bfloat16)
    value_rows = jnp.where(
        live, jnp.dot(normed, value_weight, preferred_element_type=jnp.float32), 0.0
    ).astype(jnp.bfloat16)
    cache = jnp.stack([key_rows, value_rows])
    pieces = []
    all_queries, all_keys, all_values = (
        lax.all_gather(queries, "req", axis=0, tiled=True),
        lax.all_gather(key_rows, "req", axis=0, tiled=True),
        lax.all_gather(value_rows, "req", axis=0, tiled=True),
    )
    for slot_index in range(per_home):
        span_id = plan[home_index * per_home + slot_index]
        source = span_id // per_home
        offset = span_id % per_home * SPAN
        span_queries = lax.dynamic_slice_in_dim(all_queries, span_id * SPAN, SPAN, 0)
        prefix_keys = lax.dynamic_slice_in_dim(all_keys, source * slots, slots, 0)
        prefix_values = lax.dynamic_slice_in_dim(all_values, source * slots, slots, 0)
        pieces.append(
            attend_span(span_queries, prefix_keys, prefix_values, offset, lengths[source])
        )
    return (jnp.concatenate(pieces, axis=0), cache)


def solution(mesh):
    placed = (
        P(("groups", "req"), "tp"),
        P(),
        P(None, "tp"),
        P(None, "tp"),
        P(None, "tp"),
        P("groups"),
        P("groups"),
    )
    return jax.shard_map(
        local,
        mesh=mesh,
        in_specs=placed,
        out_specs=(P(("groups", "req"), "tp"), P(None, ("groups", "req"), "tp")),
        check_vma=False,
    )
```

profile of v0, /device:TPU:0, one launch (start us, length us, event | category | flops | bytes accessed | tf_op | source)
XLA Modules:
  0.0 264.2 jit_solution(14266696549414927794)
XLA Ops:
  7.2 0.0 all-gather.5.cloned.1.call-start
  7.2 0.7 all-gather.5.cloned.1.call-update
  7.9 0.0 all-gather.7.cloned.1.call-start
  8.0 0.7 fusion.75
  18.8 0.6 fusion.74
  19.4 0.7 iota_compare_fusion.8
  20.1 1.0 multiply_cosine_fusion
  21.1 140.9 %all-gather.5.cloned.1.call-done = bf16[512,8192]{1,0:T(8,128)(2,1)} async-done(((bf16[512,2048]{1,0:T(8,128)(2,1)}), bf16[512,8192]{1,0:T(8,128)(2,1)}) %all-gather.5.cloned.1.call-update) | async-done | bytes 8388624 | tf_op jit(solution)/shard_map/all_gather | solution.py:54
  162.0 5.3 %fusion.4 = f32[512]{0:T(512)S(1)} fusion(bf16[512,8192]{1,0:T(8,128)(2,1)} %all-gather.5.cloned.1.call-done), kind=kLoop, calls=%fused_computation.6 | loop fusion | flops 12582400 | bytes 8390656 | tf_op jit(solution)/shard_map/reduce_sum | solution.py:56
  167.2 0.5 copy-done
  167.7 5.4 %fusion.11 = bf16[512,256]{1,0:T(8,128)(2,1)} fusion(bf16[8192,256]{1,0:T(8,128)(2,1)} %param.11, pred[512]{0:T(512)(128)(4,1)S(1)} %iota_compare_fusion.8, bf16[512,8192]{1,0:T(8,128)(2,1)S(1)} %copy-done, f32[8192]{0:T(1024)S(1)} %convert_element_type.121, f32[512]{0:T(512)S(1)} %add_rsqrt_fusion), kind=kOutput, calls=%fused_computation.33 | convolution fusion | flops 2164523008 | bytes 12880384 | tf_op jit(solution)/shard_map/dot_general | solution.py:75
  173.1 0.0 all-gather.7.cloned.1.call-update
  173.1 0.0 all-gather.9.cloned.1.call-start
  173.2 7.6 %fusion.70 = f32[512,256]{0,1:T(8,128)S(1)} fusion(bf16[8192,256]{1,0:T(8,128)(2,1)} %param.10, bf16[512,8192]{1,0:T(8,128)(2,1)} %all-gather.5.cloned.1.call-done, f32[8192]{0:T(1024)S(1)} %convert_element_type.121, f32[512]{0:T(512)S(1)} %add_rsqrt_fusion), kind=kOutput, calls=%fused_computation.121 | convolution fusion | flops 2164260864 | bytes 13142016 | tf_op jit(solution)/shard_map/dot_general | solution.py:70
  180.8 0.2 copy.71
  181.1 0.2 copy.70
  181.3 0.5 multiply_subtract_fusion
  181.8 0.7 pad_maximum_fusion.2
  182.6 0.9 fusion.28
  183.4 0.2 all-gather.11.cloned.1.call-start
  183.7 14.6 %convolution_bitcast_fusion = f32[64,8,8,128]{3,1,2,0:T(8,128)S(1)} fusion(bf16[8192,1024]{1,0:T(8,128)(2,1)} %param.9, bf16[512,8192]{1,0:T(8,128)(2,1)} %all-gather.5.cloned.1.call-done, f32[8192]{0:T(1024)S(1)} %convert_element_type.121, f32[512]{0:T(512)S(1)} %add_rsqrt_fusion), kind=kOutput, calls=%fused_computation.27 | convolution fusion | flops 8606711808 | bytes 27297792 | tf_op jit(solution)/shard_map/dot_general | solution.py:65
  198.2 0.5 copy.73
  198.7 0.9 subtract_convert_fusion
  199.6 0.6 pad_maximum_fusion
  200.2 1.5 copy.23
  204.2 0.6 iota_compare_fusion.7
  204.8 0.6 broadcast_compare_fusion.3
  205.5 0.6 iota_compare_fusion.6
  206.1 0.6 broadcast_compare_fusion.2
  206.8 0.6 iota_compare_fusion.4
  207.4 0.6 broadcast_compare_fusion
  208.1 0.6 iota_compare_fusion.5
  208.6 0.6 broadcast_compare_fusion.1
  209.2 0.8 fusion.31
  210.0 0.1 fusion.32
  210.1 0.1 fusion.30
  210.3 0.1 fusion.29
  210.4 0.2 reshape.244
  210.6 0.1 select_convert_fusion
  210.7 0.8 pad_maximum_fusion.3
  211.6 1.6 constant_dynamic-slice_fusion.10
  213.2 0.1 copy.22
  213.4 0.1 copy.38
  213.5 0.1 copy.33
  213.7 0.1 copy.28
  213.8 0.1 copy.27
  214.0 0.1 copy.32
  214.1 0.1 copy.37
  214.3 0.1 copy.19
  214.4 28.7 %all-gather.11.cloned.1.call-done = bf16[2048,1024]{0,1:T(8,128)(2,1)} async-done(((bf16[512,1024]{0,1:T(8,128)(2,1)}), bf16[2048,1024]{0,1:T(8,128)(2,1)}) %all-gather.11.cloned.1.call-update) | async-done | bytes 4194320 | tf_op jit(solution)/shard_map/all_gather | solution.py:80
  243.1 1.3 constant_dynamic-slice_fusion.9
  244.4 1.5 fusion.78
  245.9 2.1 fusion.13
  247.9 0.1 copy.43
  248.1 1.7 fusion.77
  249.8 2.0 fusion.14
  251.9 0.1 copy.44
  252.0 0.9 fusion.76
  252.9 1.2 fusion.15
  254.2 0.1 copy.45
  254.3 0.9 fusion.79
  255.2 1.2 fusion.12
  256.4 0.1 copy.42
  256.6 1.0 pad_maximum_fusion.1
  (24 shorter events, 0.1 us)
Async XLA Ops:
  7.2 0.8 copy-start.5
  7.2 11.5 %copy-start.3 = (bf16[8192]{0:T(1024)(128)(2,1)S(1)}, bf16[8192]{0:T(1024)(128)(2,1)}, u32[]{:S(2)}) copy-start(bf16[8192]{0:T(1024)(128)(2,1)} %param.8) | copy-start | bytes 49156
  7.2 11.6 %copy-start.4 = (s32[4]{0:T(128)S(1)}, s32[4]{0:T(128)}, u32[]{:S(2)}) copy-start(s32[4]{0:T(128)} %param.12) | copy-start | bytes 52
  7.2 154.8 %all-gather.5.cloned.1.call-start = ((), (), s32[]{:S(2)}) async-start(), calls=%async_computation | async-start | bytes 10485760 | tf_op jit(solution)/shard_map/all_gather | solution.py:54
  7.9 203.7 %all-gather.7.cloned.1.call-start = ((), (), s32[]{:S(2)}) async-start(), calls=%async_computation.1 | async-start | bytes 1310720 | tf_op jit(solution)/shard_map/all_gather | solution.py:82
  162.0 5.8 %copy-start = (bf16[512,8192]{1,0:T(8,128)(2,1)S(1)}, bf16[512,8192]{1,0:T(8,128)(2,1)}, u32[]{:S(2)}) copy-start(bf16[512,8192]{1,0:T(8,128)(2,1)} %all-gather.5.cloned.1.call-done) | copy-start | bytes 25165828
  173.1 38.4 %all-gather.9.cloned.1.call-start = ((), (), s32[]{:S(2)}) async-start(), calls=%async_computation.2 | async-start | bytes 1310720 | tf_op jit(solution)/shard_map/all_gather | solution.py:81
  183.4 59.6 %all-gather.11.cloned.1.call-start = ((), (), s32[]{:S(2)}) async-start(), calls=%async_computation.3 | async-start | bytes 5242880 | tf_op jit(solution)/shard_map/all_gather | solution.py:80
  200.2 10.6 %copy-start.1 = (bf16[512,256]{1,0:T(8,128)(2,1)S(1)}, bf16[512,256]{1,0:T(8,128)(2,1)}, u32[]{:S(2)}) copy-start(bf16[512,256]{1,0:T(8,128)(2,1)} %fusion.11) | copy-start | bytes 786436
  210.3 34.1 %copy-start.2 = (pred[128,512]{0,1:T(8,128)(4,1)}, pred[128,512]{0,1:T(8,128)(4,1)S(1)}, u32[]{:S(2)}) copy-start(pred[128,512]{0,1:T(8,128)(4,1)S(1)} %fusion.30) | copy-start | bytes 196612
Sparse Core Ops, SparseCore 0:
  9.6 152.3 all-gather.4
  173.3 14.9 all-gather.6
  189.8 16.7 all-gather.8
  208.5 34.4 all-gather.10
where the time goes:
time: 265 us; the launch traced here: 264 us
  waiting for transfers between devices  170 us (64%)
  matrix products  39.1 us (15%)
  between operations  26.8 us (10%)
  other arithmetic  18.6 us (7%)
  local copies, waits for them, and re-layouts  9.06 us (3%)
    all_gather x1, waiting for transfers between devices, local(): gathered = lax.all_gather(tokens, 'tp', axis=1, tiled=True)  141 us
    all_gather x1, waiting for transfers between devices, local(): lax.all_gather(queries, 'req', axis=0, tiled=True)  28.7 us
    dot_general x1, matrix products, local(): jnp.dot(normed, w_query, preferred_element_type=jnp.float32)  14.6 us
    dot_general x1, matrix products, local(): jnp.dot(normed, key_weight, preferred_element_type=jnp.float32)  7.57 us
    dot_general x4, matrix products, attend_span(): jnp.einsum('kgcl,lkd->ckgd', weights, value_view, preferred_element_type=...  6.54 us
    dot_general x1, matrix products, local(): jnp.dot(normed, value_weight, preferred_element_type=jnp.float32)  5.38 us
  transfers between devices with their start and end apart: 4, of which 2 were waited for; matrix products, arithmetic and copies ran while one was open for 16% of the time, Pallas kernels for 0%

commit v1 on v0

--- a/solution.py
+++ b/solution.py
@@ -7,6 +7,7 @@
 
 HEAD_SIZE = 128
 SPAN = 128
+CHUNKS = 1
 
 
 def rotate(values, positions, width):
@@ -50,46 +51,95 @@
     return mixed.reshape(count, -1).astype(jnp.bfloat16)
 
 
-def local(tokens, norm_gain, w_query, key_weight, value_weight, lengths, plan):
-    gathered = lax.all_gather(tokens, "tp", axis=1, tiled=True)
-    wide = gathered.astype(jnp.float32)
-    scale = lax.rsqrt(jnp.mean(wide * wide, axis=-1, keepdims=True) + 1e-05)
-    normed = (wide * scale * norm_gain.astype(jnp.float32)).astype(jnp.bfloat16)
+def pick(one_hot, rows):
+    return jnp.dot(
+        one_hot.astype(jnp.bfloat16), rows, preferred_element_type=jnp.float32
+    ).astype(jnp.bfloat16)
+
+
+def shift_chips(value, hop, chips):
+    pairs = [(2 * x + c, 2 * ((x + hop) % chips) + c) for x in range(chips) for c in range(2)]
+    return lax.ppermute(value, "req", pairs)
+
+
+def swap_cores(value, chips):
+    return lax.ppermute(value, "req", [(d, d ^ 1) for d in range(2 * chips)])
+
+
+def local(chips, tokens, norm_gain, w_query, key_weight, value_weight, lengths, plan):
+    workers = 2 * chips
     slots = tokens.shape[0]
     per_home = slots // SPAN
-    home_index = lax.axis_index("req")
-    length = lengths[home_index]
-    positions = jnp.arange(slots)
-    live = (positions < length)[:, None]
-    queries = rotate(
-        jnp.dot(normed, w_query, preferred_element_type=jnp.float32), positions, HEAD_SIZE
-    ).astype(jnp.bfloat16)
-    key_rows = jnp.where(
-        live,
-        rotate(
+    live_rows = workers * slots // 2
+    rows = live_rows // workers // CHUNKS
+    query_width, key_width = w_query.shape[1], key_weight.shape[1]
+    me = lax.axis_index("req")
+    chip, core = me // 2, me % 2
+    ends = jnp.cumsum(lengths)
+    starts = ends - lengths
+    slot_pos = jnp.arange(slots)
+
+    own_row = jnp.where(slot_pos < lengths[me], starts[me] + slot_pos, -1)
+    sent = []
+    for chunk in range(CHUNKS):
+        number = chunk * workers * rows + jnp.arange(workers * rows)
+        mine = pick(number[:, None] == own_row[None, :], tokens)
+        mine = mine.reshape(chips, 2, rows, tokens.shape[1])
+        other = lax.dynamic_index_in_dim(mine, 1 - core, 1, keepdims=False)
+        both = lax.dynamic_index_in_dim(mine, core, 1, keepdims=False) + swap_cores(other, chips)
+        block = lax.dynamic_index_in_dim(both, chip, 0, keepdims=False)
+        for hop in range(1, chips):
+            away = lax.dynamic_index_in_dim(both, (chip + hop) % chips, 0, keepdims=False)
+            block = block + shift_chips(away, hop, chips)
+        sent.append(block)
+
+    gathered_rows, gathered_numbers = [], []
+    for chunk in range(CHUNKS):
+        base = chunk * workers * rows
+        gathered = lax.all_gather(sent[chunk], "tp", axis=1, tiled=True)
+        wide = gathered.astype(jnp.float32)
+        scale = lax.rsqrt(jnp.mean(wide * wide, axis=-1, keepdims=True) + 1e-05)
+        normed = (wide * scale * norm_gain.astype(jnp.float32)).astype(jnp.bfloat16)
+        number = base + me * rows + jnp.arange(rows)
+        owner = jnp.sum((ends[None, :] <= number[:, None]).astype(jnp.int32), axis=1)
+        positions = number - starts[owner]
+        queries = rotate(
+            jnp.dot(normed, w_query, preferred_element_type=jnp.float32), positions, HEAD_SIZE
+        )
+        key_rows = rotate(
             jnp.dot(normed, key_weight, preferred_element_type=jnp.float32), positions, HEAD_SIZE
-        ),
-        0.0,
-    ).astype(jnp.bfloat16)
-    value_rows = jnp.where(
-        live, jnp.dot(normed, value_weight, preferred_element_type=jnp.float32), 0.0
-    ).astype(jnp.bfloat16)
-    cache = jnp.stack([key_rows, value_rows])
+        )
+        value_rows = jnp.dot(normed, value_weight, preferred_element_type=jnp.float32)
+        block = jnp.concatenate([queries, key_rows, value_rows], axis=1).astype(jnp.bfloat16)
+        held = [block] + [shift_chips(block, hop, chips) for hop in range(1, chips)]
+        swapped = [swap_cores(piece, chips) for piece in held]
+        for hop in range(chips):
+            source = (chip - hop) % chips
+            for piece, owner_core in ((held[hop], core), (swapped[hop], 1 - core)):
+                gathered_rows.append(piece)
+                gathered_numbers.append(
+                    base + (2 * source + owner_core) * rows + jnp.arange(rows)
+                )
+    all_rows = jnp.concatenate(gathered_rows, axis=0)
+    all_numbers = jnp.concatenate(gathered_numbers, axis=0)
+    keys_values = all_rows[:, query_width:]
+
+    own = pick(own_row[:, None] == all_numbers[None, :], keys_values)
+    cache = jnp.stack([own[:, :key_width], own[:, key_width:]])
     pieces = []
-    all_queries, all_keys, all_values = (
-        lax.all_gather(queries, "req", axis=0, tiled=True),
-        lax.all_gather(key_rows, "req", axis=0, tiled=True),
-        lax.all_gather(value_rows, "req", axis=0, tiled=True),
-    )
     for slot_index in range(per_home):
-        span_id = plan[home_index * per_home + slot_index]
+        span_id = plan[me * per_home + slot_index]
         source = span_id // per_home
         offset = span_id % per_home * SPAN
-        span_queries = lax.dynamic_slice_in_dim(all_queries, span_id * SPAN, SPAN, 0)
-        prefix_keys = lax.dynamic_slice_in_dim(all_keys, source * slots, slots, 0)
-        prefix_values = lax.dynamic_slice_in_dim(all_values, source * slots, slots, 0)
+        length = lengths[source]
+        request_row = jnp.where(slot_pos < length, starts[source] + slot_pos, -1)
+        span_row = lax.dynamic_slice_in_dim(request_row, offset, SPAN, 0)
+        span_queries = pick(
+            span_row[:, None] == all_numbers[None, :], all_rows[:, :query_width]
+        )
+        prefix = pick(request_row[:, None] == all_numbers[None, :], keys_values)
         pieces.append(
-            attend_span(span_queries, prefix_keys, prefix_values, offset, lengths[source])
+            attend_span(span_queries, prefix[:, :key_width], prefix[:, key_width:], offset, length)
         )
     return (jnp.concatenate(pieces, axis=0), cache)
 
@@ -104,8 +154,12 @@
         P("groups"),
         P("groups"),
     )
+
+    def block(*arrays):
+        return local(mesh.shape["req"] // 2, *arrays)
+
     return jax.shard_map(
-        local,
+        block,
         mesh=mesh,
         in_specs=placed,
         out_specs=(P(("groups", "req"), "tp"), P(None, ("groups", "req"), "tp")),

time: 265 us -> 243 us (0.917)
  waiting for transfers between devices: 170 us -> 111 us
  other arithmetic: 18.6 us -> 37.3 us
  matrix products: 39.1 us -> 47.1 us
  local copies, waits for them, and re-layouts: 9.06 us -> 16.4 us
  starting transfers between devices: 0.34 us -> 5.03 us
    all_gather x4 -> x1, waiting for transfers between devices: 170 us -> 67.9 us  [local(): gathered = lax.all_gather(sent[chunk], 'tp', axis=1, tiled=True)]
    ppermute x0 -> x5, waiting for transfers between devices: none -> 43.2 us  [the longest x2 39.3 us: shift_chips(): return lax.ppermute(value, 'req', pairs)]
    dot_general x0 -> x10, matrix products: none -> 13.6 us  [pick(): jnp.dot(one_hot.astype(jnp.bfloat16), rows, preferred_element_type=jnp.fl...]
    select_n x0 -> x5, other arithmetic: none -> 6.27 us  [the longest x4 5.06 us: local(): request_row = jnp.where(slot_pos < length, starts[source] + slot_pos, -1)]
    dot_general x1, matrix products: 14.6 us -> 8.48 us  [local(): jnp.dot(normed, w_query, preferred_element_type=jnp.float32)]
    dot_general x1, matrix products: 7.57 us -> 2.16 us  [local(): jnp.dot(normed, key_weight, preferred_element_type=jnp.float32)]
    ppermute x0 -> x5, starting transfers between devices: none -> 5 us  [the longest x2 4.47 us: shift_chips(): return lax.ppermute(value, 'req', pairs)]
    add x0 -> x5, other arithmetic: none -> 4.76 us  [the longest x1 2.43 us: local(): lax.dynamic_index_in_dim(mine, core, 1, keepdims=False)]
  transfers between devices with their start and end apart: 4 -> 6, of which waited for: 2 -> 4; matrix products, arithmetic and copies ran while one was open for 16% -> 8% of each run, Pallas kernels for 0% -> 0%
where the time goes in v1:
time: 243 us; the launch traced here: 242 us
  waiting for transfers between devices  111 us (46%)
  matrix products  47.1 us (19%)
  other arithmetic  37.3 us (15%)
  between operations  24.7 us (10%)
  local copies, waits for them, and re-layouts  16.4 us (7%)
  starting transfers between devices  5.03 us (2%)
    all_gather x1, waiting for transfers between devices, local(): gathered = lax.all_gather(sent[chunk], 'tp', axis=1, tiled=True)  67.9 us
    ppermute x2, waiting for transfers between devices, shift_chips(): return lax.ppermute(value, 'req', pairs)  39.3 us
    dot_general x10, matrix products, pick(): jnp.dot(one_hot.astype(jnp.bfloat16), rows, preferred_element_type=jnp.fl...  13.6 us
    sub x4, matrix products, attend_span(): weights = jax.nn.softmax(scores, axis=-1).astype(jnp.bfloat16)  8.74 us
    dot_general x4, matrix products, attend_span(): jnp.einsum('kgcl,lkd->ckgd', weights, value_view, preferred_element_type=...  8.57 us
    dot_general x1, matrix products, local(): jnp.dot(normed, w_query, preferred_element_type=jnp.float32)  8.48 us
    dot_general x1, matrix products, local(): jnp.dot(normed, value_weight, preferred_element_type=jnp.float32)  5.59 us
    select_n x4, other arithmetic, local(): request_row = jnp.where(slot_pos < length, starts[source] + slot_pos, -1)  5.06 us
  transfers between devices with their start and end apart: 6, of which 4 were waited for; matrix products, arithmetic and copies ran while one was open for 8% of the time, Pallas kernels for 0%

profile of v1, /device:TPU:0, one launch (start us, length us, event | category | flops | bytes accessed | tf_op | source)
XLA Modules:
  0.0 241.7 jit_solution(5877095632017811378)
XLA Ops:
  7.2 1.5 fusion.129
  18.7 0.8 reduce-window.8
  19.6 0.7 bitcast_subtract_fusion
  20.2 1.5 fusion.127
  21.8 1.2 add_select_fusion.3
  23.0 4.3 %convolution_convert_fusion = bf16[1024,2048]{1,0:T(8,128)(2,1)} fusion(bf16[512,2048]{1,0:T(8,128)(2,1)S(1)} %copy-done, s32[512]{0:T(512)S(1)} %add_select_fusion.3), kind=kOutput, calls=%fused_computation.9 | convolution fusion | flops 2150105088 | bytes 6293504 | tf_op jit(solution)/shard_map/dot_general | solution.py:55
  27.3 1.7 dynamic-slice_bitcast_fusion
  29.0 0.5 collective-permute-start
  29.5 3.9 %collective-permute-done = bf16[2,256,2048]{2,1,0:T(8,128)(2,1)} collective-permute-done((bf16[2,256,2048]{2,1,0:T(8,128)(2,1)S(1)}, bf16[2,256,2048]{2,1,0:T(8,128)(2,1)}, u32[]{:S(2)}, u32[]{:S(2)}) %collective-permute-start) | collective-permute-done | bytes 2097184 | tf_op jit(solution)/shard_map/ppermute | solution.py:66
  33.5 2.4 %bitcast_add_fusion = bf16[2,256,2048]{2,1,0:T(8,128)(2,1)S(1)} fusion(bf16[2,256,2048]{2,1,0:T(8,128)(2,1)} %collective-permute-done, bf16[2,2,256,2048]{3,2,1,0:T(8,128)(2,1)} %bitcast.151, s32[]{:T(128)S(6)} %select_n.200), kind=kLoop, calls=%fused_computation.19 | loop fusion | flops 1048576 | bytes 6291460 | tf_op jit(solution)/shard_map/add | solution.py:89
  36.0 2.9 %collective-permute-start.1 = (bf16[256,2048]{1,0:T(8,128)(2,1)S(1)}, bf16[256,2048]{1,0:T(8,128)(2,1)}, u32[]{:S(2)}, u32[]{:S(2)}) collective-permute-start(bf16[256,2048]{1,0:T(8,128)(2,1)S(1)} %dynamic-slice_bitcast_fusion.1), channel_id=1, source_target_pairs={{0,8},{4,12},{8,0},{12,4},{1,9},{5,13},{9,1},{13,5},{2,10},{6,14},... | collective-permute-start | bytes 3145736 | tf_op jit(solution)/shard_map/ppermute | solution.py:62
  38.9 23.6 %collective-permute-done.1 = bf16[256,2048]{1,0:T(8,128)(2,1)} collective-permute-done((bf16[256,2048]{1,0:T(8,128)(2,1)S(1)}, bf16[256,2048]{1,0:T(8,128)(2,1)}, u32[]{:S(2)}, u32[]{:S(2)}) %collective-permute-start.1) | collective-permute-done | bytes 1048608 | tf_op jit(solution)/shard_map/ppermute | solution.py:62
  62.5 2.3 bitcast_add_fusion.1
  65.1 2.5 %compare_select_fusion.1 = s32[256,1]{0,1:T(1,128)S(1)} fusion(s32[256,1]{0,1:T(1,128)S(1)} %bitcast.168, s32[]{:T(128)} %bitcast.13, s32[]{:T(128)} %bitcast.14, s32[]{:T(128)} %bitcast.16, s32[]{:T(128)} %bitcast.15), kind=kLoop, calls=%fused_computation.134 | loop fusion | flops 2304 | bytes 2064 | tf_op jit(solution)/shard_map/gather | solution.py:105
  68.1 1.3 add_select_fusion.4
  69.5 0.7 dynamic_slice.77
  70.1 1.2 add_select_fusion.2
  71.4 1.2 add_select_fusion.1
  72.7 0.7 iota_compare_fusion.10
  73.4 1.2 broadcast_compare_fusion.3
  74.5 0.6 iota_compare_fusion.8
  75.2 1.1 broadcast_compare_fusion.2
  76.3 0.6 iota_compare_fusion.7
  76.8 1.1 broadcast_compare_fusion.1
  78.0 1.3 add_select_fusion
  79.3 67.9 %all-gather.2.cloned.1.call-done = bf16[256,8192]{1,0:T(8,128)(2,1)} async-done(((bf16[256,2048]{1,0:T(8,128)(2,1)}), bf16[256,8192]{1,0:T(8,128)(2,1)}) %all-gather.2.cloned.1.call-update) | async-done | bytes 4194320 | tf_op jit(solution)/shard_map/all_gather | solution.py:99
  147.2 3.3 %fusion.4 = f32[256]{0:T(256)S(1)} fusion(bf16[256,8192]{1,0:T(8,128)(2,1)} %all-gather.2.cloned.1.call-done), kind=kLoop, calls=%fused_computation.6 | loop fusion | flops 6291200 | bytes 4195328 | tf_op jit(solution)/shard_map/reduce_sum | solution.py:101
  150.7 8.5 %convolution_bitcast_fusion = f32[32,8,8,128]{3,1,2,0:T(8,128)S(1)} fusion(bf16[8192,1024]{1,0:T(8,128)(2,1)} %param.9, bf16[256,8192]{1,0:T(8,128)(2,1)S(1)} %copy-done.2, f32[8192]{0:T(1024)S(1)} %convert_element_type.119, f32[256]{0:T(256)S(1)} %add_rsqrt_fusion), kind=kOutput, calls=%fused_computation.44 | convolution fusion | flops 4303355904 | bytes 22053888 | tf_op jit(solution)/shard_map/dot_general | solution.py:107
  159.4 0.5 subtract_convert_fusion
  160.3 1.3 copy-done.17
  161.6 2.2 fusion.120
  163.9 5.6 %convolution_convert_fusion.5 = bf16[256,256]{0,1:T(8,128)(2,1)S(1)} fusion(bf16[8192,256]{1,0:T(8,128)(2,1)} %param.11, bf16[256,8192]{1,0:T(8,128)(2,1)} %all-gather.2.cloned.1.call-done, f32[8192]{0:T(1024)S(1)} %convert_element_type.119, f32[256]{0:T(256)S(1)} %add_rsqrt_fusion), kind=kOutput, calls=%fused_computation.62 | convolution fusion | flops 1082195968 | bytes 8553472 | tf_op jit(solution)/shard_map/dot_general | solution.py:112
  169.7 1.5 collective-permute-start.3
  171.2 0.6 dynamic_slice.89
  171.8 0.7 iota_compare_fusion.6
  172.6 0.8 fusion.83
  173.4 15.7 %collective-permute-done.3 = bf16[256,1536]{1,0:T(8,128)(2,1)S(1)} collective-permute-done((bf16[256,1536]{1,0:T(8,128)(2,1)S(1)}, bf16[256,1536]{1,0:T(8,128)(2,1)S(1)}, u32[]{:S(2)}, u32[]{:S(2)}) %collective-permute-start.3) | collective-permute-done | bytes 786464 | tf_op jit(solution)/shard_map/ppermute | solution.py:62
  189.1 1.2 broadcast_compare_fusion
  190.2 0.8 fusion.84
  191.0 0.8 fusion.85
  191.7 0.8 fusion.86
  192.6 0.7 fusion.33
  193.4 1.7 fusion.21
  195.0 1.7 fusion.24
  196.7 1.6 fusion.27
  198.3 1.6 fusion.30
  200.0 0.8 slice_bitcast_fusion.1
  200.8 4.6 %pad_maximum_fusion = bf16[1024,1024]{1,0:T(8,128)(2,1)S(1)} fusion(bf16[256,1536]{1,0:T(8,128)(2,1)S(1)} %collective-permute-done.4, bf16[256,1536]{1,0:T(8,128)(2,1)S(1)} %collective-permute-done.3, bf16[256,1536]{1,0:T(8,128)(2,1)S(1)} %collective-permute-done.2, bf16[256,256]{1,0:T(8,128)(2,1)S(1)} %copy-done.4, bf16[256,256]{1,0:T(8,128)(2,1)S(1)} %copy.71, ...), kind=kLoop, calls=%fused_computation.10 | loop fusion | flops 12582912 | bytes 5242880 | tf_op jit(solution)/shard_map/concatenate | solution.py:123
  206.6 2.2 fusion.139
  208.8 1.9 fusion.36
  210.8 0.5 convolution_convert_fusion.3
  211.7 0.7 fusion.124
  212.5 2.2 fusion.136
  214.6 1.9 fusion.37
  216.7 0.5 convolution_convert_fusion.2
  217.4 1.1 fusion.125
  218.5 2.2 fusion.133
  220.7 1.9 fusion.38
  223.4 1.8 fusion.126
  225.2 2.2 fusion.130
  227.4 2.8 %fusion.39 = bf16[2,128,4,128]{3,1,2,0:T(8,128)(2,1)} fusion(bf16[512,2,128,1]{0,2,3,1:T(8,128)(2,1)} %bitcast.162, f32[2,4,128,512]{2,3,1,0:T(8,128)} %get-tuple-element.37, f32[2,4,128]{2,1,0:T(4,128)S(1)} %get-tuple-element.36, pred[128]{0:T(512)(128)(4,1)S(1)} %copy-done.21), kind=kOutput, calls=%fused_computation.57 | convolution fusion | flops 135528448 | bytes 2625664 | tf_op jit(solution)/shard_map/kgcl,lkd->ckgd/dot_general | solution.py:49
  230.3 1.8 copy.88
  232.0 0.8 pad_maximum_fusion.9
  232.9 2.0 pad_maximum_fusion.6
  (87 shorter events, 4.9 us)
Async XLA Ops:
  7.2 15.8 %copy-start = (bf16[512,2048]{1,0:T(8,128)(2,1)S(1)}, bf16[512,2048]{1,0:T(8,128)(2,1)}, u32[]{:S(2)}) copy-start(bf16[512,2048]{1,0:T(8,128)(2,1)} %param.7) | copy-start | bytes 6291460
  7.2 140.1 %all-gather.2.cloned.1.call-start = ((), (), s32[]{:S(2)}) async-start(), calls=%async_computation | async-start | bytes 5242880 | tf_op jit(solution)/shard_map/all_gather | solution.py:99
  29.0 4.4 %collective-permute-start = (bf16[2,256,2048]{2,1,0:T(8,128)(2,1)S(1)}, bf16[2,256,2048]{2,1,0:T(8,128)(2,1)}, u32[]{:S(2)}, u32[]{:S(2)}) collective-permute-start(bf16[2,256,2048]{2,1,0:T(8,128)(2,1)S(1)} %dynamic-slice_bitcast_fusion), channel_id=1, source_target_pairs={{0,4},{4,0},{8,12},{12,8},{1,5},{5,1},{9,13},{13,9},{2,6},{6,2},{1... | collective-permute-start | bytes 6291464 | tf_op jit(solution)/shard_map/ppermute | solution.py:66
  36.0 26.5 %collective-permute-start.1 = (bf16[256,2048]{1,0:T(8,128)(2,1)S(1)}, bf16[256,2048]{1,0:T(8,128)(2,1)}, u32[]{:S(2)}, u32[]{:S(2)}) collective-permute-start(bf16[256,2048]{1,0:T(8,128)(2,1)S(1)} %dynamic-slice_bitcast_fusion.1), channel_id=1, source_target_pairs={{0,8},{4,12},{8,0},{12,4},{1,9},{5,13},{9,1},{13,5},{2,10},{6,14},... | collective-permute-start | bytes 3145736 | tf_op jit(solution)/shard_map/ppermute | solution.py:62
  38.9 26.0 %copy-start.14 = (bf16[8192]{0:T(1024)(128)(2,1)S(1)}, bf16[8192]{0:T(1024)(128)(2,1)}, u32[]{:S(2)}) copy-start(bf16[8192]{0:T(1024)(128)(2,1)} %param.8) | copy-start | bytes 49156
  147.2 3.4 %copy-start.2 = (bf16[256,8192]{1,0:T(8,128)(2,1)S(1)}, bf16[256,8192]{1,0:T(8,128)(2,1)}, u32[]{:S(2)}) copy-start(bf16[256,8192]{1,0:T(8,128)(2,1)} %all-gather.2.cloned.1.call-done) | copy-start | bytes 12582916
  159.4 2.2 copy-start.17
  169.6 23.0 %copy-start.3 = (bf16[256,256]{1,0:T(8,128)(2,1)}, bf16[256,256]{1,0:T(8,128)(2,1)S(1)}, u32[]{:S(2)}) copy-start(bf16[256,256]{1,0:T(8,128)(2,1)S(1)} %copy.72) | copy-start | bytes 393220
  169.7 19.4 %collective-permute-start.3 = (bf16[256,1536]{1,0:T(8,128)(2,1)S(1)}, bf16[256,1536]{1,0:T(8,128)(2,1)S(1)}, u32[]{:S(2)}, u32[]{:S(2)}) collective-permute-start(bf16[256,1536]{1,0:T(8,128)(2,1)S(1)} %pad_maximum_fusion.7), channel_id=1, source_target_pairs={{0,8},{4,12},{8,0},{12,4},{1,9},{5,13},{9,1},{13,5},{2,10},{6,14},... | collective-permute-start | bytes 2359304 | tf_op jit(solution)/shard_map/ppermute | solution.py:62
  173.4 19.2 %collective-permute-start.2 = (bf16[256,1536]{1,0:T(8,128)(2,1)S(1)}, bf16[256,1536]{1,0:T(8,128)(2,1)S(1)}, u32[]{:S(2)}, u32[]{:S(2)}) collective-permute-start(bf16[256,1536]{1,0:T(8,128)(2,1)S(1)} %pad_maximum_fusion.7), channel_id=1, source_target_pairs={{0,4},{4,0},{8,12},{12,8},{1,5},{5,1},{9,13},{13,9},{2,6},{6,2},{1... | collective-permute-start | bytes 2359304 | tf_op jit(solution)/shard_map/ppermute | solution.py:66
  189.1 3.5 %collective-permute-start.4 = (bf16[256,1536]{1,0:T(8,128)(2,1)S(1)}, bf16[256,1536]{1,0:T(8,128)(2,1)S(1)}, u32[]{:S(2)}, u32[]{:S(2)}) collective-permute-start(bf16[256,1536]{1,0:T(8,128)(2,1)S(1)} %collective-permute-done.3), channel_id=1, source_target_pairs={{0,4},{4,0},{8,12},{12,8},{1,5},{5,1},{9,13},{13,9},{2,6},{6,2},{1... | collective-permute-start | bytes 2359304 | tf_op jit(solution)/shard_map/ppermute | solution.py:66
  198.3 2.5 %copy-start.4 = (bf16[256,256]{1,0:T(8,128)(2,1)S(1)}, bf16[256,256]{1,0:T(8,128)(2,1)}, u32[]{:S(2)}) copy-start(bf16[256,256]{1,0:T(8,128)(2,1)} %copy-done.3) | copy-start | bytes 393220
  200.8 4.7 %copy-start.15 = (s32[128]{0:T(128)S(1)}, s32[128]{0:T(128)}, u32[]{:S(2)}) copy-start(s32[128]{0:T(128)} %dynamic_slice.77) | copy-start | bytes 1540
  205.5 1.0 copy-start.8
  205.5 1.1 copy-start.13
  206.6 2.2 copy-start.20
  210.7 1.0 copy-start.7
  210.8 1.6 copy-start.12
  212.4 2.2 copy-start.9
  212.4 2.2 copy-start.19
  216.7 1.8 copy-start.11
  218.5 2.2 copy-start.18
  220.7 2.1 copy-start.16
  222.8 2.5 %copy-start.10 = (pred[128,512]{0,1:T(8,128)(4,1)S(1)}, pred[128,512]{0,1:T(8,128)(4,1)}, u32[]{:S(2)}) copy-start(pred[128,512]{0,1:T(8,128)(4,1)} %fusion.86) | copy-start | bytes 196612
  225.2 2.2 copy-start.21
  227.4 4.6 %copy-start.5 = (bf16[1,512,256]{2,1,0:T(8,128)(2,1)S(1)}, bf16[1,512,256]{2,1,0:T(8,128)(2,1)}, u32[]{:S(2)}) copy-start(bf16[1,512,256]{2,1,0:T(8,128)(2,1)} %get-tuple-element.4) | copy-start | bytes 786436
  227.4 4.6 %copy-start.6 = (bf16[1,512,256]{2,1,0:T(8,128)(2,1)S(1)}, bf16[1,512,256]{2,1,0:T(8,128)(2,1)}, u32[]{:S(2)}) copy-start(bf16[1,512,256]{2,1,0:T(8,128)(2,1)} %get-tuple-element.5) | copy-start | bytes 786436
  227.4 7.5 %copy-start.1 = (bf16[512,2048]{1,0:T(8,128)(2,1)S(1)}, bf16[512,2048]{1,0:T(8,128)(2,1)}, u32[]{:S(2)}) copy-start(bf16[512,2048]{1,0:T(8,128)(2,1)} %param.7) | copy-start | bytes 6291460
Sparse Core Ops, SparseCore 0:
  64.9 82.2 all-gather.1

commit v2 on v0

v2 whole, which is shorter than its diff:
```python
import functools
import math

import jax
import jax.numpy as jnp
import numpy as np
from jax import lax
from jax.experimental import pallas as pl
from jax.experimental.pallas import tpu as pltpu
from jax.sharding import PartitionSpec as P

HEAD_SIZE = 128
SPAN = 128
ALIGN = 16
SHARES = (4, 8, 4)
DEPTH = 512
VMEM_LIMIT = 40 * 1024 * 1024
F32, BF16 = jnp.float32, jnp.bfloat16


def run_of(lengths_ref, request, count):
    start = jnp.int32(0)
    length = jnp.int32(0)
    for other in range(count):
        amount = lengths_ref[other]
        start = start + jnp.where(other < request, amount, 0)
        length = jnp.where(other == request, amount, length)
    return start, length


def iota(shape, dimension):
    return lax.broadcasted_iota(jnp.int32, shape, dimension)


def deal_kernel(chips, base, rows, lengths_ref, own_ref, twin_ref, home_ref, away_ref):
    me = lax.axis_index("req")
    chip, core = lax.div(me, 2), lax.rem(me, 2)
    runs = [
        run_of(lengths_ref, request, 2 * chips) for request in (me, me + 1 - 2 * core)
    ]
    slots = own_ref.shape[0]
    for hop in range(chips):
        target = lax.rem(chip + hop, chips) * 2 + core
        number = base + target * rows + iota((rows, slots), 0)
        slot = iota((rows, slots), 1)
        total = None
        for (start, length), source in zip(runs, (own_ref, twin_ref)):
            hot = ((number - start == slot) & (slot < length)).astype(BF16)
            part = jnp.dot(hot, source[...], preferred_element_type=F32)
            total = part if total is None else total + part
        if hop == 0:
            home_ref[...] = total.astype(BF16)
        else:
            away_ref[hop - 1] = total.astype(BF16)


def deal(chips, base, rows, lengths, own, twin):
    slots, width = own.shape
    block = min(512, width)
    return pl.pallas_call(
        functools.partial(deal_kernel, chips, base, rows),
        grid=(width // block,),
        in_specs=[
            pl.BlockSpec(memory_space=pltpu.SMEM),
            pl.BlockSpec((slots, block), lambda i: (0, i)),
            pl.BlockSpec((slots, block), lambda i: (0, i)),
        ],
        out_specs=[
            pl.BlockSpec((rows, block), lambda i: (0, i)),
            pl.BlockSpec((chips - 1, rows, block), lambda i: (0, 0, i)),
        ],
        out_shape=[
            jax.ShapeDtypeStruct((rows, width), BF16),
            jax.ShapeDtypeStruct((chips - 1, rows, width), BF16),
        ],
        compiler_params=pltpu.CompilerParams(vmem_limit_bytes=VMEM_LIMIT),
        cost_estimate=pl.CostEstimate(
            flops=4 * chips * rows * slots * width,
            bytes_accessed=4 * slots * width + 2 * chips * rows * width,
            transcendentals=0,
        ),
        name="deal",
    )(lengths, own, twin)


def project_kernel(offsets, shards, steps, base, members, *refs):
    first, final = offsets == (0,), 0 not in offsets and abs(offsets[0]) == shards - 1
    place_ref, lengths_ref = refs[:2]
    refs = refs[2:]
    pieces, refs = refs[: len(offsets)], refs[len(offsets) :]
    gain_ref, query_ref, key_ref, value_ref = refs[:4]
    refs = refs[4:]
    if not first:
        sums_in, squares_in = refs[:2]
        refs = refs[2:]
    if final:
        cosine_ref, sine_ref, frequency_ref, out_ref, sums, squares = (*refs[:2], None, *refs[2:])
    elif first:
        frequency_ref, sums, squares, cosine_ref, sine_ref = refs
    else:
        sums, squares = refs
    piece, step = pl.program_id(0), pl.program_id(1)
    rows = sums.shape[0]

    @pl.when((piece == 0) & (step == 0))
    def _():
        if first:
            sums[...] = jnp.zeros_like(sums)
            squares[...] = jnp.zeros_like(squares)
            number = base + place_ref[1] * rows + iota((rows, HEAD_SIZE), 0)
            start = jnp.zeros((rows, HEAD_SIZE), jnp.int32)
            before = jnp.int32(0)
            for other in range(members):
                before = before + lengths_ref[other]
                start = jnp.where(number >= before, before, start)
            angle = (number - start).astype(F32) * frequency_ref[...]
            lower = iota((rows, HEAD_SIZE), 1) < HEAD_SIZE // 2
            sine = jnp.sin(angle)
            cosine_ref[...] = jnp.cos(angle)
            sine_ref[...] = jnp.where(lower, -sine, sine)
        else:
            sums[...] = sums_in[...]
            squares[...] = squares_in[...]

    for index, offset in enumerate(offsets):
        shard = place_ref[0] + offset

        @pl.when((piece == index) & (shard >= 0) & (shard < shards))
        def _():
            wide = pieces[index][...].astype(F32)
            square = wide * wide
            part = square[:, :128]
            for at in range(128, square.shape[1], 128):
                part = part + square[:, at : at + 128]
            squares[...] += part
            scaled = (wide * gain_ref[...]).astype(BF16)
            at = 0
            for weight in (query_ref, key_ref, value_ref):
                columns = slice(at, at + weight.shape[1])
                sums[:, columns] += jnp.dot(scaled, weight[...], preferred_element_type=F32)
                at += weight.shape[1]

    if final:

        @pl.when((piece == len(offsets) - 1) & (step == steps - 1))
        def _():
            mean = jnp.sum(squares[...], axis=1, keepdims=True) / (
                shards * steps * pieces[0].shape[1]
            )
            scale = lax.rsqrt(mean + 1e-05)
            turned = query_ref.shape[1] + key_ref.shape[1]
            for at in range(0, sums.shape[1], HEAD_SIZE):
                columns = slice(at, at + HEAD_SIZE)
                head = sums[:, columns] * scale
                if at < turned:
                    head = head * cosine_ref[...] + pltpu.roll(
                        head, HEAD_SIZE // 2, 1
                    ) * sine_ref[...]
                out_ref[:, columns] = head.astype(BF16)


def project(offsets, shards, base, place, lengths, pieces, gain, weights, carried, frequency):
    rows, width = pieces[0].shape
    depth = min(DEPTH, width)
    steps = width // depth
    columns = sum(weight.shape[1] for weight in weights)
    first = offsets == (0,)
    final = not first and abs(offsets[0]) == shards - 1

    def block_of(piece, step, place_ref):
        if len(offsets) == 1:
            return place_ref[0] * steps + step
        left, right = place_ref[0] + offsets[0], place_ref[0] + offsets[1]
        has_left, has_right = left >= 0, right < shards
        on_left = jnp.where(
            has_left, left * steps + step, jnp.where(has_right, right * steps, 0)
        )
        on_right = jnp.where(
            has_right, right * steps + step, jnp.where(has_left, left * steps + steps - 1, 0)
        )
        return jnp.where(piece == 0, on_left, on_right)

    def piece_spec(index):
        def where(piece, step, place_ref, lengths_ref):
            edge = 0 if index else steps - 1
            return (0, jnp.where(piece == index, step, edge))

        return pl.BlockSpec((rows, depth), where)

    def whole(shape):
        return pl.BlockSpec(shape, lambda piece, step, place_ref, lengths_ref: (0, 0))

    def deep(block, dimension):
        def where(piece, step, place_ref, lengths_ref):
            at = block_of(piece, step, place_ref)
            return (at, 0) if dimension == 0 else (0, at)

        return pl.BlockSpec(block, where)

    in_specs = [piece_spec(index) for index in range(len(offsets))]
    in_specs += [deep((1, depth), 1)]
    in_specs += [deep((depth, weight.shape[1]), 0) for weight in weights]
    operands = [*pieces, gain, *weights]
    sums = jax.ShapeDtypeStruct((rows, columns), F32)
    lanes = jax.ShapeDtypeStruct((rows, 128), F32)
    table = jax.ShapeDtypeStruct((rows, HEAD_SIZE), F32)
    aliases, scratch = {}, []
    if first:
        in_specs += [whole((1, HEAD_SIZE))]
        operands += [frequency]
        out_shape = [sums, lanes, table, table]
    else:
        in_specs += [whole((rows, columns)), whole((rows, 128))]
        operands += carried[:2]
        if final:
            in_specs += [whole((rows, HEAD_SIZE))] * 2
            operands += carried[2:]
            out_shape = [jax.ShapeDtypeStruct((rows, columns), BF16)]
            scratch = [pltpu.VMEM((rows, columns), F32), pltpu.VMEM((rows, 128), F32)]
        else:
            out_shape = [sums, lanes]
    return pl.pallas_call(
        functools.partial(project_kernel, offsets, shards, steps, base, lengths.shape[0]),
        grid_spec=pltpu.PrefetchScalarGridSpec(
            num_scalar_prefetch=2,
            grid=(len(offsets), steps),
            in_specs=in_specs,
            out_specs=[whole(leaf.shape) for leaf in out_shape],
            scratch_shapes=scratch,
        ),
        out_shape=out_shape,
        compiler_params=pltpu.CompilerParams(vmem_limit_bytes=VMEM_LIMIT),
        cost_estimate=pl.CostEstimate(
            flops=2 * rows * width * columns * len(offsets),
            bytes_accessed=2 * width * columns * len(offsets) + 8 * rows * columns,
            transcendentals=0,
        ),
        name="project",
    )(place, lengths, *operands)


def attend_kernel(chips, bases, sizes, query_width, key_width, lengths_ref, plan_ref, *refs):
    blocks, (attended_ref, cache_ref, rows_ref, sems) = refs[:-4], refs[-4:]
    workers = 2 * chips
    me = lax.axis_index("req")
    chip, core = lax.div(me, 2), lax.rem(me, 2)
    slots = cache_ref.shape[1]
    spans = slots // SPAN
    total = workers * sum(sizes)
    copies = []
    for chunk, (base, rows) in enumerate(zip(bases, sizes)):
        for hop in range(chips):
            source = lax.rem(chip - hop + chips, chips) * 2
            for twin in range(2):
                owner = source + (core if twin == 0 else 1 - core)
                index = (chunk * chips + hop) * 2 + twin
                at = pl.multiple_of(base + owner * rows, ALIGN)
                copies.append(
                    pltpu.make_async_copy(
                        blocks[index], rows_ref.at[pl.ds(at, rows), :], sems.at[index]
                    )
                )
    for copy in copies:
        copy.start()
    pad = rows_ref.shape[0] - total
    rows_ref[total:, :] = jnp.zeros((pad, rows_ref.shape[1]), BF16)
    for copy in copies:
        copy.wait()

    def aligned(row):
        first = pl.multiple_of(lax.div(row, ALIGN) * ALIGN, ALIGN)
        return first, row - first

    start, length = run_of(lengths_ref, me, workers)
    first, shift = aligned(start)
    reach = slots + SPAN
    row, column = iota((slots, reach), 0), iota((slots, reach), 1)
    hot = ((column == row + shift) & (row < length)).astype(BF16)
    for half in range(2):
        window = rows_ref[
            pl.ds(first, reach),
            query_width + half * key_width : query_width + (half + 1) * key_width,
        ]
        cache_ref[half] = jnp.dot(hot, window, preferred_element_type=F32).astype(BF16)

    heads, key_heads = query_width // HEAD_SIZE, key_width // HEAD_SIZE
    group = heads // key_heads
    factor = math.log2(math.e) / math.sqrt(HEAD_SIZE)
    for slot in range(spans):
        span = plan_ref[me * spans + slot]
        source = lax.div(span, spans)
        part = lax.rem(span, spans)
        start, length = run_of(lengths_ref, source, workers)
        offset = part * SPAN
        out_rows = slice(slot * SPAN, (slot + 1) * SPAN)
        dead = offset >= length

        @pl.when(dead)
        def _():
            attended_ref[out_rows, :] = jnp.zeros((SPAN, query_width), BF16)

        for count in range(1, spans + 1):

            @pl.when(jnp.logical_not(dead) & (part == count - 1))
            def _():
                first, shift = aligned(start + offset)
                hot = iota((SPAN, 2 * SPAN), 1) == iota((SPAN, 2 * SPAN), 0) + shift
                queries = jnp.dot(
                    hot.astype(BF16),
                    rows_ref[pl.ds(first, 2 * SPAN), :query_width],
                    preferred_element_type=F32,
                ).astype(BF16)
                reach = (count + 1) * SPAN
                first, shift = aligned(start)
                key_pos = iota((SPAN, reach), 1) - shift
                query_pos = (count - 1) * SPAN + iota((SPAN, reach), 0)
                allowed = (key_pos >= 0) & (key_pos <= query_pos) & (key_pos < length)
                bias = jnp.where(allowed, 0.0, -1e30)
                bias = jnp.concatenate([bias] * group, axis=0)
                live = (count - 1) * SPAN + iota((SPAN, HEAD_SIZE), 0) < length
                for head in range(key_heads):
                    stacked = jnp.concatenate(
                        [
                            queries[:, at * HEAD_SIZE : (at + 1) * HEAD_SIZE]
                            for at in range(head * group, (head + 1) * group)
                        ],
                        axis=0,
                    )
                    left = query_width + head * HEAD_SIZE
                    keys = rows_ref[pl.ds(first, reach), left : left + HEAD_SIZE]
                    left += key_width
                    values = rows_ref[pl.ds(first, reach), left : left + HEAD_SIZE]
                    scores = lax.dot_general(
                        stacked, keys, (((1,), (1,)), ((), ())), preferred_element_type=F32
                    )
                    scores = scores + bias
                    top = jnp.max(scores, axis=1, keepdims=True)
                    weights = jnp.exp2((scores - top) * factor)
                    norm = jnp.sum(weights, axis=1, keepdims=True)
                    mixed = jnp.dot(weights.astype(BF16), values, preferred_element_type=F32)
                    mixed = mixed / norm
                    for at in range(group):
                        left = (head * group + at) * HEAD_SIZE
                        attended_ref[out_rows, left : left + HEAD_SIZE] = jnp.where(
                            live, mixed[at * SPAN : (at + 1) * SPAN], 0.0
                        ).astype(BF16)


def attend(chips, bases, sizes, query_width, key_width, slots, lengths, plan, blocks):
    width = query_width + 2 * key_width
    total = 2 * chips * sum(sizes)
    return pl.pallas_call(
        functools.partial(attend_kernel, chips, bases, sizes, query_width, key_width),
        in_specs=[pl.BlockSpec(memory_space=pltpu.SMEM)] * 2
        + [pl.BlockSpec(memory_space=pl.ANY)] * len(blocks),
        out_specs=[pl.BlockSpec(memory_space=pltpu.VMEM)] * 2,
        out_shape=[
            jax.ShapeDtypeStruct((slots, query_width), BF16),
            jax.ShapeDtypeStruct((2, slots, key_width), BF16),
        ],
        scratch_shapes=[
            pltpu.VMEM((total + slots + SPAN, width), BF16),
            pltpu.SemaphoreType.DMA((len(blocks),)),
        ],
        compiler_params=pltpu.CompilerParams(vmem_limit_bytes=VMEM_LIMIT),
        name="attend",
    )(lengths, plan, *blocks)


def shift_chips(value, hop, chips):
    pairs = [(2 * x + c, 2 * ((x + hop) % chips) + c) for x in range(chips) for c in range(2)]
    return lax.ppermute(value, "req", pairs)


def swap_cores(value, chips):
    return lax.ppermute(value, "req", [(d, d ^ 1) for d in range(2 * chips)])


def local(
    chips, shards, tokens, norm_gain, w_query, key_weight, value_weight, lengths, plan
):
    workers = 2 * chips
    slots = tokens.shape[0]
    live = slots // 2
    sizes = [live * share // sum(SHARES) // ALIGN * ALIGN for share in SHARES]
    sizes[-1] = live - sum(sizes[:-1])
    bases = [workers * sum(sizes[:chunk]) for chunk in range(len(sizes))]
    weights = (w_query, key_weight, value_weight)
    place = jnp.stack([lax.axis_index("tp"), lax.axis_index("req")]).astype(jnp.int32)
    gain = norm_gain.astype(F32).reshape(1, -1)
    halfway = HEAD_SIZE // 2
    frequency = np.exp(-np.arange(halfway) * 2.0 / HEAD_SIZE * math.log(500000.0))
    frequency = jnp.asarray(np.tile(frequency, 2)[None, :], F32)

    twin = swap_cores(tokens, chips)
    held = []
    for base, rows in zip(bases, sizes):
        block, away = deal(chips, base, rows, lengths, tokens, twin)
        for hop in range(1, chips):
            block = block + shift_chips(away[hop - 1], hop, chips)
        held.append(block)

    onward = [[(block, block)] for block in held]
    for step in range(1, shards):
        right = [(at, at + 1) for at in range(step - 1, shards - 1)]
        left = [(at, at - 1) for at in range(1, shards - step + 1)]
        for line in onward:
            line.append(
                (lax.ppermute(line[-1][0], "tp", right), lax.ppermute(line[-1][1], "tp", left))
            )

    blocks = []
    for base, line in zip(bases, onward):
        carried = project(
            (0,), shards, base, place, lengths, line[0][:1], gain, weights, (), frequency
        )
        tables = carried[2:]
        for step in range(1, shards):
            last = step == shards - 1
            carried = project(
                (-step, step),
                shards,
                base,
                place,
                lengths,
                line[step],
                gain,
                weights,
                [*carried[:2], *tables] if last else carried[:2],
                frequency,
            )
        block = carried[0]
        here = [block] + [shift_chips(block, hop, chips) for hop in range(1, chips)]
        for piece in here:
            blocks += [piece, swap_cores(piece, chips)]
    return tuple(
        attend(
            chips,
            bases,
            sizes,
            w_query.shape[1],
            key_weight.shape[1],
            slots,
            lengths,
            plan,
            blocks,
        )
    )


def solution(mesh):
    placed = (
        P(("groups", "req"), "tp"),
        P(),
        P(None, "tp"),
        P(None, "tp"),
        P(None, "tp"),
        P("groups"),
        P("groups"),
    )
    return jax.shard_map(
        functools.partial(local, mesh.shape["req"] // 2, mesh.shape["tp"]),
        mesh=mesh,
        in_specs=placed,
        out_specs=(P(("groups", "req"), "tp"), P(None, ("groups", "req"), "tp")),
        check_vma=False,
    )
```

time: 265 us -> 178 us (0.67)
  the two profiles are of different devices: /device:TPU:0 before, /device:TPU:14 now
where the time goes in v2:
time: 178 us; the launch traced here: 176 us
  Pallas kernels  81.6 us (46%)
  starting transfers between devices  48 us (27%)
  waiting for transfers between devices  37.4 us (21%)
  local copies, waits for them, and re-layouts  6.66 us (4%)
    pallas_call x12, Pallas kernels, project(): pl.pallas_call(functools.partial(project_kernel, offsets, shards, steps,...  63.4 us
    ppermute x9, starting transfers between devices, local(): lax.ppermute(line[-1][0], 'tp', right)  24.9 us
    ppermute x6, waiting for transfers between devices, shift_chips(): return lax.ppermute(value, 'req', pairs)  22.4 us
    ppermute x9, starting transfers between devices, local(): lax.ppermute(line[-1][1], 'tp', left)  16.9 us
    pallas_call x1, Pallas kernels, attend(): pl.pallas_call(functools.partial(attend_kernel, chips, bases, sizes, quer...  9.24 us
    ppermute x9, waiting for transfers between devices, local(): lax.ppermute(line[-1][0], 'tp', right)  9.16 us
    pallas_call x3, Pallas kernels, deal(): pl.pallas_call(functools.partial(deal_kernel, chips, base, rows), grid=(w...  8.96 us
    unnamed x20, local copies, waits for them, and re-layouts  6.66 us
  transfers between devices with their start and end apart: 31, of which 7 were waited for; matrix products, arithmetic and copies ran while one was open for 1% of the time, Pallas kernels for 40%

profile of v2, /device:TPU:14, one launch (start us, length us, event | category | flops | bytes accessed | tf_op | source)
XLA Modules:
  0.0 176.3 jit_solution(5871384892011593378)
XLA Ops:
  0.6 0.1 collective-permute-start
  0.7 4.4 %collective-permute-done.twin_ref = bf16[512,2048]{1,0:T(8,128)(2,1)S(1)} collective-permute-done((bf16[512,2048]{1,0:T(8,128)(2,1)}, bf16[512,2048]{1,0:T(8,128)(2,1)S(1)}, u32[]{:S(2)}, u32[]{:S(2)}) %collective-permute-start) | collective-permute-done | bytes 2097184 | tf_op jit(solution)/shard_map/ppermute | solution.py:376
  5.1 1.6 copy-done.3
  6.7 0.7 copy-done.5
  7.3 2.7 %deal.4 = (bf16[128,2048]{1,0:T(8,128)(2,1)S(1)}, bf16[1,128,2048]{2,1,0:T(8,128)(2,1)S(1)}) custom-call(s32[4]{0:T(128)S(1)} %copy-done.5, bf16[512,2048]{1,0:T(8,128)(2,1)S(1)} %copy-done.3, bf16[512,2048]{1,0:T(8,128)(2,1)S(1)} %collective-permute-done.twin_ref), custom_call_target="tpu_custom_call" | custom-call | flops 1073741824 | bytes 5242880 | tf_op jit(solution)/shard_map/deal/pallas_call | solution.py:60
  10.0 0.6 collective-permute-start.11
  10.6 13.4 %collective-permute-done.11 = bf16[128,2048]{1,0:T(8,128)(2,1)S(1)} collective-permute-done((bf16[128,2048]{1,0:T(8,128)(2,1)S(1)}, bf16[128,2048]{1,0:T(8,128)(2,1)S(1)}, u32[]{:S(2)}, u32[]{:S(2)}) %collective-permute-start.11) | collective-permute-done | bytes 524320 | tf_op jit(solution)/shard_map/ppermute | solution.py:372
  24.1 0.1 add.10.refs_2_
  24.2 0.0 copy-start.9
  24.2 0.0 copy-start.6
  24.2 0.0 copy-start.7
  24.2 3.6 %collective-permute-start.12 = (bf16[128,2048]{1,0:T(8,128)(2,1)S(1)}, bf16[128,2048]{1,0:T(8,128)(2,1)S(1)}, u32[]{:S(2)}, u32[]{:S(2)}) collective-permute-start(bf16[128,2048]{1,0:T(8,128)(2,1)S(1)} %add.10.refs_2_), channel_id=1, source_target_pairs={{0,1},{1,2},{2,3},{4,5},{5,6},{6,7},{8,9},{9,10},{10,11},{12,13},{... | collective-permute-start | bytes 1572872 | tf_op jit(solution)/shard_map/ppermute | solution.py:409
  27.9 2.4 %collective-permute-start.15 = (bf16[128,2048]{1,0:T(8,128)(2,1)S(1)}, bf16[128,2048]{1,0:T(8,128)(2,1)S(1)}, u32[]{:S(2)}, u32[]{:S(2)}) collective-permute-start(bf16[128,2048]{1,0:T(8,128)(2,1)S(1)} %add.10.refs_2_), channel_id=1, source_target_pairs={{1,0},{2,1},{3,2},{5,4},{6,5},{7,6},{9,8},{10,9},{11,10},{13,12},{... | collective-permute-start | bytes 1572872 | tf_op jit(solution)/shard_map/ppermute | solution.py:409
  30.2 9.1 %collective-permute-done.12.refs_2_ = bf16[128,2048]{1,0:T(8,128)(2,1)S(1)} collective-permute-done((bf16[128,2048]{1,0:T(8,128)(2,1)S(1)}, bf16[128,2048]{1,0:T(8,128)(2,1)S(1)}, u32[]{:S(2)}, u32[]{:S(2)}) %collective-permute-start.12) | collective-permute-done | bytes 524320 | tf_op jit(solution)/shard_map/ppermute | solution.py:409
  39.4 3.5 %collective-permute-start.13 = (bf16[128,2048]{1,0:T(8,128)(2,1)S(1)}, bf16[128,2048]{1,0:T(8,128)(2,1)S(1)}, u32[]{:S(2)}, u32[]{:S(2)}) collective-permute-start(bf16[128,2048]{1,0:T(8,128)(2,1)S(1)} %collective-permute-done.12.refs_2_), channel_id=1, source_target_pairs={{1,2},{2,3},{5,6},{6,7},{9,10},{10,11},{13,14},{14,15},{17,18},{18... | collective-permute-start | bytes 1572872 | tf_op jit(solution)/shard_map/ppermute | solution.py:409
  42.9 2.1 %collective-permute-start.16 = (bf16[128,2048]{1,0:T(8,128)(2,1)S(1)}, bf16[128,2048]{1,0:T(8,128)(2,1)S(1)}, u32[]{:S(2)}, u32[]{:S(2)}) collective-permute-start(bf16[128,2048]{1,0:T(8,128)(2,1)S(1)} %collective-permute-done.15.refs_3_), channel_id=1, source_target_pairs={{1,0},{2,1},{5,4},{6,5},{9,8},{10,9},{13,12},{14,13},{17,16},{18,1... | collective-permute-start | bytes 1572872 | tf_op jit(solution)/shard_map/ppermute | solution.py:409
  45.0 2.8 %deal.5 = (bf16[64,2048]{1,0:T(8,128)(2,1)S(1)}, bf16[1,64,2048]{2,1,0:T(8,128)(2,1)S(1)}) custom-call(s32[4]{0:T(128)S(1)} %copy-done.5, bf16[512,2048]{1,0:T(8,128)(2,1)S(1)} %copy-done.3, bf16[512,2048]{1,0:T(8,128)(2,1)S(1)} %collective-permute-done.twin_ref), custom_call_target="tpu_custom_call" | custom-call | flops 536870912 | bytes 4718592 | tf_op jit(solution)/shard_map/deal/pallas_call | solution.py:60
  47.8 0.6 collective-permute-start.21
  48.4 3.4 %deal.3 = (bf16[64,2048]{1,0:T(8,128)(2,1)S(1)}, bf16[1,64,2048]{2,1,0:T(8,128)(2,1)}) custom-call(s32[4]{0:T(128)S(1)} %copy-done.5, bf16[512,2048]{1,0:T(8,128)(2,1)S(1)} %copy-done.3, bf16[512,2048]{1,0:T(8,128)(2,1)S(1)} %collective-permute-done.twin_ref), custom_call_target="tpu_custom_call" | custom-call | flops 536870912 | bytes 4718592 | tf_op jit(solution)/shard_map/deal/pallas_call | solution.py:60
  51.9 1.5 collective-permute-start.1
  53.3 2.8 %collective-permute-done.21 = bf16[64,2048]{1,0:T(8,128)(2,1)S(1)} collective-permute-done((bf16[64,2048]{1,0:T(8,128)(2,1)S(1)}, bf16[64,2048]{1,0:T(8,128)(2,1)S(1)}, u32[]{:S(2)}, u32[]{:S(2)}) %collective-permute-start.21) | collective-permute-done | bytes 262176 | tf_op jit(solution)/shard_map/ppermute | solution.py:372
  56.2 0.1 add.11.refs_2_
  56.2 4.0 %collective-permute-start.22 = (bf16[64,2048]{1,0:T(8,128)(2,1)S(1)}, bf16[64,2048]{1,0:T(8,128)(2,1)S(1)}, u32[]{:S(2)}, u32[]{:S(2)}) collective-permute-start(bf16[64,2048]{1,0:T(8,128)(2,1)S(1)} %add.11.refs_2_), channel_id=1, source_target_pairs={{0,1},{1,2},{2,3},{4,5},{5,6},{6,7},{8,9},{9,10},{10,11},{12,13},{... | collective-permute-start | bytes 786440 | tf_op jit(solution)/shard_map/ppermute | solution.py:409
  60.2 1.9 %collective-permute-start.25 = (bf16[64,2048]{1,0:T(8,128)(2,1)S(1)}, bf16[64,2048]{1,0:T(8,128)(2,1)S(1)}, u32[]{:S(2)}, u32[]{:S(2)}) collective-permute-start(bf16[64,2048]{1,0:T(8,128)(2,1)S(1)} %add.11.refs_2_), channel_id=1, source_target_pairs={{1,0},{2,1},{3,2},{5,4},{6,5},{7,6},{9,8},{10,9},{11,10},{13,12},{... | collective-permute-start | bytes 786440 | tf_op jit(solution)/shard_map/ppermute | solution.py:409
  62.2 1.1 add.9.refs_2_
  63.3 3.9 %collective-permute-start.2 = (bf16[64,2048]{1,0:T(8,128)(2,1)S(1)}, bf16[64,2048]{1,0:T(8,128)(2,1)S(1)}, u32[]{:S(2)}, u32[]{:S(2)}) collective-permute-start(bf16[64,2048]{1,0:T(8,128)(2,1)S(1)} %add.9.refs_2_), channel_id=1, source_target_pairs={{0,1},{1,2},{2,3},{4,5},{5,6},{6,7},{8,9},{9,10},{10,11},{12,13},{... | collective-permute-start | bytes 786440 | tf_op jit(solution)/shard_map/ppermute | solution.py:409
  67.2 0.7 collective-permute-start.14
  67.9 2.0 %collective-permute-start.17 = (bf16[128,2048]{1,0:T(8,128)(2,1)S(1)}, bf16[128,2048]{1,0:T(8,128)(2,1)S(1)}, u32[]{:S(2)}, u32[]{:S(2)}) collective-permute-start(bf16[128,2048]{1,0:T(8,128)(2,1)S(1)} %collective-permute-done.16.refs_3_), channel_id=1, source_target_pairs={{1,0},{5,4},{9,8},{13,12},{17,16},{21,20},{25,24},{29,28}} | collective-permute-start | bytes 1572872 | tf_op jit(solution)/shard_map/ppermute | solution.py:409
  69.9 0.1 pad_add_fusion.refs_0_
  70.0 2.2 %copy-done = bf16[8192,256]{1,0:T(8,128)(2,1)S(1)} copy-done((bf16[8192,256]{1,0:T(8,128)(2,1)S(1)}, bf16[8192,256]{1,0:T(8,128)(2,1)}, u32[]{:S(2)}) %copy-start) | copy-done | bytes 4194328
  72.2 2.2 %copy-done.2 = bf16[8192,256]{1,0:T(8,128)(2,1)S(1)} copy-done((bf16[8192,256]{1,0:T(8,128)(2,1)S(1)}, bf16[8192,256]{1,0:T(8,128)(2,1)}, u32[]{:S(2)}) %copy-start.2) | copy-done | bytes 4194328
  74.4 4.8 %project.20 = (f32[64,1536]{1,0:T(8,128)S(1)}, f32[64,128]{1,0:T(8,128)S(1)}, f32[64,128]{1,0:T(8,128)S(1)}, f32[64,128]{1,0:T(8,128)S(1)}) custom-call(s32[2]{0:T(128)S(1)} %pad_add_fusion.refs_0_, s32[4]{0:T(128)S(1)} %copy-done.6, bf16[64,2048]{1,0:T(8,128)(2,1)S(1)} %add.11.refs_2_, f32[1,8192]{1,0:T(1,128)S(1)} %bitcast.6, bf16[8192,1024]{1,0:T(8,128)(2,1)} %refs_5_.23, ...), custom_call_target="tpu_custom_call" | custom-call | flops 402653184 | bytes 7077888 | tf_op jit(solution)/shard_map/project/pallas_call | solution.py:222
  79.2 1.9 %collective-permute-start.5 = (bf16[64,2048]{1,0:T(8,128)(2,1)S(1)}, bf16[64,2048]{1,0:T(8,128)(2,1)S(1)}, u32[]{:S(2)}, u32[]{:S(2)}) collective-permute-start(bf16[64,2048]{1,0:T(8,128)(2,1)S(1)} %add.9.refs_2_), channel_id=1, source_target_pairs={{1,0},{2,1},{3,2},{5,4},{6,5},{7,6},{9,8},{10,9},{11,10},{13,12},{... | collective-permute-start | bytes 786440 | tf_op jit(solution)/shard_map/ppermute | solution.py:409
  81.1 3.9 %collective-permute-start.23 = (bf16[64,2048]{1,0:T(8,128)(2,1)S(1)}, bf16[64,2048]{1,0:T(8,128)(2,1)S(1)}, u32[]{:S(2)}, u32[]{:S(2)}) collective-permute-start(bf16[64,2048]{1,0:T(8,128)(2,1)S(1)} %collective-permute-done.22.refs_2_), channel_id=1, source_target_pairs={{1,2},{2,3},{5,6},{6,7},{9,10},{10,11},{13,14},{14,15},{17,18},{18... | collective-permute-start | bytes 786440 | tf_op jit(solution)/shard_map/ppermute | solution.py:409
  85.1 4.5 %project.12 = (f32[64,1536]{1,0:T(8,128)S(1)}, f32[64,128]{1,0:T(8,128)S(1)}, f32[64,128]{1,0:T(8,128)S(1)}, f32[64,128]{1,0:T(8,128)S(1)}) custom-call(s32[2]{0:T(128)S(1)} %pad_add_fusion.refs_0_, s32[4]{0:T(128)S(1)} %copy-done.6, bf16[64,2048]{1,0:T(8,128)(2,1)S(1)} %add.9.refs_2_, f32[1,8192]{1,0:T(1,128)S(1)} %bitcast.7, bf16[8192,1024]{1,0:T(8,128)(2,1)} %refs_5_.23, ...), custom_call_target="tpu_custom_call" | custom-call | flops 402653184 | bytes 7077888 | tf_op jit(solution)/shard_map/project/pallas_call | solution.py:222
  89.6 4.7 %project.16 = (f32[128,1536]{1,0:T(8,128)S(1)}, f32[128,128]{1,0:T(8,128)S(1)}, f32[128,128]{1,0:T(8,128)S(1)}, f32[128,128]{1,0:T(8,128)S(1)}) custom-call(s32[2]{0:T(128)S(1)} %pad_add_fusion.refs_0_, s32[4]{0:T(128)S(1)} %copy-done.6, bf16[128,2048]{1,0:T(8,128)(2,1)S(1)} %add.10.refs_2_, f32[1,8192]{1,0:T(1,128)S(1)} %bitcast.8, ...), custom_call_target="tpu_custom_call" | custom-call | flops 805306368 | bytes 7864320 | tf_op jit(solution)/shard_map/project/pallas_call | solution.py:222
  94.3 1.9 %collective-permute-start.26 = (bf16[64,2048]{1,0:T(8,128)(2,1)S(1)}, bf16[64,2048]{1,0:T(8,128)(2,1)S(1)}, u32[]{:S(2)}, u32[]{:S(2)}) collective-permute-start(bf16[64,2048]{1,0:T(8,128)(2,1)S(1)} %collective-permute-done.25.refs_3_), channel_id=1, source_target_pairs={{1,0},{2,1},{5,4},{6,5},{9,8},{10,9},{13,12},{14,13},{17,16},{18,1... | collective-permute-start | bytes 786440 | tf_op jit(solution)/shard_map/ppermute | solution.py:409
  96.3 8.1 %project.17 = (f32[128,1536]{1,0:T(8,128)S(1)}, f32[128,128]{1,0:T(8,128)S(1)}) custom-call(s32[2]{0:T(128)S(1)} %pad_add_fusion.refs_0_, s32[4]{0:T(128)S(1)} %copy-done.6, bf16[128,2048]{1,0:T(8,128)(2,1)S(1)} %collective-permute-done.12.refs_2_, bf16[128,2048]{1,0:T(8,128)(2,1)S(1)} %collective-permute-done.15.refs_3_, f32[1,8192]{1,0:T(1,128)S(1)} %bitcast.9, ...), custom_call_target="tpu_custom_call" | custom-call | flops 1610612736 | bytes 14155776 | tf_op jit(solution)/shard_map/project/pallas_call | solution.py:222
  104.4 3.9 %collective-permute-start.3 = (bf16[64,2048]{1,0:T(8,128)(2,1)S(1)}, bf16[64,2048]{1,0:T(8,128)(2,1)S(1)}, u32[]{:S(2)}, u32[]{:S(2)}) collective-permute-start(bf16[64,2048]{1,0:T(8,128)(2,1)S(1)} %collective-permute-done.2.refs_2_), channel_id=1, source_target_pairs={{1,2},{2,3},{5,6},{6,7},{9,10},{10,11},{13,14},{14,15},{17,18},{18... | collective-permute-start | bytes 786440 | tf_op jit(solution)/shard_map/ppermute | solution.py:409
  108.3 1.9 %collective-permute-start.6 = (bf16[64,2048]{1,0:T(8,128)(2,1)S(1)}, bf16[64,2048]{1,0:T(8,128)(2,1)S(1)}, u32[]{:S(2)}, u32[]{:S(2)}) collective-permute-start(bf16[64,2048]{1,0:T(8,128)(2,1)S(1)} %collective-permute-done.5.refs_3_), channel_id=1, source_target_pairs={{1,0},{2,1},{5,4},{6,5},{9,8},{10,9},{13,12},{14,13},{17,16},{18,1... | collective-permute-start | bytes 786440 | tf_op jit(solution)/shard_map/ppermute | solution.py:409
  110.2 5.6 %project.18 = (f32[128,1536]{1,0:T(8,128)S(1)}, f32[128,128]{1,0:T(8,128)S(1)}) custom-call(s32[2]{0:T(128)S(1)} %pad_add_fusion.refs_0_, s32[4]{0:T(128)S(1)} %copy-done.6, bf16[128,2048]{1,0:T(8,128)(2,1)S(1)} %collective-permute-done.13.refs_2_, bf16[128,2048]{1,0:T(8,128)(2,1)S(1)} %collective-permute-done.16.refs_3_, f32[1,8192]{1,0:T(1,128)S(1)} %bitcast.10, ...), custom_call_target="tpu_custom_call" | custom-call | flops 1610612736 | bytes 14155776 | tf_op jit(solution)/shard_map/project/pallas_call | solution.py:222
  115.8 0.7 collective-permute-start.24
  116.5 1.3 collective-permute-start.27
  117.9 3.0 %project.19.refs_4_ = bf16[128,1536]{1,0:T(8,128)(2,1)S(1)} custom-call(s32[2]{0:T(128)S(1)} %pad_add_fusion.refs_0_, s32[4]{0:T(128)S(1)} %copy-done.6, bf16[128,2048]{1,0:T(8,128)(2,1)S(1)} %collective-permute-done.14.refs_2_, bf16[128,2048]{1,0:T(8,128)(2,1)S(1)} %collective-permute-done.17.refs_3_, f32[1,8192]{1,0:T(1,128)S(1)} %bitcast.11, ...), custom_call_target="tpu_custom_call" | custom-call | flops 1610612736 | bytes 14155776 | tf_op jit(solution)/shard_map/project/pallas_call | solution.py:222
  120.8 0.1 collective-permute-start.19
  120.9 8.0 %project.21 = (f32[64,1536]{1,0:T(8,128)S(1)}, f32[64,128]{1,0:T(8,128)S(1)}) custom-call(s32[2]{0:T(128)S(1)} %pad_add_fusion.refs_0_, s32[4]{0:T(128)S(1)} %copy-done.6, bf16[64,2048]{1,0:T(8,128)(2,1)S(1)} %collective-permute-done.22.refs_2_, bf16[64,2048]{1,0:T(8,128)(2,1)S(1)} %collective-permute-done.25.refs_3_, f32[1,8192]{1,0:T(1,128)S(1)} %bitcast.12, ...), custom_call_target="tpu_custom_call" | custom-call | flops 805306368 | bytes 13369344 | tf_op jit(solution)/shard_map/project/pallas_call | solution.py:222
  128.9 0.7 collective-permute-start.4
  129.6 1.5 collective-permute-start.7
  131.1 8.0 %project.13 = (f32[64,1536]{1,0:T(8,128)S(1)}, f32[64,128]{1,0:T(8,128)S(1)}) custom-call(s32[2]{0:T(128)S(1)} %pad_add_fusion.refs_0_, s32[4]{0:T(128)S(1)} %copy-done.6, bf16[64,2048]{1,0:T(8,128)(2,1)S(1)} %collective-permute-done.2.refs_2_, bf16[64,2048]{1,0:T(8,128)(2,1)S(1)} %collective-permute-done.5.refs_3_, f32[1,8192]{1,0:T(1,128)S(1)} %bitcast.13, ...), custom_call_target="tpu_custom_call" | custom-call | flops 805306368 | bytes 13369344 | tf_op jit(solution)/shard_map/project/pallas_call | solution.py:222
  139.2 5.5 %project.22 = (f32[64,1536]{1,0:T(8,128)S(1)}, f32[64,128]{1,0:T(8,128)S(1)}) custom-call(s32[2]{0:T(128)S(1)} %pad_add_fusion.refs_0_, s32[4]{0:T(128)S(1)} %copy-done.6, bf16[64,2048]{1,0:T(8,128)(2,1)S(1)} %collective-permute-done.23.refs_2_, bf16[64,2048]{1,0:T(8,128)(2,1)S(1)} %collective-permute-done.26.refs_3_, f32[1,8192]{1,0:T(1,128)S(1)} %bitcast.14, ...), custom_call_target="tpu_custom_call" | custom-call | flops 805306368 | bytes 13369344 | tf_op jit(solution)/shard_map/project/pallas_call | solution.py:222
  144.7 5.5 %project.14 = (f32[64,1536]{1,0:T(8,128)S(1)}, f32[64,128]{1,0:T(8,128)S(1)}) custom-call(s32[2]{0:T(128)S(1)} %pad_add_fusion.refs_0_, s32[4]{0:T(128)S(1)} %copy-done.6, bf16[64,2048]{1,0:T(8,128)(2,1)S(1)} %collective-permute-done.3.refs_2_, bf16[64,2048]{1,0:T(8,128)(2,1)S(1)} %collective-permute-done.6.refs_3_, f32[1,8192]{1,0:T(1,128)S(1)} %bitcast.15, ...), custom_call_target="tpu_custom_call" | custom-call | flops 805306368 | bytes 13369344 | tf_op jit(solution)/shard_map/project/pallas_call | solution.py:222
  150.3 2.8 %project.23.refs_8_ = bf16[64,1536]{1,0:T(8,128)(2,1)S(1)} custom-call(s32[2]{0:T(128)S(1)} %pad_add_fusion.refs_0_, s32[4]{0:T(128)S(1)} %copy-done.6, bf16[64,2048]{1,0:T(8,128)(2,1)S(1)} %collective-permute-done.24.refs_2_, bf16[64,2048]{1,0:T(8,128)(2,1)S(1)} %collective-permute-done.27.refs_3_, f32[1,8192]{1,0:T(1,128)S(1)} %bitcast.16, ...), custom_call_target="tpu_custom_call" | custom-call | flops 805306368 | bytes 13369344 | tf_op jit(solution)/shard_map/project/pallas_call | solution.py:222
  153.1 2.1 %collective-permute-start.29 = (bf16[64,1536]{1,0:T(8,128)(2,1)S(1)}, bf16[64,1536]{1,0:T(8,128)(2,1)S(1)}, u32[]{:S(2)}, u32[]{:S(2)}) collective-permute-start(bf16[64,1536]{1,0:T(8,128)(2,1)S(1)} %project.23.refs_8_), channel_id=1, source_target_pairs={{0,8},{4,12},{8,0},{12,4},{1,9},{5,13},{9,1},{13,5},{2,10},{6,14},... | collective-permute-start | bytes 589832 | tf_op jit(solution)/shard_map/ppermute | solution.py:372
  155.2 0.0 copy-start.8
  155.2 2.8 %project.15.refs_0_ = bf16[64,1536]{1,0:T(8,128)(2,1)S(1)} custom-call(s32[2]{0:T(128)S(1)} %pad_add_fusion.refs_0_, s32[4]{0:T(128)S(1)} %copy-done.6, bf16[64,2048]{1,0:T(8,128)(2,1)S(1)} %collective-permute-done.4.refs_2_, bf16[64,2048]{1,0:T(8,128)(2,1)S(1)} %collective-permute-done.7.refs_3_, f32[1,8192]{1,0:T(1,128)S(1)} %bitcast.17, ...), custom_call_target="tpu_custom_call" | custom-call | flops 805306368 | bytes 13369344 | tf_op jit(solution)/shard_map/project/pallas_call | solution.py:222
  158.0 0.2 collective-permute-start.9
  158.2 0.5 collective-permute-start.18
  158.7 0.1 collective-permute-start.20
  158.8 0.1 collective-permute-done.29.refs_10_
  158.8 0.4 collective-permute-start.8
  159.2 0.2 collective-permute-start.30
  159.4 6.0 %collective-permute-done.9.refs_2_ = bf16[64,1536]{1,0:T(8,128)(2,1)S(1)} collective-permute-done((bf16[64,1536]{1,0:T(8,128)(2,1)S(1)}, bf16[64,1536]{1,0:T(8,128)(2,1)S(1)}, u32[]{:S(2)}, u32[]{:S(2)}) %collective-permute-start.9) | collective-permute-done | bytes 196640 | tf_op jit(solution)/shard_map/ppermute | solution.py:372
  165.4 1.4 collective-permute-done.10.refs_3_
  166.9 9.2 %attend.1 = (bf16[512,1024]{1,0:T(8,128)(2,1)}, bf16[2,512,256]{2,1,0:T(8,128)(2,1)}) custom-call(s32[4]{0:T(128)S(1)} %copy-done.6, s32[16]{0:T(128)S(1)} %copy-done.8, bf16[64,1536]{1,0:T(8,128)(2,1)S(1)} %project.15.refs_0_, bf16[64,1536]{1,0:T(8,128)(2,1)S(1)} %collective-permute-done.8.refs_1_, bf16[64,1536]{1,0:T(8,128)(2,1)S(1)} %collective-permute-done.9.refs_2_, ...), custom_call_target="tpu_custom_call" | custom-call | tf_op jit(solution)/shard_map/attend/pallas_call | solution.py:352
  (39 shorter events, 0.1 us)
Async XLA Ops:
  0.6 4.4 %collective-permute-start = (bf16[512,2048]{1,0:T(8,128)(2,1)}, bf16[512,2048]{1,0:T(8,128)(2,1)S(1)}, u32[]{:S(2)}, u32[]{:S(2)}) collective-permute-start(bf16[512,2048]{1,0:T(8,128)(2,1)} %own_ref.5), channel_id=1, source_target_pairs={{0,4},{4,0},{8,12},{12,8},{1,5},{5,1},{9,13},{13,9},{2,6},{6,2},{1... | collective-permute-start | bytes 6291464 | tf_op jit(solution)/shard_map/ppermute | solution.py:376
  5.1 1.6 copy-start.3
  6.7 0.7 copy-start.5
  10.0 14.0 %collective-permute-start.11 = (bf16[128,2048]{1,0:T(8,128)(2,1)S(1)}, bf16[128,2048]{1,0:T(8,128)(2,1)S(1)}, u32[]{:S(2)}, u32[]{:S(2)}) collective-permute-start(bf16[128,2048]{1,0:T(8,128)(2,1)S(1)} %bitcast.18), channel_id=1, source_target_pairs={{0,8},{4,12},{8,0},{12,4},{1,9},{5,13},{9,1},{13,5},{2,10},{6,14},... | collective-permute-start | bytes 1572872 | tf_op jit(solution)/shard_map/ppermute | solution.py:372
  24.2 38.0 %copy-start.9 = (bf16[8192]{0:T(1024)(128)(2,1)S(1)}, bf16[8192]{0:T(1024)(128)(2,1)}, u32[]{:S(2)}) copy-start(bf16[8192]{0:T(1024)(128)(2,1)} %param.9) | copy-start | bytes 49156
  24.2 45.8 %copy-start.6 = (s32[4]{0:T(128)S(1)}, s32[4]{0:T(128)}, u32[]{:S(2)}) copy-start(s32[4]{0:T(128)} %lengths_ref.7) | copy-start | bytes 52
  24.2 45.8 %copy-start.7 = (f32[1,128]{1,0:T(1,128)S(1)}, f32[1,128]{1,0:T(1,128)}, u32[]{:S(2)}) copy-start(f32[1,128]{1,0:T(1,128)} %constant.9.clone.refs_7_) | copy-start | bytes 1540
  24.2 15.2 %collective-permute-start.12 = (bf16[128,2048]{1,0:T(8,128)(2,1)S(1)}, bf16[128,2048]{1,0:T(8,128)(2,1)S(1)}, u32[]{:S(2)}, u32[]{:S(2)}) collective-permute-start(bf16[128,2048]{1,0:T(8,128)(2,1)S(1)} %add.10.refs_2_), channel_id=1, source_target_pairs={{0,1},{1,2},{2,3},{4,5},{5,6},{6,7},{8,9},{9,10},{10,11},{12,13},{... | collective-permute-start | bytes 1572872 | tf_op jit(solution)/shard_map/ppermute | solution.py:409
  27.9 15.1 %collective-permute-start.15 = (bf16[128,2048]{1,0:T(8,128)(2,1)S(1)}, bf16[128,2048]{1,0:T(8,128)(2,1)S(1)}, u32[]{:S(2)}, u32[]{:S(2)}) collective-permute-start(bf16[128,2048]{1,0:T(8,128)(2,1)S(1)} %add.10.refs_2_), channel_id=1, source_target_pairs={{1,0},{2,1},{3,2},{5,4},{6,5},{7,6},{9,8},{10,9},{11,10},{13,12},{... | collective-permute-start | bytes 1572872 | tf_op jit(solution)/shard_map/ppermute | solution.py:409
  39.4 27.8 %collective-permute-start.13 = (bf16[128,2048]{1,0:T(8,128)(2,1)S(1)}, bf16[128,2048]{1,0:T(8,128)(2,1)S(1)}, u32[]{:S(2)}, u32[]{:S(2)}) collective-permute-start(bf16[128,2048]{1,0:T(8,128)(2,1)S(1)} %collective-permute-done.12.refs_2_), channel_id=1, source_target_pairs={{1,2},{2,3},{5,6},{6,7},{9,10},{10,11},{13,14},{14,15},{17,18},{18... | collective-permute-start | bytes 1572872 | tf_op jit(solution)/shard_map/ppermute | solution.py:409
  42.9 25.0 %collective-permute-start.16 = (bf16[128,2048]{1,0:T(8,128)(2,1)S(1)}, bf16[128,2048]{1,0:T(8,128)(2,1)S(1)}, u32[]{:S(2)}, u32[]{:S(2)}) collective-permute-start(bf16[128,2048]{1,0:T(8,128)(2,1)S(1)} %collective-permute-done.15.refs_3_), channel_id=1, source_target_pairs={{1,0},{2,1},{5,4},{6,5},{9,8},{10,9},{13,12},{14,13},{17,16},{18,1... | collective-permute-start | bytes 1572872 | tf_op jit(solution)/shard_map/ppermute | solution.py:409
  47.8 8.4 %collective-permute-start.21 = (bf16[64,2048]{1,0:T(8,128)(2,1)S(1)}, bf16[64,2048]{1,0:T(8,128)(2,1)S(1)}, u32[]{:S(2)}, u32[]{:S(2)}) collective-permute-start(bf16[64,2048]{1,0:T(8,128)(2,1)S(1)} %bitcast.19), channel_id=1, source_target_pairs={{0,8},{4,12},{8,0},{12,4},{1,9},{5,13},{9,1},{13,5},{2,10},{6,14},... | collective-permute-start | bytes 786440 | tf_op jit(solution)/shard_map/ppermute | solution.py:372
  51.9 4.4 %copy-start.4 = (bf16[64,2048]{1,0:T(8,128)(2,1)}, bf16[64,2048]{1,0:T(8,128)(2,1)S(1)}, u32[]{:S(2)}) copy-start(bf16[64,2048]{1,0:T(8,128)(2,1)S(1)} %get-tuple-element.32) | copy-start | bytes 786436
  51.9 10.3 %collective-permute-start.1 = (bf16[64,2048]{1,0:T(8,128)(2,1)}, bf16[64,2048]{1,0:T(8,128)(2,1)}, u32[]{:S(2)}, u32[]{:S(2)}) collective-permute-start(bf16[64,2048]{1,0:T(8,128)(2,1)} %bitcast.2), channel_id=1, source_target_pairs={{0,8},{4,12},{8,0},{12,4},{1,9},{5,13},{9,1},{13,5},{2,10},{6,14},... | collective-permute-start | bytes 786440 | tf_op jit(solution)/shard_map/ppermute | solution.py:372
  56.2 22.9 %collective-permute-start.22 = (bf16[64,2048]{1,0:T(8,128)(2,1)S(1)}, bf16[64,2048]{1,0:T(8,128)(2,1)S(1)}, u32[]{:S(2)}, u32[]{:S(2)}) collective-permute-start(bf16[64,2048]{1,0:T(8,128)(2,1)S(1)} %add.11.refs_2_), channel_id=1, source_target_pairs={{0,1},{1,2},{2,3},{4,5},{5,6},{6,7},{8,9},{9,10},{10,11},{12,13},{... | collective-permute-start | bytes 786440 | tf_op jit(solution)/shard_map/ppermute | solution.py:409
  60.2 20.9 %collective-permute-start.25 = (bf16[64,2048]{1,0:T(8,128)(2,1)S(1)}, bf16[64,2048]{1,0:T(8,128)(2,1)S(1)}, u32[]{:S(2)}, u32[]{:S(2)}) collective-permute-start(bf16[64,2048]{1,0:T(8,128)(2,1)S(1)} %add.11.refs_2_), channel_id=1, source_target_pairs={{1,0},{2,1},{3,2},{5,4},{6,5},{7,6},{9,8},{10,9},{11,10},{13,12},{... | collective-permute-start | bytes 786440 | tf_op jit(solution)/shard_map/ppermute | solution.py:409
  63.3 31.1 %collective-permute-start.2 = (bf16[64,2048]{1,0:T(8,128)(2,1)S(1)}, bf16[64,2048]{1,0:T(8,128)(2,1)S(1)}, u32[]{:S(2)}, u32[]{:S(2)}) collective-permute-start(bf16[64,2048]{1,0:T(8,128)(2,1)S(1)} %add.9.refs_2_), channel_id=1, source_target_pairs={{0,1},{1,2},{2,3},{4,5},{5,6},{6,7},{8,9},{9,10},{10,11},{12,13},{... | collective-permute-start | bytes 786440 | tf_op jit(solution)/shard_map/ppermute | solution.py:409
  67.2 49.3 %collective-permute-start.14 = (bf16[128,2048]{1,0:T(8,128)(2,1)S(1)}, bf16[128,2048]{1,0:T(8,128)(2,1)S(1)}, u32[]{:S(2)}, u32[]{:S(2)}) collective-permute-start(bf16[128,2048]{1,0:T(8,128)(2,1)S(1)} %collective-permute-done.13.refs_2_), channel_id=1, source_target_pairs={{2,3},{6,7},{10,11},{14,15},{18,19},{22,23},{26,27},{30,31}} | collective-permute-start | bytes 1572872 | tf_op jit(solution)/shard_map/ppermute | solution.py:409
  67.9 49.9 %collective-permute-start.17 = (bf16[128,2048]{1,0:T(8,128)(2,1)S(1)}, bf16[128,2048]{1,0:T(8,128)(2,1)S(1)}, u32[]{:S(2)}, u32[]{:S(2)}) collective-permute-start(bf16[128,2048]{1,0:T(8,128)(2,1)S(1)} %collective-permute-done.16.refs_3_), channel_id=1, source_target_pairs={{1,0},{5,4},{9,8},{13,12},{17,16},{21,20},{25,24},{29,28}} | collective-permute-start | bytes 1572872 | tf_op jit(solution)/shard_map/ppermute | solution.py:409
  70.0 2.2 %copy-start = (bf16[8192,256]{1,0:T(8,128)(2,1)S(1)}, bf16[8192,256]{1,0:T(8,128)(2,1)}, u32[]{:S(2)}) copy-start(bf16[8192,256]{1,0:T(8,128)(2,1)} %refs_6_.23) | copy-start | bytes 12582916
  72.2 2.2 %copy-start.2 = (bf16[8192,256]{1,0:T(8,128)(2,1)S(1)}, bf16[8192,256]{1,0:T(8,128)(2,1)}, u32[]{:S(2)}) copy-start(bf16[8192,256]{1,0:T(8,128)(2,1)} %refs_7_.20) | copy-start | bytes 12582916
  74.4 10.7 %copy-start.1 = (bf16[8192,256]{1,0:T(8,128)(2,1)S(1)}, bf16[8192,256]{1,0:T(8,128)(2,1)}, u32[]{:S(2)}) copy-start(bf16[8192,256]{1,0:T(8,128)(2,1)} %refs_6_.23) | copy-start | bytes 12582916
  79.2 25.2 %collective-permute-start.5 = (bf16[64,2048]{1,0:T(8,128)(2,1)S(1)}, bf16[64,2048]{1,0:T(8,128)(2,1)S(1)}, u32[]{:S(2)}, u32[]{:S(2)}) collective-permute-start(bf16[64,2048]{1,0:T(8,128)(2,1)S(1)} %add.9.refs_2_), channel_id=1, source_target_pairs={{1,0},{2,1},{3,2},{5,4},{6,5},{7,6},{9,8},{10,9},{11,10},{13,12},{... | collective-permute-start | bytes 786440 | tf_op jit(solution)/shard_map/ppermute | solution.py:409
  81.1 27.2 %collective-permute-start.23 = (bf16[64,2048]{1,0:T(8,128)(2,1)S(1)}, bf16[64,2048]{1,0:T(8,128)(2,1)S(1)}, u32[]{:S(2)}, u32[]{:S(2)}) collective-permute-start(bf16[64,2048]{1,0:T(8,128)(2,1)S(1)} %collective-permute-done.22.refs_2_), channel_id=1, source_target_pairs={{1,2},{2,3},{5,6},{6,7},{9,10},{10,11},{13,14},{14,15},{17,18},{18... | collective-permute-start | bytes 786440 | tf_op jit(solution)/shard_map/ppermute | solution.py:409
  94.3 21.5 %collective-permute-start.26 = (bf16[64,2048]{1,0:T(8,128)(2,1)S(1)}, bf16[64,2048]{1,0:T(8,128)(2,1)S(1)}, u32[]{:S(2)}, u32[]{:S(2)}) collective-permute-start(bf16[64,2048]{1,0:T(8,128)(2,1)S(1)} %collective-permute-done.25.refs_3_), channel_id=1, source_target_pairs={{1,0},{2,1},{5,4},{6,5},{9,8},{10,9},{13,12},{14,13},{17,16},{18,1... | collective-permute-start | bytes 786440 | tf_op jit(solution)/shard_map/ppermute | solution.py:409
  104.4 24.6 %collective-permute-start.3 = (bf16[64,2048]{1,0:T(8,128)(2,1)S(1)}, bf16[64,2048]{1,0:T(8,128)(2,1)S(1)}, u32[]{:S(2)}, u32[]{:S(2)}) collective-permute-start(bf16[64,2048]{1,0:T(8,128)(2,1)S(1)} %collective-permute-done.2.refs_2_), channel_id=1, source_target_pairs={{1,2},{2,3},{5,6},{6,7},{9,10},{10,11},{13,14},{14,15},{17,18},{18... | collective-permute-start | bytes 786440 | tf_op jit(solution)/shard_map/ppermute | solution.py:409
  108.3 21.3 %collective-permute-start.6 = (bf16[64,2048]{1,0:T(8,128)(2,1)S(1)}, bf16[64,2048]{1,0:T(8,128)(2,1)S(1)}, u32[]{:S(2)}, u32[]{:S(2)}) collective-permute-start(bf16[64,2048]{1,0:T(8,128)(2,1)S(1)} %collective-permute-done.5.refs_3_), channel_id=1, source_target_pairs={{1,0},{2,1},{5,4},{6,5},{9,8},{10,9},{13,12},{14,13},{17,16},{18,1... | collective-permute-start | bytes 786440 | tf_op jit(solution)/shard_map/ppermute | solution.py:409
  115.8 34.4 %collective-permute-start.24 = (bf16[64,2048]{1,0:T(8,128)(2,1)S(1)}, bf16[64,2048]{1,0:T(8,128)(2,1)S(1)}, u32[]{:S(2)}, u32[]{:S(2)}) collective-permute-start(bf16[64,2048]{1,0:T(8,128)(2,1)S(1)} %collective-permute-done.23.refs_2_), channel_id=1, source_target_pairs={{2,3},{6,7},{10,11},{14,15},{18,19},{22,23},{26,27},{30,31}} | collective-permute-start | bytes 786440 | tf_op jit(solution)/shard_map/ppermute | solution.py:409
  116.5 33.7 %collective-permute-start.27 = (bf16[64,2048]{1,0:T(8,128)(2,1)S(1)}, bf16[64,2048]{1,0:T(8,128)(2,1)S(1)}, u32[]{:S(2)}, u32[]{:S(2)}) collective-permute-start(bf16[64,2048]{1,0:T(8,128)(2,1)S(1)} %collective-permute-done.26.refs_3_), channel_id=1, source_target_pairs={{1,0},{5,4},{9,8},{13,12},{17,16},{21,20},{25,24},{29,28}} | collective-permute-start | bytes 786440 | tf_op jit(solution)/shard_map/ppermute | solution.py:409
  120.8 37.8 %collective-permute-start.19 = (bf16[128,1536]{1,0:T(8,128)(2,1)S(1)}, bf16[128,1536]{1,0:T(8,128)(2,1)S(1)}, u32[]{:S(2)}, u32[]{:S(2)}) collective-permute-start(bf16[128,1536]{1,0:T(8,128)(2,1)S(1)} %project.19.refs_4_), channel_id=1, source_target_pairs={{0,8},{4,12},{8,0},{12,4},{1,9},{5,13},{9,1},{13,5},{2,10},{6,14},... | collective-permute-start | bytes 1179656 | tf_op jit(solution)/shard_map/ppermute | solution.py:372
  128.9 26.2 %collective-permute-start.4 = (bf16[64,2048]{1,0:T(8,128)(2,1)S(1)}, bf16[64,2048]{1,0:T(8,128)(2,1)S(1)}, u32[]{:S(2)}, u32[]{:S(2)}) collective-permute-start(bf16[64,2048]{1,0:T(8,128)(2,1)S(1)} %collective-permute-done.3.refs_2_), channel_id=1, source_target_pairs={{2,3},{6,7},{10,11},{14,15},{18,19},{22,23},{26,27},{30,31}} | collective-permute-start | bytes 786440 | tf_op jit(solution)/shard_map/ppermute | solution.py:409
  129.6 25.5 %collective-permute-start.7 = (bf16[64,2048]{1,0:T(8,128)(2,1)S(1)}, bf16[64,2048]{1,0:T(8,128)(2,1)S(1)}, u32[]{:S(2)}, u32[]{:S(2)}) collective-permute-start(bf16[64,2048]{1,0:T(8,128)(2,1)S(1)} %collective-permute-done.6.refs_3_), channel_id=1, source_target_pairs={{1,0},{5,4},{9,8},{13,12},{17,16},{21,20},{25,24},{29,28}} | collective-permute-start | bytes 786440 | tf_op jit(solution)/shard_map/ppermute | solution.py:409
  153.1 5.7 %collective-permute-start.29 = (bf16[64,1536]{1,0:T(8,128)(2,1)S(1)}, bf16[64,1536]{1,0:T(8,128)(2,1)S(1)}, u32[]{:S(2)}, u32[]{:S(2)}) collective-permute-start(bf16[64,1536]{1,0:T(8,128)(2,1)S(1)} %project.23.refs_8_), channel_id=1, source_target_pairs={{0,8},{4,12},{8,0},{12,4},{1,9},{5,13},{9,1},{13,5},{2,10},{6,14},... | collective-permute-start | bytes 589832 | tf_op jit(solution)/shard_map/ppermute | solution.py:372
  155.2 4.0 %collective-permute-start.28 = (bf16[64,1536]{1,0:T(8,128)(2,1)S(1)}, bf16[64,1536]{1,0:T(8,128)(2,1)S(1)}, u32[]{:S(2)}, u32[]{:S(2)}) collective-permute-start(bf16[64,1536]{1,0:T(8,128)(2,1)S(1)} %project.23.refs_8_), channel_id=1, source_target_pairs={{0,4},{4,0},{8,12},{12,8},{1,5},{5,1},{9,13},{13,9},{2,6},{6,2},{1... | collective-permute-start | bytes 589832 | tf_op jit(solution)/shard_map/ppermute | solution.py:376
  155.2 11.7 %copy-start.8 = (s32[16]{0:T(128)S(1)}, s32[16]{0:T(128)}, u32[]{:S(2)}) copy-start(s32[16]{0:T(128)} %plan_ref.1) | copy-start | bytes 196
  158.0 7.4 %collective-permute-start.9 = (bf16[64,1536]{1,0:T(8,128)(2,1)S(1)}, bf16[64,1536]{1,0:T(8,128)(2,1)S(1)}, u32[]{:S(2)}, u32[]{:S(2)}) collective-permute-start(bf16[64,1536]{1,0:T(8,128)(2,1)S(1)} %project.15.refs_0_), channel_id=1, source_target_pairs={{0,8},{4,12},{8,0},{12,4},{1,9},{5,13},{9,1},{13,5},{2,10},{6,14},... | collective-permute-start | bytes 589832 | tf_op jit(solution)/shard_map/ppermute | solution.py:372
  158.2 8.6 %collective-permute-start.18 = (bf16[128,1536]{1,0:T(8,128)(2,1)S(1)}, bf16[128,1536]{1,0:T(8,128)(2,1)S(1)}, u32[]{:S(2)}, u32[]{:S(2)}) collective-permute-start(bf16[128,1536]{1,0:T(8,128)(2,1)S(1)} %project.19.refs_4_), channel_id=1, source_target_pairs={{0,4},{4,0},{8,12},{12,8},{1,5},{5,1},{9,13},{13,9},{2,6},{6,2},{1... | collective-permute-start | bytes 1179656 | tf_op jit(solution)/shard_map/ppermute | solution.py:376
  158.7 8.2 %collective-permute-start.20 = (bf16[128,1536]{1,0:T(8,128)(2,1)S(1)}, bf16[128,1536]{1,0:T(8,128)(2,1)S(1)}, u32[]{:S(2)}, u32[]{:S(2)}) collective-permute-start(bf16[128,1536]{1,0:T(8,128)(2,1)S(1)} %collective-permute-done.19.refs_6_), channel_id=1, source_target_pairs={{0,4},{4,0},{8,12},{12,8},{1,5},{5,1},{9,13},{13,9},{2,6},{6,2},{1... | collective-permute-start | bytes 1179656 | tf_op jit(solution)/shard_map/ppermute | solution.py:376
  158.8 6.6 %collective-permute-start.8 = (bf16[64,1536]{1,0:T(8,128)(2,1)S(1)}, bf16[64,1536]{1,0:T(8,128)(2,1)S(1)}, u32[]{:S(2)}, u32[]{:S(2)}) collective-permute-start(bf16[64,1536]{1,0:T(8,128)(2,1)S(1)} %project.15.refs_0_), channel_id=1, source_target_pairs={{0,4},{4,0},{8,12},{12,8},{1,5},{5,1},{9,13},{13,9},{2,6},{6,2},{1... | collective-permute-start | bytes 589832 | tf_op jit(solution)/shard_map/ppermute | solution.py:376
  159.2 6.2 %collective-permute-start.30 = (bf16[64,1536]{1,0:T(8,128)(2,1)S(1)}, bf16[64,1536]{1,0:T(8,128)(2,1)S(1)}, u32[]{:S(2)}, u32[]{:S(2)}) collective-permute-start(bf16[64,1536]{1,0:T(8,128)(2,1)S(1)} %collective-permute-done.29.refs_10_), channel_id=1, source_target_pairs={{0,4},{4,0},{8,12},{12,8},{1,5},{5,1},{9,13},{13,9},{2,6},{6,2},{1... | collective-permute-start | bytes 589832 | tf_op jit(solution)/shard_map/ppermute | solution.py:376
  165.4 1.4 collective-permute-start.10

commit v3 on v2

v3 whole, which is shorter than its diff:
```python
import functools
import math

import jax
import jax.numpy as jnp
import numpy as np
from jax import lax
from jax.experimental import pallas as pl
from jax.experimental.pallas import tpu as pltpu
from jax.sharding import PartitionSpec as P

HEAD_SIZE = 128
SPAN = 128
ALIGN = 16
SHARES = (4, 8, 4)
DEPTH = 1024
VMEM_LIMIT = 56 * 1024 * 1024
F32, BF16 = jnp.float32, jnp.bfloat16


def run_of(lengths_ref, request, count):
    start = jnp.int32(0)
    length = jnp.int32(0)
    for other in range(count):
        amount = lengths_ref[other]
        start = start + jnp.where(other < request, amount, 0)
        length = jnp.where(other == request, amount, length)
    return start, length


def iota(shape, dimension):
    return lax.broadcasted_iota(jnp.int32, shape, dimension)


def deal_kernel(chips, bases, sizes, lengths_ref, own_ref, twin_ref, *out_refs):
    me = lax.axis_index("req")
    chip, core = lax.div(me, 2), lax.rem(me, 2)
    runs = [
        run_of(lengths_ref, request, 2 * chips) for request in (me, me + 1 - 2 * core)
    ]
    slots = own_ref.shape[0]
    for chunk, (base, rows) in enumerate(zip(bases, sizes)):
        home_ref, away_ref = out_refs[2 * chunk : 2 * chunk + 2]
        for hop in range(chips):
            target = lax.rem(chip + hop, chips) * 2 + core
            number = base + target * rows + iota((rows, slots), 0)
            slot = iota((rows, slots), 1)
            total = None
            for (start, length), source in zip(runs, (own_ref, twin_ref)):
                hot = ((number - start == slot) & (slot < length)).astype(BF16)
                part = jnp.dot(hot, source[...], preferred_element_type=F32)
                total = part if total is None else total + part
            if hop == 0:
                home_ref[...] = total.astype(BF16)
            else:
                away_ref[hop - 1] = total.astype(BF16)


def deal(chips, bases, sizes, lengths, own, twin):
    slots, width = own.shape
    block = min(512, width)
    out_specs, out_shape = [], []
    for rows in sizes:
        out_specs += [
            pl.BlockSpec((rows, block), lambda i: (0, i)),
            pl.BlockSpec((chips - 1, rows, block), lambda i: (0, 0, i)),
        ]
        out_shape += [
            jax.ShapeDtypeStruct((rows, width), BF16),
            jax.ShapeDtypeStruct((chips - 1, rows, width), BF16),
        ]
    return pl.pallas_call(
        functools.partial(deal_kernel, chips, bases, sizes),
        grid=(width // block,),
        in_specs=[
            pl.BlockSpec(memory_space=pltpu.SMEM),
            pl.BlockSpec((slots, block), lambda i: (0, i)),
            pl.BlockSpec((slots, block), lambda i: (0, i)),
        ],
        out_specs=out_specs,
        out_shape=out_shape,
        compiler_params=pltpu.CompilerParams(vmem_limit_bytes=VMEM_LIMIT),
        cost_estimate=pl.CostEstimate(
            flops=4 * chips * sum(sizes) * slots * width,
            bytes_accessed=4 * slots * width + 2 * chips * sum(sizes) * width,
            transcendentals=0,
        ),
        name="deal",
    )(lengths, own, twin)


def merge_kernel(count, home_ref, *refs):
    total = home_ref[...]
    for ref in refs[:count]:
        total = total + ref[...]
    refs[-1 if len(refs) == count + 1 else -2][...] = total


def merge(home, arrived, later):
    count = len(arrived)
    vmem, anywhere = pl.BlockSpec(memory_space=pltpu.VMEM), pl.BlockSpec(memory_space=pl.ANY)
    operands, in_specs = [home, *arrived], [vmem] * (count + 1)
    out_shape, out_specs = [jax.ShapeDtypeStruct(home.shape, home.dtype)], [vmem]
    aliases = {}
    if later is not None:
        operands.append(later)
        in_specs.append(anywhere)
        out_shape.append(jax.ShapeDtypeStruct(later.shape, later.dtype))
        out_specs.append(anywhere)
        aliases = {count + 1: 1}
    results = pl.pallas_call(
        functools.partial(merge_kernel, count),
        in_specs=in_specs,
        out_specs=out_specs,
        out_shape=out_shape,
        input_output_aliases=aliases,
        compiler_params=pltpu.CompilerParams(vmem_limit_bytes=VMEM_LIMIT),
        cost_estimate=pl.CostEstimate(
            flops=home.size, bytes_accessed=2 * home.size * (count + 2), transcendentals=0
        ),
        name="merge",
    )(*operands)
    return results if later is not None else (results[0], None)


def routes_of(shards):
    if shards == 4:
        routes = [
            (-1, [(0, 1), (1, 0), (2, 3), (3, 2)]),
            (-1, [(1, 2), (2, 1)]),
            (-1, [(0, 2), (1, 3), (2, 0), (3, 1)]),
            (2, [(2, 3), (1, 0)]),
        ]
    else:
        routes = []
        for step in range(1, shards):
            source = len(routes) - 2 if step > 1 else -1
            routes.append((source, [(at, at + 1) for at in range(step - 1, shards - 1)]))
            source = len(routes) - 2 if step > 1 else -1
            routes.append((source, [(at, at - 1) for at in range(1, shards - step + 1)]))
    held, depth = [list(range(shards))], [0]
    for source, pairs in routes:
        now = [-1] * shards
        for start, end in pairs:
            now[end] = held[source + 1][start]
        held.append(now)
        depth.append(depth[source + 1] + 1)
    return routes, held, depth


def visits_of(held, shards):
    visits = [
        [(piece, now[at]) for piece, now in enumerate(held) if now[at] >= 0]
        for at in range(shards)
    ]
    count = max(len(line) for line in visits)
    table = []
    for line in visits:
        pad = (-1, line[-1][1] if line else 0)
        line = line + [pad] * (count - len(line))
        table.append([piece for piece, _ in line] + [shard for _, shard in line])
    return np.array(table, np.int32), count


def project_kernel(
    count, carries, final, shards, steps, base, members, place_ref, lengths_ref, *refs
):
    pieces, refs = refs[:count], refs[count:]
    gain_ref, query_ref, key_ref, value_ref = refs[:4]
    refs = refs[4:]
    if carries:
        sums_in, squares_in = refs[:2]
        refs = refs[2:]
    frequency_ref, refs = refs[0], refs[1:]
    if final:
        out_ref, refs = refs[0], refs[1:]
    sums, squares, chosen = refs
    visit, step = pl.program_id(0), pl.program_id(1)
    visits = pl.num_programs(0)
    rows, depth = chosen.shape
    piece = place_ref[visit]

    @pl.when((visit == 0) & (step == 0))
    def _():
        sums[...] = sums_in[...] if carries else jnp.zeros_like(sums)
        squares[...] = squares_in[...] if carries else jnp.zeros_like(squares)

    for index in range(count):

        @pl.when(piece == index)
        def _():
            columns = pl.ds(pl.multiple_of(step * depth, depth), depth)
            chosen[...] = pieces[index][:, columns]

    @pl.when(piece >= 0)
    def _():
        wide = chosen[...].astype(F32)
        square = wide * wide
        part = square[:, :128]
        for at in range(128, depth, 128):
            part = part + square[:, at : at + 128]
        squares[...] += part
        scaled = (wide * gain_ref[...]).astype(BF16)
        at = 0
        for weight in (query_ref, key_ref, value_ref):
            columns = slice(at, at + weight.shape[1])
            sums[:, columns] += jnp.dot(scaled, weight[...], preferred_element_type=F32)
            at += weight.shape[1]

    if final:

        @pl.when((visit == visits - 1) & (step == steps - 1))
        def _():
            me = lax.axis_index("req")
            number = base + me * rows + iota((rows, HEAD_SIZE), 0)
            start = jnp.zeros((rows, HEAD_SIZE), jnp.int32)
            before = jnp.int32(0)
            for other in range(members):
                before = before + lengths_ref[other]
                start = jnp.where(number >= before, before, start)
            angle = (number - start).astype(F32) * frequency_ref[...]
            cosine, sine = jnp.cos(angle), jnp.sin(angle)
            sine = jnp.where(iota((rows, HEAD_SIZE), 1) < HEAD_SIZE // 2, -sine, sine)
            mean = jnp.sum(squares[...], axis=1, keepdims=True) / (shards * steps * depth)
            scale = lax.rsqrt(mean + 1e-05)
            turned = query_ref.shape[1] + key_ref.shape[1]
            for at in range(0, sums.shape[1], HEAD_SIZE):
                columns = slice(at, at + HEAD_SIZE)
                head = sums[:, columns] * scale
                if at < turned:
                    head = head * cosine + pltpu.roll(head, HEAD_SIZE // 2, 1) * sine
                out_ref[:, columns] = head.astype(BF16)


def project(final, shards, base, place, visits, lengths, pieces, gain, weights, carried, frequency):
    rows, width = pieces[0].shape
    depth = min(DEPTH, width)
    steps = width // depth
    columns = sum(weight.shape[1] for weight in weights)

    def block_of(visit, step, place_ref):
        step = jnp.where(place_ref[visit] < 0, steps - 1, step)
        return place_ref[visits + visit] * steps + step

    def whole(shape):
        return pl.BlockSpec(shape, lambda visit, step, place_ref, lengths_ref: (0, 0))

    def deep(block, dimension):
        def where(visit, step, place_ref, lengths_ref):
            at = block_of(visit, step, place_ref)
            return (at, 0) if dimension == 0 else (0, at)

        return pl.BlockSpec(block, where)

    operands = [*pieces, gain, *weights, *carried, frequency]
    in_specs = [whole((rows, width)) for _ in pieces]
    in_specs += [deep((1, depth), 1)]
    in_specs += [deep((depth, weight.shape[1]), 0) for weight in weights]
    in_specs += [whole(leaf.shape) for leaf in carried]
    in_specs += [whole((1, HEAD_SIZE))]
    scratch = [pltpu.VMEM((rows, depth), BF16)]
    if final:
        out_shape = [jax.ShapeDtypeStruct((rows, columns), BF16)]
        scratch = [pltpu.VMEM((rows, columns), F32), pltpu.VMEM((rows, 128), F32), *scratch]
    else:
        out_shape = [
            jax.ShapeDtypeStruct((rows, columns), F32),
            jax.ShapeDtypeStruct((rows, 128), F32),
        ]
    return pl.pallas_call(
        functools.partial(
            project_kernel,
            len(pieces),
            bool(carried),
            final,
            shards,
            steps,
            base,
            lengths.shape[0],
        ),
        grid_spec=pltpu.PrefetchScalarGridSpec(
            num_scalar_prefetch=2,
            grid=(visits, steps),
            in_specs=in_specs,
            out_specs=[whole(leaf.shape) for leaf in out_shape],
            scratch_shapes=scratch,
        ),
        out_shape=out_shape,
        compiler_params=pltpu.CompilerParams(vmem_limit_bytes=VMEM_LIMIT),
        cost_estimate=pl.CostEstimate(
            flops=2 * rows * width * columns * visits,
            bytes_accessed=2 * width * columns * visits + 8 * rows * columns,
            transcendentals=0,
        ),
        name="project",
    )(place, lengths, *operands)


def attend_kernel(chips, bases, sizes, query_width, key_width, lengths_ref, plan_ref, *refs):
    blocks, (attended_ref, cache_ref, rows_ref, sems) = refs[:-4], refs[-4:]
    workers = 2 * chips
    me = lax.axis_index("req")
    chip, core = lax.div(me, 2), lax.rem(me, 2)
    slots = cache_ref.shape[1]
    spans = slots // SPAN
    total = workers * sum(sizes)
    copies = []
    for chunk, (base, rows) in enumerate(zip(bases, sizes)):
        for hop in range(chips):
            source = lax.rem(chip - hop + chips, chips) * 2
            for twin in range(2):
                owner = source + (core if twin == 0 else 1 - core)
                index = (chunk * chips + hop) * 2 + twin
                at = pl.multiple_of(base + owner * rows, ALIGN)
                copies.append(
                    pltpu.make_async_copy(
                        blocks[index], rows_ref.at[pl.ds(at, rows), :], sems.at[index]
                    )
                )
    for copy in copies:
        copy.start()
    pad = rows_ref.shape[0] - total
    rows_ref[total:, :] = jnp.zeros((pad, rows_ref.shape[1]), BF16)
    for copy in copies:
        copy.wait()

    def aligned(row):
        first = pl.multiple_of(lax.div(row, ALIGN) * ALIGN, ALIGN)
        return first, row - first

    start, length = run_of(lengths_ref, me, workers)
    first, shift = aligned(start)
    reach = slots + SPAN
    row, column = iota((slots, reach), 0), iota((slots, reach), 1)
    hot = ((column == row + shift) & (row < length)).astype(BF16)
    for half in range(2):
        window = rows_ref[
            pl.ds(first, reach),
            query_width + half * key_width : query_width + (half + 1) * key_width,
        ]
        cache_ref[half] = jnp.dot(hot, window, preferred_element_type=F32).astype(BF16)

    heads, key_heads = query_width // HEAD_SIZE, key_width // HEAD_SIZE
    group = heads // key_heads
    factor = math.log2(math.e) / math.sqrt(HEAD_SIZE)
    for slot in range(spans):
        span = plan_ref[me * spans + slot]
        source = lax.div(span, spans)
        part = lax.rem(span, spans)
        start, length = run_of(lengths_ref, source, workers)
        offset = part * SPAN
        out_rows = slice(slot * SPAN, (slot + 1) * SPAN)
        dead = offset >= length

        @pl.when(dead)
        def _():
            attended_ref[out_rows, :] = jnp.zeros((SPAN, query_width), BF16)

        for count in range(1, spans + 1):

            @pl.when(jnp.logical_not(dead) & (part == count - 1))
            def _():
                first, shift = aligned(start + offset)
                hot = iota((SPAN, 2 * SPAN), 1) == iota((SPAN, 2 * SPAN), 0) + shift
                queries = jnp.dot(
                    hot.astype(BF16),
                    rows_ref[pl.ds(first, 2 * SPAN), :query_width],
                    preferred_element_type=F32,
                ).astype(BF16)
                reach = (count + 1) * SPAN
                first, shift = aligned(start)
                key_pos = iota((SPAN, reach), 1) - shift
                query_pos = (count - 1) * SPAN + iota((SPAN, reach), 0)
                allowed = (key_pos >= 0) & (key_pos <= query_pos) & (key_pos < length)
                bias = jnp.where(allowed, 0.0, -1e30)
                bias = jnp.concatenate([bias] * group, axis=0)
                live = (count - 1) * SPAN + iota((SPAN, HEAD_SIZE), 0) < length
                for head in range(key_heads):
                    stacked = jnp.concatenate(
                        [
                            queries[:, at * HEAD_SIZE : (at + 1) * HEAD_SIZE]
                            for at in range(head * group, (head + 1) * group)
                        ],
                        axis=0,
                    )
                    left = query_width + head * HEAD_SIZE
                    keys = rows_ref[pl.ds(first, reach), left : left + HEAD_SIZE]
                    left += key_width
                    values = rows_ref[pl.ds(first, reach), left : left + HEAD_SIZE]
                    scores = lax.dot_general(
                        stacked, keys, (((1,), (1,)), ((), ())), preferred_element_type=F32
                    )
                    scores = scores + bias
                    top = jnp.max(scores, axis=1, keepdims=True)
                    weights = jnp.exp2((scores - top) * factor)
                    norm = jnp.sum(weights, axis=1, keepdims=True)
                    mixed = jnp.dot(weights.astype(BF16), values, preferred_element_type=F32)
                    mixed = mixed / norm
                    for at in range(group):
                        left = (head * group + at) * HEAD_SIZE
                        attended_ref[out_rows, left : left + HEAD_SIZE] = jnp.where(
                            live, mixed[at * SPAN : (at + 1) * SPAN], 0.0
                        ).astype(BF16)


def attend(chips, bases, sizes, query_width, key_width, slots, lengths, plan, blocks):
    width = query_width + 2 * key_width
    total = 2 * chips * sum(sizes)
    return pl.pallas_call(
        functools.partial(attend_kernel, chips, bases, sizes, query_width, key_width),
        in_specs=[pl.BlockSpec(memory_space=pltpu.SMEM)] * 2
        + [pl.BlockSpec(memory_space=pl.ANY)] * len(blocks),
        out_specs=[pl.BlockSpec(memory_space=pltpu.VMEM)] * 2,
        out_shape=[
            jax.ShapeDtypeStruct((slots, query_width), BF16),
            jax.ShapeDtypeStruct((2, slots, key_width), BF16),
        ],
        scratch_shapes=[
            pltpu.VMEM((total + slots + SPAN, width), BF16),
            pltpu.SemaphoreType.DMA((len(blocks),)),
        ],
        compiler_params=pltpu.CompilerParams(vmem_limit_bytes=VMEM_LIMIT),
        name="attend",
    )(lengths, plan, *blocks)


def shift_chips(value, hop, chips):
    pairs = [(2 * x + c, 2 * ((x + hop) % chips) + c) for x in range(chips) for c in range(2)]
    return lax.ppermute(value, "req", pairs)


def swap_cores(value, chips):
    return lax.ppermute(value, "req", [(d, d ^ 1) for d in range(2 * chips)])


def local(
    chips, shards, tokens, norm_gain, w_query, key_weight, value_weight, lengths, plan
):
    workers = 2 * chips
    slots = tokens.shape[0]
    live = slots // 2
    sizes = [live * share // sum(SHARES) // ALIGN * ALIGN for share in SHARES]
    sizes[-1] = live - sum(sizes[:-1])
    bases = [workers * sum(sizes[:chunk]) for chunk in range(len(sizes))]
    weights = (w_query, key_weight, value_weight)
    gain = norm_gain.astype(F32).reshape(1, -1)
    halfway = HEAD_SIZE // 2
    frequency = np.exp(-np.arange(halfway) * 2.0 / HEAD_SIZE * math.log(500000.0))
    frequency = jnp.asarray(np.tile(frequency, 2)[None, :], F32)

    twin = swap_cores(tokens, chips)
    dealt = [
        *deal(chips, bases[:1], sizes[:1], lengths, tokens, twin),
        *deal(chips, bases[1:], sizes[1:], lengths, tokens, twin),
    ]
    homes, aways = dealt[::2], dealt[1::2]
    held = []
    for chunk in range(len(sizes)):
        arrived = [shift_chips(aways[chunk][hop - 1], hop, chips) for hop in range(1, chips)]
        later = aways[chunk + 1] if chunk + 1 < len(sizes) else None
        block, later = merge(homes[chunk], arrived, later)
        if later is not None:
            aways[chunk + 1] = later
        held.append(block)

    routes, owned, depth = routes_of(shards)
    lines = []
    for block in held:
        line = [block]
        for source, pairs in routes:
            line.append(lax.ppermute(line[source + 1], "tp", pairs))
        lines.append(line)

    early = [piece for piece in range(len(owned)) if depth[piece] < max(depth)]
    late = [piece for piece in range(len(owned)) if depth[piece] == max(depth)]
    tables, counts = zip(
        *(
            visits_of([owned[piece] for piece in group], shards)
            for group in (range(len(owned)), early, late)
        )
    )
    table = jnp.asarray(np.concatenate(tables, axis=1))
    table = lax.dynamic_index_in_dim(table, lax.axis_index("tp"), 0, keepdims=False)
    places = [
        table[2 * sum(counts[:at]) : 2 * sum(counts[: at + 1])] for at in range(3)
    ]

    blocks = []
    for chunk, (base, line) in enumerate(zip(bases, lines)):
        common = (gain, weights)
        if chunk + 1 < len(sizes):
            (block,) = project(
                True, shards, base, places[0], counts[0], lengths, line, *common, (), frequency
            )
        else:
            pieces = [line[piece] for piece in early]
            carried = project(
                False, shards, base, places[1], counts[1], lengths, pieces, *common, (), frequency
            )
            pieces = [line[piece] for piece in late]
            (block,) = project(
                True,
                shards,
                base,
                places[2],
                counts[2],
                lengths,
                pieces,
                *common,
                carried,
                frequency,
            )
        here = [block] + [shift_chips(block, hop, chips) for hop in range(1, chips)]
        for piece in here:
            blocks += [piece, swap_cores(piece, chips)]
    return tuple(
        attend(
            chips,
            bases,
            sizes,
            w_query.shape[1],
            key_weight.shape[1],
            slots,
            lengths,
            plan,
            blocks,
        )
    )


def solution(mesh):
    placed = (
        P(("groups", "req"), "tp"),
        P(),
        P(None, "tp"),
        P(None, "tp"),
        P(None, "tp"),
        P("groups"),
        P("groups"),
    )
    return jax.shard_map(
        functools.partial(local, mesh.shape["req"] // 2, mesh.shape["tp"]),
        mesh=mesh,
        in_specs=placed,
        out_specs=(P(("groups", "req"), "tp"), P(None, ("groups", "req"), "tp")),
        check_vma=False,
    )
```

time: 178 us -> 170 us (0.955)
  the two profiles are of different devices: /device:TPU:14 before, /device:TPU:0 now
where the time goes in v3:
time: 170 us; the launch traced here: 168 us
  Pallas kernels  71 us (42%)
  waiting for transfers between devices  54.8 us (32%)
  starting transfers between devices  32.4 us (19%)
  local copies, waits for them, and re-layouts  8.5 us (5%)
    pallas_call x4, Pallas kernels, project(): pl.pallas_call(functools.partial(project_kernel, len(pieces), bool(carrie...  47 us
    ppermute x12, waiting for transfers between devices, local(): line.append(lax.ppermute(line[source + 1], 'tp', pairs))  26.9 us
    ppermute x6, waiting for transfers between devices, shift_chips(): return lax.ppermute(value, 'req', pairs)  22.5 us
    ppermute x12, starting transfers between devices, local(): line.append(lax.ppermute(line[source + 1], 'tp', pairs))  21.2 us
    pallas_call x2, Pallas kernels, deal(): pl.pallas_call(functools.partial(deal_kernel, chips, bases, sizes), grid=...  10.3 us
    ppermute x6, starting transfers between devices, shift_chips(): return lax.ppermute(value, 'req', pairs)  9.69 us
    pallas_call x1, Pallas kernels, attend(): pl.pallas_call(functools.partial(attend_kernel, chips, bases, sizes, quer...  8.23 us
    unnamed x56, local copies, waits for them, and re-layouts  6.61 us
  transfers between devices with their start and end apart: 25, of which 8 were waited for; matrix products, arithmetic and copies ran while one was open for 1% of the time, Pallas kernels for 32%

profile of v3, /device:TPU:0, one launch (start us, length us, event | category | flops | bytes accessed | tf_op | source)
XLA Modules:
  0.0 168.5 jit_solution(10216320364388512084)
XLA Ops:
  0.6 0.5 collective-permute-start
  1.1 4.0 %collective-permute-done.twin_ref = bf16[512,2048]{1,0:T(8,128)(2,1)S(1)} collective-permute-done((bf16[512,2048]{1,0:T(8,128)(2,1)}, bf16[512,2048]{1,0:T(8,128)(2,1)S(1)}, u32[]{:S(2)}, u32[]{:S(2)}) %collective-permute-start) | collective-permute-done | bytes 2097184 | tf_op jit(solution)/shard_map/ppermute | solution.py:433
  5.1 1.3 copy-done
  6.4 4.7 %deal.2 = (bf16[64,2048]{1,0:T(8,128)(2,1)}, bf16[1,64,2048]{2,1,0:T(8,128)(2,1)}) custom-call(s32[4]{0:T(128)} %lengths_ref.13, bf16[512,2048]{1,0:T(8,128)(2,1)} %own_ref.3, bf16[512,2048]{1,0:T(8,128)(2,1)} %copy-done), custom_call_target="tpu_custom_call" | custom-call | flops 536870912 | bytes 4718592 | tf_op jit(solution)/shard_map/deal/pallas_call | solution.py:72
  11.2 2.9 %collective-permute-start.1 = (bf16[64,2048]{1,0:T(8,128)(2,1)}, bf16[64,2048]{1,0:T(8,128)(2,1)S(1)}, u32[]{:S(2)}, u32[]{:S(2)}) collective-permute-start(bf16[64,2048]{1,0:T(8,128)(2,1)} %bitcast.16), channel_id=1, source_target_pairs={{0,8},{4,12},{8,0},{12,4},{1,9},{5,13},{9,1},{13,5},{2,10},{6,14},... | collective-permute-start | bytes 786440 | tf_op jit(solution)/shard_map/ppermute | solution.py:429
  14.0 5.5 %deal.3 = (bf16[128,2048]{1,0:T(8,128)(2,1)}, bf16[1,128,2048]{2,1,0:T(8,128)(2,1)}, bf16[64,2048]{1,0:T(8,128)(2,1)}, bf16[1,64,2048]{2,1,0:T(8,128)(2,1)}) custom-call(s32[4]{0:T(128)} %lengths_ref.13, bf16[512,2048]{1,0:T(8,128)(2,1)} %own_ref.3, bf16[512,2048]{1,0:T(8,128)(2,1)} %copy-done), custom_call_target="tpu_custom_call" | custom-call | flops 1610612736 | bytes 5767168 | tf_op jit(solution)/shard_map/deal/pallas_call | solution.py:72
  19.6 1.3 collective-permute-done.1.refs_0_
  20.8 0.7 copy-done.20
  21.6 1.8 %merge.3 = (bf16[64,2048]{1,0:T(8,128)(2,1)}, bf16[1,128,2048]{2,1,0:T(8,128)(2,1)}) custom-call(bf16[64,2048]{1,0:T(8,128)(2,1)} %get-tuple-element.14.home_ref, bf16[64,2048]{1,0:T(8,128)(2,1)} %copy-done.20, bf16[1,128,2048]{2,1,0:T(8,128)(2,1)} %get-tuple-element.16.refs_1_), custom_call_target="tpu_custom_call", output_to_operand_aliasing={{1}: (2, {})} | custom-call | flops 131072 | bytes 786432 | tf_op jit(solution)/shard_map/merge/pallas_call | solution.py:111
  23.3 1.7 %collective-permute-start.9 = (bf16[128,2048]{1,0:T(8,128)(2,1)}, bf16[128,2048]{1,0:T(8,128)(2,1)S(1)}, u32[]{:S(2)}, u32[]{:S(2)}) collective-permute-start(bf16[128,2048]{1,0:T(8,128)(2,1)} %bitcast.14), channel_id=1, source_target_pairs={{0,8},{4,12},{8,0},{12,4},{1,9},{5,13},{9,1},{13,5},{2,10},{6,14},... | collective-permute-start | bytes 1572872 | tf_op jit(solution)/shard_map/ppermute | solution.py:429
  25.1 11.9 %collective-permute-done.9.refs_0_ = bf16[128,2048]{1,0:T(8,128)(2,1)S(1)} collective-permute-done((bf16[128,2048]{1,0:T(8,128)(2,1)}, bf16[128,2048]{1,0:T(8,128)(2,1)S(1)}, u32[]{:S(2)}, u32[]{:S(2)}) %collective-permute-start.9) | collective-permute-done | bytes 524320 | tf_op jit(solution)/shard_map/ppermute | solution.py:429
  37.0 0.8 copy-done.3
  37.8 2.0 %merge.4 = (bf16[128,2048]{1,0:T(8,128)(2,1)}, bf16[1,64,2048]{2,1,0:T(8,128)(2,1)}) custom-call(bf16[128,2048]{1,0:T(8,128)(2,1)} %get-tuple-element.18.home_ref, bf16[128,2048]{1,0:T(8,128)(2,1)} %copy-done.3, bf16[1,64,2048]{2,1,0:T(8,128)(2,1)} %get-tuple-element.20.refs_1_), custom_call_target="tpu_custom_call", output_to_operand_aliasing={{1}: (2, {})} | custom-call | flops 262144 | bytes 1572864 | tf_op jit(solution)/shard_map/merge/pallas_call | solution.py:111
  39.8 2.5 %collective-permute-start.12 = (bf16[128,2048]{1,0:T(8,128)(2,1)}, bf16[128,2048]{1,0:T(8,128)(2,1)S(1)}, u32[]{:S(2)}, u32[]{:S(2)}) collective-permute-start(bf16[128,2048]{1,0:T(8,128)(2,1)} %get-tuple-element.21.refs_0_), channel_id=1, source_target_pairs={{0,2},{1,3},{2,0},{3,1},{4,6},{5,7},{6,4},{7,5},{8,10},{9,11},{10,... | collective-permute-start | bytes 1572872 | tf_op jit(solution)/shard_map/ppermute | solution.py:471
  42.4 0.7 collective-permute-start.11
  43.0 2.9 %collective-permute-start.10 = (bf16[128,2048]{1,0:T(8,128)(2,1)}, bf16[128,2048]{1,0:T(8,128)(2,1)S(1)}, u32[]{:S(2)}, u32[]{:S(2)}) collective-permute-start(bf16[128,2048]{1,0:T(8,128)(2,1)} %get-tuple-element.21.refs_0_), channel_id=1, source_target_pairs={{0,1},{1,0},{2,3},{3,2},{4,5},{5,4},{6,7},{7,6},{8,9},{9,8},{10,11... | collective-permute-start | bytes 1572872 | tf_op jit(solution)/shard_map/ppermute | solution.py:471
  45.9 19.6 %collective-permute-done.12.refs_3_ = bf16[128,2048]{1,0:T(8,128)(2,1)S(1)} collective-permute-done((bf16[128,2048]{1,0:T(8,128)(2,1)}, bf16[128,2048]{1,0:T(8,128)(2,1)S(1)}, u32[]{:S(2)}, u32[]{:S(2)}) %collective-permute-start.12) | collective-permute-done | bytes 524320 | tf_op jit(solution)/shard_map/ppermute | solution.py:471
  65.6 1.3 collective-permute-start.13
  66.8 3.7 %collective-permute-start.4 = (bf16[64,2048]{1,0:T(8,128)(2,1)}, bf16[64,2048]{1,0:T(8,128)(2,1)S(1)}, u32[]{:S(2)}, u32[]{:S(2)}) collective-permute-start(bf16[64,2048]{1,0:T(8,128)(2,1)} %get-tuple-element.17.refs_0_), channel_id=1, source_target_pairs={{0,2},{1,3},{2,0},{3,1},{4,6},{5,7},{6,4},{7,5},{8,10},{9,11},{10,... | collective-permute-start | bytes 786440 | tf_op jit(solution)/shard_map/ppermute | solution.py:471
  70.5 1.5 collective-permute-start.17
  72.0 0.7 constant_dynamic-slice_fusion
  72.7 0.6 reshape.14
  73.3 0.7 slice_bitcast_fusion
  74.0 4.3 %collective-permute-done.17.refs_0_ = bf16[64,2048]{1,0:T(8,128)(2,1)S(1)} collective-permute-done((bf16[64,2048]{1,0:T(8,128)(2,1)}, bf16[64,2048]{1,0:T(8,128)(2,1)S(1)}, u32[]{:S(2)}, u32[]{:S(2)}) %collective-permute-start.17) | collective-permute-done | bytes 262176 | tf_op jit(solution)/shard_map/ppermute | solution.py:429
  78.3 0.7 collective-permute-start.3
  79.0 0.0 copy-done.19
  79.0 1.8 %merge.5.refs_0_ = bf16[64,2048]{1,0:T(8,128)(2,1)} custom-call(bf16[64,2048]{1,0:T(8,128)(2,1)} %get-tuple-element.22.home_ref, bf16[64,2048]{1,0:T(8,128)(2,1)} %copy-done.19), custom_call_target="tpu_custom_call" | custom-call | flops 131072 | bytes 786432 | tf_op jit(solution)/shard_map/merge/pallas_call | solution.py:111
  80.8 7.3 %collective-permute-done.4.refs_3_ = bf16[64,2048]{1,0:T(8,128)(2,1)S(1)} collective-permute-done((bf16[64,2048]{1,0:T(8,128)(2,1)}, bf16[64,2048]{1,0:T(8,128)(2,1)S(1)}, u32[]{:S(2)}, u32[]{:S(2)}) %collective-permute-start.4) | collective-permute-done | bytes 262176 | tf_op jit(solution)/shard_map/ppermute | solution.py:471
  88.0 0.0 collective-permute-start.2
  88.0 0.0 collective-permute-done.11.refs_2_
  88.0 0.0 copy-start.5
  88.0 1.3 collective-permute-start.5
  89.3 0.0 collective-permute-done.10.refs_1_
  89.4 0.0 copy-start.6
  89.4 0.7 collective-permute-start.21
  90.1 5.4 %collective-permute-start.18 = (bf16[64,2048]{1,0:T(8,128)(2,1)}, bf16[64,2048]{1,0:T(8,128)(2,1)S(1)}, u32[]{:S(2)}, u32[]{:S(2)}) collective-permute-start(bf16[64,2048]{1,0:T(8,128)(2,1)} %merge.5.refs_0_), channel_id=1, source_target_pairs={{0,2},{1,3},{2,0},{3,1},{4,6},{5,7},{6,4},{7,5},{8,10},{9,11},{10,... | collective-permute-start | bytes 786440 | tf_op jit(solution)/shard_map/ppermute | solution.py:471
  95.5 15.0 %project.5.refs_4_ = bf16[128,1536]{1,0:T(8,128)(2,1)} custom-call(s32[8]{0:T(128)} %get-tuple-element.27.place_ref, s32[4]{0:T(128)} %lengths_ref.13, bf16[128,2048]{1,0:T(8,128)(2,1)} %get-tuple-element.21.refs_0_, bf16[128,2048]{1,0:T(8,128)(2,1)} %copy-done.6, bf16[128,2048]{1,0:T(8,128)(2,1)} %copy-done.5, bf16[128,2048]{1,0:T(8,128)(2,1)} %copy-done.4, ...), custom_call_target="tpu_custom_call" | custom-call | flops 3221225472 | bytes 26738688 | tf_op jit(solution)/shard_map/project/pallas_call | solution.py:270
  110.5 0.0 collective-permute-done.3.refs_2_
  110.5 0.0 copy-start.12
  110.5 0.8 collective-permute-start.20
  111.4 1.5 collective-permute-start.15
  112.9 0.6 slice_bitcast_fusion.1.place_ref
  113.4 1.3 collective-permute-start.19
  114.7 0.7 copy-done.16
  115.5 14.4 %project.4.refs_0_ = bf16[64,1536]{1,0:T(8,128)(2,1)} custom-call(s32[8]{0:T(128)} %get-tuple-element.27.place_ref, s32[4]{0:T(128)} %lengths_ref.13, bf16[64,2048]{1,0:T(8,128)(2,1)} %get-tuple-element.17.refs_0_, bf16[64,2048]{1,0:T(8,128)(2,1)} %copy-done.15, bf16[64,2048]{1,0:T(8,128)(2,1)} %copy-done.12, bf16[64,2048]{1,0:T(8,128)(2,1)} %copy-done.11, ...), custom_call_target="tpu_custom_call" | custom-call | flops 1610612736 | bytes 25952256 | tf_op jit(solution)/shard_map/project/pallas_call | solution.py:270
  129.9 0.6 collective-permute-start.7
  130.5 0.0 copy-start.17
  130.5 0.7 copy-done.13
  131.2 0.1 copy-done.17
  131.3 11.7 %project.6 = (f32[64,1536]{1,0:T(8,128)}, f32[64,128]{1,0:T(8,128)}) custom-call(s32[8]{0:T(128)} %get-tuple-element.26.place_ref, s32[4]{0:T(128)} %lengths_ref.13, bf16[64,2048]{1,0:T(8,128)(2,1)} %merge.5.refs_0_, bf16[64,2048]{1,0:T(8,128)(2,1)} %copy-done.17, bf16[64,2048]{1,0:T(8,128)(2,1)} %copy-done.13, bf16[64,2048]{1,0:T(8,128)(2,1)} %copy-done.14, ...), custom_call_target="tpu_custom_call" | custom-call | flops 1610612736 | bytes 25952256 | tf_op jit(solution)/shard_map/project/pallas_call | solution.py:270
  143.0 0.0 copy-start.18
  143.0 0.7 copy-done.18
  143.7 5.9 %project.7.refs_8_ = bf16[64,1536]{1,0:T(8,128)(2,1)} custom-call(s32[2]{0:T(128)} %slice_bitcast_fusion.1.place_ref, s32[4]{0:T(128)} %lengths_ref.13, bf16[64,2048]{1,0:T(8,128)(2,1)} %copy-done.18, f32[1,8192]{1,0:T(1,128)} %bitcast.13, bf16[8192,1024]{1,0:T(8,128)(2,1)} %refs_2_.1, bf16[8192,256]{1,0:T(8,128)(2,1)} %refs_3_.1, ...), custom_call_target="tpu_custom_call" | custom-call | flops 402653184 | bytes 7077888 | tf_op jit(solution)/shard_map/project/pallas_call | solution.py:270
  149.6 1.5 collective-permute-start.23
  151.0 0.2 collective-permute-start.14
  151.2 0.3 collective-permute-start.16
  151.6 0.2 collective-permute-start.8
  151.7 0.3 collective-permute-start.22
  152.1 5.0 %collective-permute-done.23.refs_10_ = bf16[64,1536]{1,0:T(8,128)(2,1)S(1)} collective-permute-done((bf16[64,1536]{1,0:T(8,128)(2,1)}, bf16[64,1536]{1,0:T(8,128)(2,1)S(1)}, u32[]{:S(2)}, u32[]{:S(2)}) %collective-permute-start.23) | collective-permute-done | bytes 196640 | tf_op jit(solution)/shard_map/ppermute | solution.py:429
  157.1 1.4 collective-permute-done.24.refs_11_
  158.5 0.6 copy-done.26
  159.2 0.1 copy-done.9
  159.3 0.7 copy-done.10
  160.0 8.2 %attend.1 = (bf16[512,1024]{1,0:T(8,128)(2,1)}, bf16[2,512,256]{2,1,0:T(8,128)(2,1)}) custom-call(s32[4]{0:T(128)} %lengths_ref.13, s32[16]{0:T(128)} %plan_ref.1, bf16[64,1536]{1,0:T(8,128)(2,1)} %project.4.refs_0_, bf16[64,1536]{1,0:T(8,128)(2,1)} %copy-done.22, bf16[64,1536]{1,0:T(8,128)(2,1)} %copy-done.21, bf16[64,1536]{1,0:T(8,128)(2,1)} %copy-done.24, ...), custom_call_target="tpu_custom_call" | custom-call | tf_op jit(solution)/shard_map/attend/pallas_call | solution.py:409
  (56 shorter events, 0.1 us)
Async XLA Ops:
  0.6 4.5 %collective-permute-start = (bf16[512,2048]{1,0:T(8,128)(2,1)}, bf16[512,2048]{1,0:T(8,128)(2,1)S(1)}, u32[]{:S(2)}, u32[]{:S(2)}) collective-permute-start(bf16[512,2048]{1,0:T(8,128)(2,1)} %own_ref.3), channel_id=1, source_target_pairs={{0,4},{4,0},{8,12},{12,8},{1,5},{5,1},{9,13},{13,9},{2,6},{6,2},{1... | collective-permute-start | bytes 6291464 | tf_op jit(solution)/shard_map/ppermute | solution.py:433
  5.1 1.3 copy-start
  11.2 61.5 %copy-start.27 = (bf16[8192]{0:T(1024)(128)(2,1)S(1)}, bf16[8192]{0:T(1024)(128)(2,1)}, u32[]{:S(2)}) copy-start(bf16[8192]{0:T(1024)(128)(2,1)} %param.10) | copy-start | bytes 49156
  11.2 9.7 %collective-permute-start.1 = (bf16[64,2048]{1,0:T(8,128)(2,1)}, bf16[64,2048]{1,0:T(8,128)(2,1)S(1)}, u32[]{:S(2)}, u32[]{:S(2)}) collective-permute-start(bf16[64,2048]{1,0:T(8,128)(2,1)} %bitcast.16), channel_id=1, source_target_pairs={{0,8},{4,12},{8,0},{12,4},{1,9},{5,13},{9,1},{13,5},{2,10},{6,14},... | collective-permute-start | bytes 786440 | tf_op jit(solution)/shard_map/ppermute | solution.py:429
  20.8 0.7 copy-start.20
  23.3 13.7 %collective-permute-start.9 = (bf16[128,2048]{1,0:T(8,128)(2,1)}, bf16[128,2048]{1,0:T(8,128)(2,1)S(1)}, u32[]{:S(2)}, u32[]{:S(2)}) collective-permute-start(bf16[128,2048]{1,0:T(8,128)(2,1)} %bitcast.14), channel_id=1, source_target_pairs={{0,8},{4,12},{8,0},{12,4},{1,9},{5,13},{9,1},{13,5},{2,10},{6,14},... | collective-permute-start | bytes 1572872 | tf_op jit(solution)/shard_map/ppermute | solution.py:429
  37.0 0.8 copy-start.3
  39.8 25.7 %collective-permute-start.12 = (bf16[128,2048]{1,0:T(8,128)(2,1)}, bf16[128,2048]{1,0:T(8,128)(2,1)S(1)}, u32[]{:S(2)}, u32[]{:S(2)}) collective-permute-start(bf16[128,2048]{1,0:T(8,128)(2,1)} %get-tuple-element.21.refs_0_), channel_id=1, source_target_pairs={{0,2},{1,3},{2,0},{3,1},{4,6},{5,7},{6,4},{7,5},{8,10},{9,11},{10,... | collective-permute-start | bytes 1572872 | tf_op jit(solution)/shard_map/ppermute | solution.py:471
  42.4 45.7 %collective-permute-start.11 = (bf16[128,2048]{1,0:T(8,128)(2,1)}, bf16[128,2048]{1,0:T(8,128)(2,1)S(1)}, u32[]{:S(2)}, u32[]{:S(2)}) collective-permute-start(bf16[128,2048]{1,0:T(8,128)(2,1)} %get-tuple-element.21.refs_0_), channel_id=1, source_target_pairs={{1,2},{2,1},{5,6},{6,5},{9,10},{10,9},{13,14},{14,13},{17,18},{18,... | collective-permute-start | bytes 1572872 | tf_op jit(solution)/shard_map/ppermute | solution.py:471
  43.0 46.3 %collective-permute-start.10 = (bf16[128,2048]{1,0:T(8,128)(2,1)}, bf16[128,2048]{1,0:T(8,128)(2,1)S(1)}, u32[]{:S(2)}, u32[]{:S(2)}) collective-permute-start(bf16[128,2048]{1,0:T(8,128)(2,1)} %get-tuple-element.21.refs_0_), channel_id=1, source_target_pairs={{0,1},{1,0},{2,3},{3,2},{4,5},{5,4},{6,7},{7,6},{8,9},{9,8},{10,11... | collective-permute-start | bytes 1572872 | tf_op jit(solution)/shard_map/ppermute | solution.py:471
  65.6 29.9 %copy-start.4 = (bf16[128,2048]{1,0:T(8,128)(2,1)}, bf16[128,2048]{1,0:T(8,128)(2,1)S(1)}, u32[]{:S(2)}) copy-start(bf16[128,2048]{1,0:T(8,128)(2,1)S(1)} %collective-permute-done.12.refs_3_) | copy-start | bytes 1572868
  65.6 24.5 %collective-permute-start.13 = (bf16[128,2048]{1,0:T(8,128)(2,1)S(1)}, bf16[128,2048]{1,0:T(8,128)(2,1)S(1)}, u32[]{:S(2)}, u32[]{:S(2)}) collective-permute-start(bf16[128,2048]{1,0:T(8,128)(2,1)S(1)} %collective-permute-done.12.refs_3_), channel_id=1, source_target_pairs={{2,3},{1,0},{6,7},{5,4},{10,11},{9,8},{14,15},{13,12},{18,19},{17,... | collective-permute-start | bytes 1572872 | tf_op jit(solution)/shard_map/ppermute | solution.py:471
  66.8 21.2 %collective-permute-start.4 = (bf16[64,2048]{1,0:T(8,128)(2,1)}, bf16[64,2048]{1,0:T(8,128)(2,1)S(1)}, u32[]{:S(2)}, u32[]{:S(2)}) collective-permute-start(bf16[64,2048]{1,0:T(8,128)(2,1)} %get-tuple-element.17.refs_0_), channel_id=1, source_target_pairs={{0,2},{1,3},{2,0},{3,1},{4,6},{5,7},{6,4},{7,5},{8,10},{9,11},{10,... | collective-permute-start | bytes 786440 | tf_op jit(solution)/shard_map/ppermute | solution.py:471
  70.5 7.8 %collective-permute-start.17 = (bf16[64,2048]{1,0:T(8,128)(2,1)}, bf16[64,2048]{1,0:T(8,128)(2,1)S(1)}, u32[]{:S(2)}, u32[]{:S(2)}) collective-permute-start(bf16[64,2048]{1,0:T(8,128)(2,1)} %bitcast.15), channel_id=1, source_target_pairs={{0,8},{4,12},{8,0},{12,4},{1,9},{5,13},{9,1},{13,5},{2,10},{6,14},... | collective-permute-start | bytes 786440 | tf_op jit(solution)/shard_map/ppermute | solution.py:429
  78.3 0.7 copy-start.19
  78.3 32.2 %collective-permute-start.3 = (bf16[64,2048]{1,0:T(8,128)(2,1)}, bf16[64,2048]{1,0:T(8,128)(2,1)S(1)}, u32[]{:S(2)}, u32[]{:S(2)}) collective-permute-start(bf16[64,2048]{1,0:T(8,128)(2,1)} %get-tuple-element.17.refs_0_), channel_id=1, source_target_pairs={{1,2},{2,1},{5,6},{6,5},{9,10},{10,9},{13,14},{14,13},{17,18},{18,... | collective-permute-start | bytes 786440 | tf_op jit(solution)/shard_map/ppermute | solution.py:471
  88.0 22.5 %copy-start.11 = (bf16[64,2048]{1,0:T(8,128)(2,1)}, bf16[64,2048]{1,0:T(8,128)(2,1)S(1)}, u32[]{:S(2)}) copy-start(bf16[64,2048]{1,0:T(8,128)(2,1)S(1)} %collective-permute-done.4.refs_3_) | copy-start | bytes 786436
  88.0 23.3 %collective-permute-start.2 = (bf16[64,2048]{1,0:T(8,128)(2,1)}, bf16[64,2048]{1,0:T(8,128)(2,1)S(1)}, u32[]{:S(2)}, u32[]{:S(2)}) collective-permute-start(bf16[64,2048]{1,0:T(8,128)(2,1)} %get-tuple-element.17.refs_0_), channel_id=1, source_target_pairs={{0,1},{1,0},{2,3},{3,2},{4,5},{5,4},{6,7},{7,6},{8,9},{9,8},{10,11... | collective-permute-start | bytes 786440 | tf_op jit(solution)/shard_map/ppermute | solution.py:471
  88.0 7.5 %copy-start.5 = (bf16[128,2048]{1,0:T(8,128)(2,1)}, bf16[128,2048]{1,0:T(8,128)(2,1)S(1)}, u32[]{:S(2)}) copy-start(bf16[128,2048]{1,0:T(8,128)(2,1)S(1)} %collective-permute-done.11.refs_2_) | copy-start | bytes 1572868
  88.0 26.7 %collective-permute-start.5 = (bf16[64,2048]{1,0:T(8,128)(2,1)S(1)}, bf16[64,2048]{1,0:T(8,128)(2,1)S(1)}, u32[]{:S(2)}, u32[]{:S(2)}) collective-permute-start(bf16[64,2048]{1,0:T(8,128)(2,1)S(1)} %collective-permute-done.4.refs_3_), channel_id=1, source_target_pairs={{2,3},{1,0},{6,7},{5,4},{10,11},{9,8},{14,15},{13,12},{18,19},{17,... | collective-permute-start | bytes 786440 | tf_op jit(solution)/shard_map/ppermute | solution.py:471
  89.4 6.1 %copy-start.6 = (bf16[128,2048]{1,0:T(8,128)(2,1)}, bf16[128,2048]{1,0:T(8,128)(2,1)S(1)}, u32[]{:S(2)}) copy-start(bf16[128,2048]{1,0:T(8,128)(2,1)S(1)} %collective-permute-done.10.refs_1_) | copy-start | bytes 1572868
  89.4 41.1 %collective-permute-start.21 = (bf16[64,2048]{1,0:T(8,128)(2,1)}, bf16[64,2048]{1,0:T(8,128)(2,1)S(1)}, u32[]{:S(2)}, u32[]{:S(2)}) collective-permute-start(bf16[64,2048]{1,0:T(8,128)(2,1)} %merge.5.refs_0_), channel_id=1, source_target_pairs={{1,2},{2,1},{5,6},{6,5},{9,10},{10,9},{13,14},{14,13},{17,18},{18,... | collective-permute-start | bytes 786440 | tf_op jit(solution)/shard_map/ppermute | solution.py:471
  90.1 5.4 %copy-start.7 = (bf16[128,2048]{1,0:T(8,128)(2,1)}, bf16[128,2048]{1,0:T(8,128)(2,1)S(1)}, u32[]{:S(2)}) copy-start(bf16[128,2048]{1,0:T(8,128)(2,1)S(1)} %collective-permute-done.13.refs_4_) | copy-start | bytes 1572868
  90.1 23.3 %collective-permute-start.18 = (bf16[64,2048]{1,0:T(8,128)(2,1)}, bf16[64,2048]{1,0:T(8,128)(2,1)S(1)}, u32[]{:S(2)}, u32[]{:S(2)}) collective-permute-start(bf16[64,2048]{1,0:T(8,128)(2,1)} %merge.5.refs_0_), channel_id=1, source_target_pairs={{0,2},{1,3},{2,0},{3,1},{4,6},{5,7},{6,4},{7,5},{8,10},{9,11},{10,... | collective-permute-start | bytes 786440 | tf_op jit(solution)/shard_map/ppermute | solution.py:471
  95.5 15.0 %copy-start.2 = (bf16[64,2048]{1,0:T(8,128)(2,1)S(1)}, bf16[64,2048]{1,0:T(8,128)(2,1)}, u32[]{:S(2)}) copy-start(bf16[64,2048]{1,0:T(8,128)(2,1)} %merge.5.refs_0_) | copy-start | bytes 786436
  110.5 4.2 %copy-start.12 = (bf16[64,2048]{1,0:T(8,128)(2,1)}, bf16[64,2048]{1,0:T(8,128)(2,1)S(1)}, u32[]{:S(2)}) copy-start(bf16[64,2048]{1,0:T(8,128)(2,1)S(1)} %collective-permute-done.3.refs_2_) | copy-start | bytes 786436
  110.5 19.9 %collective-permute-start.20 = (bf16[64,2048]{1,0:T(8,128)(2,1)S(1)}, bf16[64,2048]{1,0:T(8,128)(2,1)S(1)}, u32[]{:S(2)}, u32[]{:S(2)}) collective-permute-start(bf16[64,2048]{1,0:T(8,128)(2,1)S(1)} %copy-done.2), channel_id=1, source_target_pairs={{0,1},{1,0},{2,3},{3,2},{4,5},{5,4},{6,7},{7,6},{8,9},{9,8},{10,11... | collective-permute-start | bytes 786440 | tf_op jit(solution)/shard_map/ppermute | solution.py:471
  111.3 3.4 %copy-start.15 = (bf16[64,2048]{1,0:T(8,128)(2,1)}, bf16[64,2048]{1,0:T(8,128)(2,1)S(1)}, u32[]{:S(2)}) copy-start(bf16[64,2048]{1,0:T(8,128)(2,1)S(1)} %collective-permute-done.2.refs_1_) | copy-start | bytes 786436
  111.4 39.9 %collective-permute-start.15 = (bf16[128,1536]{1,0:T(8,128)(2,1)}, bf16[128,1536]{1,0:T(8,128)(2,1)S(1)}, u32[]{:S(2)}, u32[]{:S(2)}) collective-permute-start(bf16[128,1536]{1,0:T(8,128)(2,1)} %project.5.refs_4_), channel_id=1, source_target_pairs={{0,8},{4,12},{8,0},{12,4},{1,9},{5,13},{9,1},{13,5},{2,10},{6,14},... | collective-permute-start | bytes 1179656 | tf_op jit(solution)/shard_map/ppermute | solution.py:429
  113.4 16.5 %copy-start.14 = (bf16[64,2048]{1,0:T(8,128)(2,1)}, bf16[64,2048]{1,0:T(8,128)(2,1)S(1)}, u32[]{:S(2)}) copy-start(bf16[64,2048]{1,0:T(8,128)(2,1)S(1)} %collective-permute-done.18.refs_3_) | copy-start | bytes 786436
  113.4 29.5 %collective-permute-start.19 = (bf16[64,2048]{1,0:T(8,128)(2,1)S(1)}, bf16[64,2048]{1,0:T(8,128)(2,1)S(1)}, u32[]{:S(2)}, u32[]{:S(2)}) collective-permute-start(bf16[64,2048]{1,0:T(8,128)(2,1)S(1)} %collective-permute-done.18.refs_3_), channel_id=1, source_target_pairs={{2,3},{1,0},{6,7},{5,4},{10,11},{9,8},{14,15},{13,12},{18,19},{17,... | collective-permute-start | bytes 786440 | tf_op jit(solution)/shard_map/ppermute | solution.py:471
  114.7 0.7 copy-start.16
  129.9 21.7 %collective-permute-start.7 = (bf16[64,1536]{1,0:T(8,128)(2,1)}, bf16[64,1536]{1,0:T(8,128)(2,1)S(1)}, u32[]{:S(2)}, u32[]{:S(2)}) collective-permute-start(bf16[64,1536]{1,0:T(8,128)(2,1)} %project.4.refs_0_), channel_id=1, source_target_pairs={{0,8},{4,12},{8,0},{12,4},{1,9},{5,13},{9,1},{13,5},{2,10},{6,14},... | collective-permute-start | bytes 589832 | tf_op jit(solution)/shard_map/ppermute | solution.py:429
  130.5 0.7 copy-start.13
  130.5 21.2 %collective-permute-start.6 = (bf16[64,1536]{1,0:T(8,128)(2,1)}, bf16[64,1536]{1,0:T(8,128)(2,1)S(1)}, u32[]{:S(2)}, u32[]{:S(2)}) collective-permute-start(bf16[64,1536]{1,0:T(8,128)(2,1)} %project.4.refs_0_), channel_id=1, source_target_pairs={{0,4},{4,0},{8,12},{12,8},{1,5},{5,1},{9,13},{13,9},{2,6},{6,2},{1... | collective-permute-start | bytes 589832 | tf_op jit(solution)/shard_map/ppermute | solution.py:433
  130.5 0.8 copy-start.17
  143.0 0.7 copy-start.18
  143.7 7.4 %copy-start.1 = (bf16[128,1536]{1,0:T(8,128)(2,1)S(1)}, bf16[128,1536]{1,0:T(8,128)(2,1)}, u32[]{:S(2)}) copy-start(bf16[128,1536]{1,0:T(8,128)(2,1)} %project.5.refs_4_) | copy-start | bytes 1179652
  149.6 7.5 %collective-permute-start.23 = (bf16[64,1536]{1,0:T(8,128)(2,1)}, bf16[64,1536]{1,0:T(8,128)(2,1)S(1)}, u32[]{:S(2)}, u32[]{:S(2)}) collective-permute-start(bf16[64,1536]{1,0:T(8,128)(2,1)} %project.7.refs_8_), channel_id=1, source_target_pairs={{0,8},{4,12},{8,0},{12,4},{1,9},{5,13},{9,1},{13,5},{2,10},{6,14},... | collective-permute-start | bytes 589832 | tf_op jit(solution)/shard_map/ppermute | solution.py:429
  151.0 7.4 %collective-permute-start.14 = (bf16[128,1536]{1,0:T(8,128)(2,1)S(1)}, bf16[128,1536]{1,0:T(8,128)(2,1)S(1)}, u32[]{:S(2)}, u32[]{:S(2)}) collective-permute-start(bf16[128,1536]{1,0:T(8,128)(2,1)S(1)} %copy-done.1), channel_id=1, source_target_pairs={{0,4},{4,0},{8,12},{12,8},{1,5},{5,1},{9,13},{13,9},{2,6},{6,2},{1... | collective-permute-start | bytes 1179656 | tf_op jit(solution)/shard_map/ppermute | solution.py:433
  151.2 7.3 %copy-start.8 = (bf16[128,1536]{1,0:T(8,128)(2,1)}, bf16[128,1536]{1,0:T(8,128)(2,1)S(1)}, u32[]{:S(2)}) copy-start(bf16[128,1536]{1,0:T(8,128)(2,1)S(1)} %collective-permute-done.15.refs_6_) | copy-start | bytes 1179652
  151.2 7.3 %collective-permute-start.16 = (bf16[128,1536]{1,0:T(8,128)(2,1)S(1)}, bf16[128,1536]{1,0:T(8,128)(2,1)S(1)}, u32[]{:S(2)}, u32[]{:S(2)}) collective-permute-start(bf16[128,1536]{1,0:T(8,128)(2,1)S(1)} %collective-permute-done.15.refs_6_), channel_id=1, source_target_pairs={{0,4},{4,0},{8,12},{12,8},{1,5},{5,1},{9,13},{13,9},{2,6},{6,2},{1... | collective-permute-start | bytes 1179656 | tf_op jit(solution)/shard_map/ppermute | solution.py:433
  151.6 6.9 %copy-start.21 = (bf16[64,1536]{1,0:T(8,128)(2,1)}, bf16[64,1536]{1,0:T(8,128)(2,1)S(1)}, u32[]{:S(2)}) copy-start(bf16[64,1536]{1,0:T(8,128)(2,1)S(1)} %collective-permute-done.7.refs_2_) | copy-start | bytes 589828
  151.6 5.5 %collective-permute-start.8 = (bf16[64,1536]{1,0:T(8,128)(2,1)S(1)}, bf16[64,1536]{1,0:T(8,128)(2,1)S(1)}, u32[]{:S(2)}, u32[]{:S(2)}) collective-permute-start(bf16[64,1536]{1,0:T(8,128)(2,1)S(1)} %collective-permute-done.7.refs_2_), channel_id=1, source_target_pairs={{0,4},{4,0},{8,12},{12,8},{1,5},{5,1},{9,13},{13,9},{2,6},{6,2},{1... | collective-permute-start | bytes 589832 | tf_op jit(solution)/shard_map/ppermute | solution.py:433
  151.7 6.8 %copy-start.22 = (bf16[64,1536]{1,0:T(8,128)(2,1)}, bf16[64,1536]{1,0:T(8,128)(2,1)S(1)}, u32[]{:S(2)}) copy-start(bf16[64,1536]{1,0:T(8,128)(2,1)S(1)} %collective-permute-done.6.refs_1_) | copy-start | bytes 589828
  151.7 5.3 %collective-permute-start.22 = (bf16[64,1536]{1,0:T(8,128)(2,1)}, bf16[64,1536]{1,0:T(8,128)(2,1)S(1)}, u32[]{:S(2)}, u32[]{:S(2)}) collective-permute-start(bf16[64,1536]{1,0:T(8,128)(2,1)} %project.7.refs_8_), channel_id=1, source_target_pairs={{0,4},{4,0},{8,12},{12,8},{1,5},{5,1},{9,13},{13,9},{2,6},{6,2},{1... | collective-permute-start | bytes 589832 | tf_op jit(solution)/shard_map/ppermute | solution.py:433
  157.0 1.5 copy-start.23
  157.0 1.4 collective-permute-start.24
  157.0 1.5 copy-start.24
  157.1 1.5 copy-start.25
  158.5 0.7 copy-start.26
  158.5 0.8 copy-start.9
  159.3 0.7 copy-start.10

commit v4 on v3

--- a/solution.py
+++ b/solution.py
@@ -12,9 +12,10 @@
 HEAD_SIZE = 128
 SPAN = 128
 ALIGN = 16
-SHARES = (4, 8, 4)
+SHARES = (4, 4, 8)
+GROUPS = ((0, 1), (2,))
 DEPTH = 1024
-VMEM_LIMIT = 56 * 1024 * 1024
+MEBI = 1024 * 1024
 F32, BF16 = jnp.float32, jnp.bfloat16
 
 
@@ -32,13 +33,15 @@
     return lax.broadcasted_iota(jnp.int32, shape, dimension)
 
 
-def deal_kernel(chips, bases, sizes, lengths_ref, own_ref, twin_ref, *out_refs):
+def deal_kernel(chips, bases, sizes, twins, lengths_ref, *refs):
     me = lax.axis_index("req")
     chip, core = lax.div(me, 2), lax.rem(me, 2)
-    runs = [
-        run_of(lengths_ref, request, 2 * chips) for request in (me, me + 1 - 2 * core)
-    ]
-    slots = own_ref.shape[0]
+    sources, refs = refs[: len(twins)], refs[len(twins) :]
+    count = 2 * len(sizes)
+    priors, out_refs = refs[:-count], refs[-count:]
+    requests = [me + 1 - 2 * core if twin else me for twin in twins]
+    runs = [run_of(lengths_ref, request, 2 * chips) for request in requests]
+    slots = sources[0].shape[0]
     for chunk, (base, rows) in enumerate(zip(bases, sizes)):
         home_ref, away_ref = out_refs[2 * chunk : 2 * chunk + 2]
         for hop in range(chips):
@@ -46,19 +49,22 @@
             number = base + target * rows + iota((rows, slots), 0)
             slot = iota((rows, slots), 1)
             total = None
-            for (start, length), source in zip(runs, (own_ref, twin_ref)):
+            for (start, length), source in zip(runs, sources):
                 hot = ((number - start == slot) & (slot < length)).astype(BF16)
                 part = jnp.dot(hot, source[...], preferred_element_type=F32)
                 total = part if total is None else total + part
+            total = total.astype(BF16)
             if hop == 0:
-                home_ref[...] = total.astype(BF16)
+                home_ref[...] = total + priors[2 * chunk][...] if priors else total
+            elif priors:
+                away_ref[hop - 1] = total + priors[2 * chunk + 1][hop - 1]
             else:
-                away_ref[hop - 1] = total.astype(BF16)
-
-
-def deal(chips, bases, sizes, lengths, own, twin):
-    slots, width = own.shape
-    block = min(512, width)
+                away_ref[hop - 1] = total
+
+
+def deal(chips, bases, sizes, lengths, sources, twins, priors=()):
+    slots, width = sources[0].shape
+    block = min(1024, width)
     out_specs, out_shape = [], []
     for rows in sizes:
         out_specs += [
@@ -70,57 +76,47 @@
             jax.ShapeDtypeStruct((chips - 1, rows, width), BF16),
         ]
     return pl.pallas_call(
-        functools.partial(deal_kernel, chips, bases, sizes),
+        functools.partial(deal_kernel, chips, bases, sizes, twins),
         grid=(width // block,),
-        in_specs=[
-            pl.BlockSpec(memory_space=pltpu.SMEM),
-            pl.BlockSpec((slots, block), lambda i: (0, i)),
-            pl.BlockSpec((slots, block), lambda i: (0, i)),
-        ],
+        in_specs=[pl.BlockSpec(memory_space=pltpu.SMEM)]
+        + [pl.BlockSpec((slots, block), lambda i: (0, i)) for _ in sources]
+        + (out_specs if priors else []),
         out_specs=out_specs,
         out_shape=out_shape,
-        compiler_params=pltpu.CompilerParams(vmem_limit_bytes=VMEM_LIMIT),
+        compiler_params=pltpu.CompilerParams(vmem_limit_bytes=24 * MEBI),
         cost_estimate=pl.CostEstimate(
-            flops=4 * chips * sum(sizes) * slots * width,
-            bytes_accessed=4 * slots * width + 2 * chips * sum(sizes) * width,
+            flops=2 * len(sources) * chips * sum(sizes) * slots * width,
+            bytes_accessed=2 * len(sources) * slots * width + 2 * chips * sum(sizes) * width,
             transcendentals=0,
         ),
         name="deal",
-    )(lengths, own, twin)
+    )(lengths, *sources, *priors)
 
 
 def merge_kernel(count, home_ref, *refs):
     total = home_ref[...]
     for ref in refs[:count]:
         total = total + ref[...]
-    refs[-1 if len(refs) == count + 1 else -2][...] = total
+    passed = (len(refs) - count - 1) // 2
+    refs[count + passed][...] = total
 
 
 def merge(home, arrived, later):
     count = len(arrived)
     vmem, anywhere = pl.BlockSpec(memory_space=pltpu.VMEM), pl.BlockSpec(memory_space=pl.ANY)
-    operands, in_specs = [home, *arrived], [vmem] * (count + 1)
-    out_shape, out_specs = [jax.ShapeDtypeStruct(home.shape, home.dtype)], [vmem]
-    aliases = {}
-    if later is not None:
-        operands.append(later)
-        in_specs.append(anywhere)
-        out_shape.append(jax.ShapeDtypeStruct(later.shape, later.dtype))
-        out_specs.append(anywhere)
-        aliases = {count + 1: 1}
-    results = pl.pallas_call(
+    block, *later = pl.pallas_call(
         functools.partial(merge_kernel, count),
-        in_specs=in_specs,
-        out_specs=out_specs,
-        out_shape=out_shape,
-        input_output_aliases=aliases,
-        compiler_params=pltpu.CompilerParams(vmem_limit_bytes=VMEM_LIMIT),
+        in_specs=[vmem] * (count + 1) + [anywhere] * len(later),
+        out_specs=[vmem] + [anywhere] * len(later),
+        out_shape=[jax.ShapeDtypeStruct(leaf.shape, leaf.dtype) for leaf in (home, *later)],
+        input_output_aliases={count + 1 + at: 1 + at for at in range(len(later))},
+        compiler_params=pltpu.CompilerParams(vmem_limit_bytes=8 * MEBI),
         cost_estimate=pl.CostEstimate(
             flops=home.size, bytes_accessed=2 * home.size * (count + 2), transcendentals=0
         ),
         name="merge",
-    )(*operands)
-    return results if later is not None else (results[0], None)
+    )(home, *arrived, *later)
+    return block, later
 
 
 def routes_of(shards):
@@ -163,9 +159,9 @@
 
 
 def project_kernel(
-    count, carries, final, shards, steps, base, members, place_ref, lengths_ref, *refs
+    count, carries, final, shards, steps, bases, sizes, members, place_ref, lengths_ref, *refs
 ):
-    pieces, refs = refs[:count], refs[count:]
+    pieces, refs = refs[: count * len(sizes)], refs[count * len(sizes) :]
     gain_ref, query_ref, key_ref, value_ref = refs[:4]
     refs = refs[4:]
     if carries:
@@ -190,7 +186,10 @@
         @pl.when(piece == index)
         def _():
             columns = pl.ds(pl.multiple_of(step * depth, depth), depth)
-            chosen[...] = pieces[index][:, columns]
+            at = 0
+            for chunk, size in enumerate(sizes):
+                chosen[at : at + size, :] = pieces[chunk * count + index][:, columns]
+                at += size
 
     @pl.when(piece >= 0)
     def _():
@@ -212,7 +211,13 @@
         @pl.when((visit == visits - 1) & (step == steps - 1))
         def _():
             me = lax.axis_index("req")
-            number = base + me * rows + iota((rows, HEAD_SIZE), 0)
+            number = jnp.concatenate(
+                [
+                    base + me * size + iota((size, HEAD_SIZE), 0)
+                    for base, size in zip(bases, sizes)
+                ],
+                axis=0,
+            )
             start = jnp.zeros((rows, HEAD_SIZE), jnp.int32)
             before = jnp.int32(0)
             for other in range(members):
@@ -232,8 +237,11 @@
                 out_ref[:, columns] = head.astype(BF16)
 
 
-def project(final, shards, base, place, visits, lengths, pieces, gain, weights, carried, frequency):
-    rows, width = pieces[0].shape
+def project(
+    final, shards, bases, sizes, place, visits, lengths, lines, gain, weights, carried, frequency
+):
+    pieces = [piece for line in lines for piece in line]
+    rows, width = sum(sizes), pieces[0].shape[1]
     depth = min(DEPTH, width)
     steps = width // depth
     columns = sum(weight.shape[1] for weight in weights)
@@ -253,7 +261,7 @@
         return pl.BlockSpec(block, where)
 
     operands = [*pieces, gain, *weights, *carried, frequency]
-    in_specs = [whole((rows, width)) for _ in pieces]
+    in_specs = [whole(piece.shape) for piece in pieces]
     in_specs += [deep((1, depth), 1)]
     in_specs += [deep((depth, weight.shape[1]), 0) for weight in weights]
     in_specs += [whole(leaf.shape) for leaf in carried]
@@ -270,12 +278,13 @@
     return pl.pallas_call(
         functools.partial(
             project_kernel,
-            len(pieces),
+            len(lines[0]),
             bool(carried),
             final,
             shards,
             steps,
-            base,
+            bases,
+            sizes,
             lengths.shape[0],
         ),
         grid_spec=pltpu.PrefetchScalarGridSpec(
@@ -286,7 +295,7 @@
             scratch_shapes=scratch,
         ),
         out_shape=out_shape,
-        compiler_params=pltpu.CompilerParams(vmem_limit_bytes=VMEM_LIMIT),
+        compiler_params=pltpu.CompilerParams(vmem_limit_bytes=32 * MEBI),
         cost_estimate=pl.CostEstimate(
             flops=2 * rows * width * columns * visits,
             bytes_accessed=2 * width * columns * visits + 8 * rows * columns,
@@ -296,27 +305,32 @@
     )(place, lengths, *operands)
 
 
-def attend_kernel(chips, bases, sizes, query_width, key_width, lengths_ref, plan_ref, *refs):
+def attend_kernel(chips, groups, query_width, key_width, lengths_ref, plan_ref, *refs):
     blocks, (attended_ref, cache_ref, rows_ref, sems) = refs[:-4], refs[-4:]
     workers = 2 * chips
     me = lax.axis_index("req")
     chip, core = lax.div(me, 2), lax.rem(me, 2)
     slots = cache_ref.shape[1]
     spans = slots // SPAN
-    total = workers * sum(sizes)
+    total = workers * sum(sum(sizes) for _, sizes in groups)
     copies = []
-    for chunk, (base, rows) in enumerate(zip(bases, sizes)):
+    for group, (bases, sizes) in enumerate(groups):
         for hop in range(chips):
             source = lax.rem(chip - hop + chips, chips) * 2
             for twin in range(2):
                 owner = source + (core if twin == 0 else 1 - core)
-                index = (chunk * chips + hop) * 2 + twin
-                at = pl.multiple_of(base + owner * rows, ALIGN)
-                copies.append(
-                    pltpu.make_async_copy(
-                        blocks[index], rows_ref.at[pl.ds(at, rows), :], sems.at[index]
+                block = blocks[(group * chips + hop) * 2 + twin]
+                first = 0
+                for base, rows in zip(bases, sizes):
+                    at = pl.multiple_of(base + owner * rows, ALIGN)
+                    copies.append(
+                        pltpu.make_async_copy(
+                            block.at[pl.ds(first, rows), :],
+                            rows_ref.at[pl.ds(at, rows), :],
+                            sems.at[len(copies)],
+                        )
                     )
-                )
+                    first += rows
     for copy in copies:
         copy.start()
     pad = rows_ref.shape[0] - total
@@ -403,11 +417,12 @@
                         ).astype(BF16)
 
 
-def attend(chips, bases, sizes, query_width, key_width, slots, lengths, plan, blocks):
+def attend(chips, groups, query_width, key_width, slots, lengths, plan, blocks):
     width = query_width + 2 * key_width
-    total = 2 * chips * sum(sizes)
+    total = 2 * chips * sum(sum(sizes) for _, sizes in groups)
+    copies = 2 * chips * sum(len(sizes) for _, sizes in groups)
     return pl.pallas_call(
-        functools.partial(attend_kernel, chips, bases, sizes, query_width, key_width),
+        functools.partial(attend_kernel, chips, groups, query_width, key_width),
         in_specs=[pl.BlockSpec(memory_space=pltpu.SMEM)] * 2
         + [pl.BlockSpec(memory_space=pl.ANY)] * len(blocks),
         out_specs=[pl.BlockSpec(memory_space=pltpu.VMEM)] * 2,
@@ -417,9 +432,9 @@
         ],
         scratch_shapes=[
             pltpu.VMEM((total + slots + SPAN, width), BF16),
-            pltpu.SemaphoreType.DMA((len(blocks),)),
+            pltpu.SemaphoreType.DMA((copies,)),
         ],
-        compiler_params=pltpu.CompilerParams(vmem_limit_bytes=VMEM_LIMIT),
+        compiler_params=pltpu.CompilerParams(vmem_limit_bytes=32 * MEBI),
         name="attend",
     )(lengths, plan, *blocks)
 
@@ -449,75 +464,74 @@
     frequency = jnp.asarray(np.tile(frequency, 2)[None, :], F32)
 
     twin = swap_cores(tokens, chips)
+    first = deal(chips, bases[:1], sizes[:1], lengths, [tokens], [False])
     dealt = [
-        *deal(chips, bases[:1], sizes[:1], lengths, tokens, twin),
-        *deal(chips, bases[1:], sizes[1:], lengths, tokens, twin),
+        *deal(chips, bases[:1], sizes[:1], lengths, [twin], [True], first),
+        *deal(chips, bases[1:], sizes[1:], lengths, [tokens, twin], [False, True]),
     ]
     homes, aways = dealt[::2], dealt[1::2]
-    held = []
+    routes, owned, depth = routes_of(shards)
+    early = [piece for piece in range(len(owned)) if depth[piece] < max(depth)]
+    late = [piece for piece in range(len(owned)) if depth[piece] == max(depth)]
+    direct = [piece for piece in range(len(owned)) if depth[piece] == 1]
+    relayed = {source + 1 for source, _ in routes} - {0}
+
+    lines = []
     for chunk in range(len(sizes)):
         arrived = [shift_chips(aways[chunk][hop - 1], hop, chips) for hop in range(1, chips)]
-        later = aways[chunk + 1] if chunk + 1 < len(sizes) else None
+        places = [(chunk - 1, piece) for piece in direct if piece not in relayed]
+        places += [(chunk - 2, piece) for piece in direct if piece in relayed]
+        places = [(at, piece) for at, piece in places if at >= 0]
+        later = aways[chunk + 1 : chunk + 2] + [lines[at][piece] for at, piece in places]
         block, later = merge(homes[chunk], arrived, later)
-        if later is not None:
-            aways[chunk + 1] = later
-        held.append(block)
-
-    routes, owned, depth = routes_of(shards)
-    lines = []
-    for block in held:
-        line = [block]
-        for source, pairs in routes:
-            line.append(lax.ppermute(line[source + 1], "tp", pairs))
+        if chunk + 1 < len(sizes):
+            aways[chunk + 1] = later.pop(0)
+        for (at, piece), leaf in zip(places, later):
+            lines[at][piece] = leaf
+        line = {0: block}
+        for index, (source, pairs) in enumerate(routes):
+            if index + 1 in direct:
+                line[index + 1] = lax.ppermute(block, "tp", pairs)
         lines.append(line)
-
-    early = [piece for piece in range(len(owned)) if depth[piece] < max(depth)]
-    late = [piece for piece in range(len(owned)) if depth[piece] == max(depth)]
+    for line in lines:
+        for index, (source, pairs) in enumerate(routes):
+            if index + 1 not in direct:
+                line[index + 1] = lax.ppermute(line[source + 1], "tp", pairs)
+
     tables, counts = zip(
-        *(
-            visits_of([owned[piece] for piece in group], shards)
-            for group in (range(len(owned)), early, late)
-        )
+        *(visits_of([owned[piece] for piece in group], shards) for group in (early, late))
     )
     table = jnp.asarray(np.concatenate(tables, axis=1))
     table = lax.dynamic_index_in_dim(table, lax.axis_index("tp"), 0, keepdims=False)
-    places = [
-        table[2 * sum(counts[:at]) : 2 * sum(counts[: at + 1])] for at in range(3)
-    ]
-
-    blocks = []
-    for chunk, (base, line) in enumerate(zip(bases, lines)):
-        common = (gain, weights)
-        if chunk + 1 < len(sizes):
-            (block,) = project(
-                True, shards, base, places[0], counts[0], lengths, line, *common, (), frequency
-            )
-        else:
-            pieces = [line[piece] for piece in early]
+    places = table[: 2 * counts[0]], table[2 * counts[0] :]
+
+    blocks, groups = [], []
+    for chunks in GROUPS:
+        span = [bases[chunk] for chunk in chunks], [sizes[chunk] for chunk in chunks]
+        groups.append(span)
+        carried = ()
+        for place, count, chosen in zip(places, counts, (early, late)):
             carried = project(
-                False, shards, base, places[1], counts[1], lengths, pieces, *common, (), frequency
-            )
-            pieces = [line[piece] for piece in late]
-            (block,) = project(
-                True,
+                chosen is late,
                 shards,
-                base,
-                places[2],
-                counts[2],
+                *span,
+                place,
+                count,
                 lengths,
-                pieces,
-                *common,
+                [[lines[chunk][piece] for piece in chosen] for chunk in chunks],
+                gain,
+                weights,
                 carried,
                 frequency,
             )
+        block = carried[0]
         here = [block] + [shift_chips(block, hop, chips) for hop in range(1, chips)]
         for piece in here:
             blocks += [piece, swap_cores(piece, chips)]
     return tuple(
         attend(
             chips,
-            bases,
-            sizes,
+            groups,
             w_query.shape[1],
             key_weight.shape[1],
             slots,

time: 170 us -> 140 us (0.82)
  the two profiles are of different devices: /device:TPU:0 before, /device:TPU:9 now
where the time goes in v4:
time: 140 us; the launch traced here: 139 us
  waiting for transfers between devices  54 us (39%)
  Pallas kernels  43 us (31%)
  starting transfers between devices  33.2 us (24%)
  local copies, waits for them, and re-layouts  7.42 us (5%)
    ppermute x9, waiting for transfers between devices, local(): line[index + 1] = lax.ppermute(block, 'tp', pairs)  46.8 us
    pallas_call x4, Pallas kernels, project(): pl.pallas_call(functools.partial(project_kernel, len(lines[0]), bool(carr...  27.7 us
    ppermute x5, starting transfers between devices, swap_cores(): return lax.ppermute(value, 'req', [(d, d ^ 1) for d in range(2 * chips)])  11.5 us
    ppermute x9, starting transfers between devices, local(): line[index + 1] = lax.ppermute(block, 'tp', pairs)  11.2 us
    pallas_call x1, Pallas kernels, attend(): pl.pallas_call(functools.partial(attend_kernel, chips, groups, query_widt...  8.18 us
    pallas_call x3, Pallas kernels, deal(): pl.pallas_call(functools.partial(deal_kernel, chips, bases, sizes, twins)...  7.04 us
    unnamed x22, local copies, waits for them, and re-layouts  6.65 us
    ppermute x3, starting transfers between devices, local(): line[index + 1] = lax.ppermute(line[source + 1], 'tp', pairs)  6.01 us
  transfers between devices with their start and end apart: 22, of which 10 were waited for; matrix products, arithmetic and copies ran while one was open for 1% of the time, Pallas kernels for 24%

profile of v4, /device:TPU:9, one launch (start us, length us, event | category | flops | bytes accessed | tf_op | source)
XLA Modules:
  0.0 138.8 jit_solution(9063847091278755894)
XLA Ops:
  0.6 0.7 collective-permute-start
  1.4 1.6 %copy-done.4 = bf16[512,2048]{1,0:T(8,128)(2,1)S(1)} copy-done((bf16[512,2048]{1,0:T(8,128)(2,1)S(1)}, bf16[512,2048]{1,0:T(8,128)(2,1)}, u32[]{:S(2)}) %copy-start.4) | copy-done | bytes 2097176
  3.0 0.7 copy-done.6
  3.6 1.6 %deal.4 = (bf16[64,2048]{1,0:T(8,128)(2,1)S(1)}, bf16[1,64,2048]{2,1,0:T(8,128)(2,1)S(1)}) custom-call(s32[4]{0:T(128)S(1)} %copy-done.6, bf16[512,2048]{1,0:T(8,128)(2,1)S(1)} %copy-done.4), custom_call_target="tpu_custom_call" | custom-call | flops 268435456 | bytes 2621440 | tf_op jit(solution)/shard_map/deal/pallas_call | solution.py:78
  5.3 0.1 collective-permute-done.refs_1_.refs_0_
  5.4 1.7 %deal.5 = (bf16[64,2048]{1,0:T(8,128)(2,1)S(1)}, bf16[1,64,2048]{2,1,0:T(8,128)(2,1)S(1)}) custom-call(s32[4]{0:T(128)S(1)} %copy-done.6, bf16[512,2048]{1,0:T(8,128)(2,1)S(1)} %collective-permute-done.refs_1_.refs_0_, bf16[64,2048]{1,0:T(8,128)(2,1)S(1)} %get-tuple-element.26.refs_1_, bf16[1,64,2048]{2,1,0:T(8,128)(2,1)S(1)} %get-tuple-element.27.refs_2_), custom_call_target="tpu_custom_call" | custom-call | flops 268435456 | bytes 2621440 | tf_op jit(solution)/shard_map/deal/pallas_call | solution.py:78
  7.0 0.0 copy-start.10
  7.1 0.0 copy-start.7
  7.1 0.0 copy-start.8
  7.1 1.3 collective-permute-start.1
  8.4 3.7 %deal.3 = (bf16[64,2048]{1,0:T(8,128)(2,1)S(1)}, bf16[1,64,2048]{2,1,0:T(8,128)(2,1)S(1)}, bf16[128,2048]{1,0:T(8,128)(2,1)S(1)}, bf16[1,128,2048]{2,1,0:T(8,128)(2,1)S(1)}) custom-call(s32[4]{0:T(128)S(1)} %copy-done.6, bf16[512,2048]{1,0:T(8,128)(2,1)S(1)} %copy-done.5, bf16[512,2048]{1,0:T(8,128)(2,1)S(1)} %collective-permute-done.refs_1_.refs_0_), custom_call_target="tpu_custom_call" | custom-call | flops 1610612736 | bytes 5767168 | tf_op jit(solution)/shard_map/deal/pallas_call | solution.py:78
  12.1 2.6 %collective-permute-done.1.refs_0_ = bf16[64,2048]{1,0:T(8,128)(2,1)S(1)} collective-permute-done((bf16[64,2048]{1,0:T(8,128)(2,1)S(1)}, bf16[64,2048]{1,0:T(8,128)(2,1)S(1)}, u32[]{:S(2)}, u32[]{:S(2)}) %collective-permute-start.1) | collective-permute-done | bytes 262176 | tf_op jit(solution)/shard_map/ppermute | solution.py:444
  14.7 1.3 collective-permute-start.2
  16.0 3.2 %collective-permute-start.4 = (bf16[64,2048]{1,0:T(8,128)(2,1)S(1)}, bf16[64,2048]{1,0:T(8,128)(2,1)S(1)}, u32[]{:S(2)}, u32[]{:S(2)}) collective-permute-start(bf16[64,2048]{1,0:T(8,128)(2,1)S(1)} %get-tuple-element.33.refs_0_), channel_id=1, source_target_pairs={{1,2},{2,1},{5,6},{6,5},{9,10},{10,9},{13,14},{14,13},{17,18},{18,... | collective-permute-start | bytes 786440 | tf_op jit(solution)/shard_map/ppermute | solution.py:494
  19.2 0.1 collective-permute-start.3
  19.2 2.1 %collective-permute-done.2.refs_0_ = bf16[64,2048]{1,0:T(8,128)(2,1)S(1)} collective-permute-done((bf16[64,2048]{1,0:T(8,128)(2,1)S(1)}, bf16[64,2048]{1,0:T(8,128)(2,1)S(1)}, u32[]{:S(2)}, u32[]{:S(2)}) %collective-permute-start.2) | collective-permute-done | bytes 262176 | tf_op jit(solution)/shard_map/ppermute | solution.py:444
  21.3 2.8 %collective-permute-done.4.refs_3_ = bf16[64,2048]{1,0:T(8,128)(2,1)S(1)} collective-permute-done((bf16[64,2048]{1,0:T(8,128)(2,1)S(1)}, bf16[64,2048]{1,0:T(8,128)(2,1)S(1)}, u32[]{:S(2)}, u32[]{:S(2)}) %collective-permute-start.4) | collective-permute-done | bytes 262176 | tf_op jit(solution)/shard_map/ppermute | solution.py:494
  24.2 1.1 collective-permute-done.3.refs_2_
  25.3 0.3 collective-permute-start.5
  25.6 0.2 collective-permute-start.8
  25.8 3.2 %collective-permute-start.7 = (bf16[64,2048]{1,0:T(8,128)(2,1)S(1)}, bf16[64,2048]{1,0:T(8,128)(2,1)S(1)}, u32[]{:S(2)}, u32[]{:S(2)}) collective-permute-start(bf16[64,2048]{1,0:T(8,128)(2,1)S(1)} %get-tuple-element.35.refs_4_), channel_id=1, source_target_pairs={{1,2},{2,1},{5,6},{6,5},{9,10},{10,9},{13,14},{14,13},{17,18},{18,... | collective-permute-start | bytes 786440 | tf_op jit(solution)/shard_map/ppermute | solution.py:494
  29.0 0.1 collective-permute-start.6
  29.1 7.2 %collective-permute-done.8.refs_3_ = bf16[64,2048]{1,0:T(8,128)(2,1)S(1)} collective-permute-done((bf16[64,2048]{1,0:T(8,128)(2,1)S(1)}, bf16[64,2048]{1,0:T(8,128)(2,1)S(1)}, u32[]{:S(2)}, u32[]{:S(2)}) %collective-permute-start.8) | collective-permute-done | bytes 262176 | tf_op jit(solution)/shard_map/ppermute | solution.py:494
  36.3 7.9 %collective-permute-done.7.refs_2_ = bf16[64,2048]{1,0:T(8,128)(2,1)S(1)} collective-permute-done((bf16[64,2048]{1,0:T(8,128)(2,1)S(1)}, bf16[64,2048]{1,0:T(8,128)(2,1)S(1)}, u32[]{:S(2)}, u32[]{:S(2)}) %collective-permute-start.7) | collective-permute-done | bytes 262176 | tf_op jit(solution)/shard_map/ppermute | solution.py:494
  44.1 0.0 collective-permute-done.6.refs_1_
  44.1 0.0 collective-permute-done.5.refs_0_
  44.1 0.1 merge.5
  44.2 0.1 collective-permute-start.15
  44.3 0.7 constant_dynamic-slice_fusion
  45.0 2.3 %collective-permute-start.10 = (bf16[64,2048]{1,0:T(8,128)(2,1)S(1)}, bf16[64,2048]{1,0:T(8,128)(2,1)S(1)}, u32[]{:S(2)}, u32[]{:S(2)}) collective-permute-start(bf16[64,2048]{1,0:T(8,128)(2,1)S(1)} %get-tuple-element.35.refs_4_), channel_id=1, source_target_pairs={{0,2},{1,3},{2,0},{3,1},{4,6},{5,7},{6,4},{7,5},{8,10},{9,11},{10,... | collective-permute-start | bytes 786440 | tf_op jit(solution)/shard_map/ppermute | solution.py:494
  47.3 2.0 %collective-permute-start.18 = (bf16[128,2048]{1,0:T(8,128)(2,1)S(1)}, bf16[128,2048]{1,0:T(8,128)(2,1)S(1)}, u32[]{:S(2)}, u32[]{:S(2)}) collective-permute-start(bf16[128,2048]{1,0:T(8,128)(2,1)S(1)} %get-tuple-element.43.refs_0_), channel_id=1, source_target_pairs={{1,2},{2,1},{5,6},{6,5},{9,10},{10,9},{13,14},{14,13},{17,18},{18,... | collective-permute-start | bytes 1572872 | tf_op jit(solution)/shard_map/ppermute | solution.py:494
  49.4 0.1 collective-permute-start.17
  49.4 0.1 slice_bitcast_fusion.1.place_ref
  49.5 27.8 %collective-permute-done.10.refs_7_ = bf16[64,2048]{1,0:T(8,128)(2,1)S(1)} collective-permute-done((bf16[64,2048]{1,0:T(8,128)(2,1)S(1)}, bf16[64,2048]{1,0:T(8,128)(2,1)S(1)}, u32[]{:S(2)}, u32[]{:S(2)}) %collective-permute-start.10) | collective-permute-done | bytes 262176 | tf_op jit(solution)/shard_map/ppermute | solution.py:494
  77.3 3.4 %collective-permute-start.11 = (bf16[64,2048]{1,0:T(8,128)(2,1)S(1)}, bf16[64,2048]{1,0:T(8,128)(2,1)S(1)}, u32[]{:S(2)}, u32[]{:S(2)}) collective-permute-start(bf16[64,2048]{1,0:T(8,128)(2,1)S(1)} %collective-permute-done.10.refs_7_), channel_id=1, source_target_pairs={{2,3},{1,0},{6,7},{5,4},{10,11},{9,8},{14,15},{13,12},{18,19},{17,... | collective-permute-start | bytes 786440 | tf_op jit(solution)/shard_map/ppermute | solution.py:499
  80.7 1.3 collective-permute-start.9
  82.0 0.0 collective-permute-done.15.refs_3_
  82.0 1.3 collective-permute-start.16
  83.4 0.0 copy-start
  83.4 2.2 %copy-done = bf16[8192,256]{1,0:T(8,128)(2,1)S(1)} copy-done((bf16[8192,256]{1,0:T(8,128)(2,1)S(1)}, bf16[8192,256]{1,0:T(8,128)(2,1)}, u32[]{:S(2)}) %copy-start) | copy-done | bytes 4194328
  85.6 2.2 %copy-done.2 = bf16[8192,256]{1,0:T(8,128)(2,1)S(1)} copy-done((bf16[8192,256]{1,0:T(8,128)(2,1)S(1)}, bf16[8192,256]{1,0:T(8,128)(2,1)}, u32[]{:S(2)}) %copy-start.2) | copy-done | bytes 4194328
  87.8 11.5 %project.4 = (f32[128,1536]{1,0:T(8,128)S(1)}, f32[128,128]{1,0:T(8,128)S(1)}) custom-call(s32[8]{0:T(128)S(1)} %slice_bitcast_fusion.place_ref, s32[4]{0:T(128)S(1)} %copy-done.7, bf16[64,2048]{1,0:T(8,128)(2,1)S(1)} %get-tuple-element.33.refs_0_, bf16[64,2048]{1,0:T(8,128)(2,1)S(1)} %get-tuple-element.37.refs_1_, ...), custom_call_target="tpu_custom_call" | custom-call | flops 3221225472 | bytes 26738688 | tf_op jit(solution)/shard_map/project/pallas_call | solution.py:278
  99.2 0.0 collective-permute-done.11.refs_1_
  99.2 0.0 collective-permute-done.9.refs_0_
  99.3 2.7 %project.5.refs_0_ = bf16[128,1536]{1,0:T(8,128)(2,1)S(1)} custom-call(s32[2]{0:T(128)S(1)} %slice_bitcast_fusion.1.place_ref, s32[4]{0:T(128)S(1)} %copy-done.7, bf16[64,2048]{1,0:T(8,128)(2,1)S(1)} %collective-permute-done.9.refs_0_, bf16[64,2048]{1,0:T(8,128)(2,1)S(1)} %collective-permute-done.11.refs_1_, f32[1,8192]{1,0:T(1,128)S(1)} %bitcast.9, ...), custom_call_target="tpu_custom_call" | custom-call | flops 805306368 | bytes 7864320 | tf_op jit(solution)/shard_map/project/pallas_call | solution.py:278
  102.0 1.3 collective-permute-start.13
  103.3 0.0 collective-permute-done.18.refs_2_
  103.3 0.0 collective-permute-done.17.refs_1_
  103.3 10.7 %project.6 = (f32[128,1536]{1,0:T(8,128)S(1)}, f32[128,128]{1,0:T(8,128)S(1)}) custom-call(s32[8]{0:T(128)S(1)} %slice_bitcast_fusion.place_ref, s32[4]{0:T(128)S(1)} %copy-done.7, bf16[128,2048]{1,0:T(8,128)(2,1)S(1)} %get-tuple-element.43.refs_0_, bf16[128,2048]{1,0:T(8,128)(2,1)S(1)} %collective-permute-done.17.refs_1_, ...), custom_call_target="tpu_custom_call" | custom-call | flops 3221225472 | bytes 26738688 | tf_op jit(solution)/shard_map/project/pallas_call | solution.py:278
  114.0 0.0 collective-permute-done.16.refs_0_
  114.1 0.0 copy-start.9
  114.1 2.7 %project.7.refs_4_ = bf16[128,1536]{1,0:T(8,128)(2,1)S(1)} custom-call(s32[2]{0:T(128)S(1)} %slice_bitcast_fusion.1.place_ref, s32[4]{0:T(128)S(1)} %copy-done.7, bf16[128,2048]{1,0:T(8,128)(2,1)S(1)} %collective-permute-done.16.refs_0_, f32[1,8192]{1,0:T(1,128)S(1)} %bitcast.11, bf16[8192,1024]{1,0:T(8,128)(2,1)} %refs_2_.1, ...), custom_call_target="tpu_custom_call" | custom-call | flops 805306368 | bytes 7864320 | tf_op jit(solution)/shard_map/project/pallas_call | solution.py:278
  116.8 0.3 collective-permute-start.20
  117.1 4.7 %collective-permute-start.12 = (bf16[128,1536]{1,0:T(8,128)(2,1)S(1)}, bf16[128,1536]{1,0:T(8,128)(2,1)S(1)}, u32[]{:S(2)}, u32[]{:S(2)}) collective-permute-start(bf16[128,1536]{1,0:T(8,128)(2,1)S(1)} %project.5.refs_0_), channel_id=1, source_target_pairs={{0,4},{4,0},{8,12},{12,8},{1,5},{5,1},{9,13},{13,9},{2,6},{6,2},{1... | collective-permute-start | bytes 1179656 | tf_op jit(solution)/shard_map/ppermute | solution.py:448
  121.8 0.0 collective-permute-done.13.refs_2_
  121.8 0.0 collective-permute-start.14
  121.8 0.5 collective-permute-start.19
  122.3 1.2 collective-permute-done.20.refs_6_
  123.5 5.6 %collective-permute-start.21 = (bf16[128,1536]{1,0:T(8,128)(2,1)S(1)}, bf16[128,1536]{1,0:T(8,128)(2,1)S(1)}, u32[]{:S(2)}, u32[]{:S(2)}) collective-permute-start(bf16[128,1536]{1,0:T(8,128)(2,1)S(1)} %collective-permute-done.20.refs_6_), channel_id=1, source_target_pairs={{0,4},{4,0},{8,12},{12,8},{1,5},{5,1},{9,13},{13,9},{2,6},{6,2},{1... | collective-permute-start | bytes 1179656 | tf_op jit(solution)/shard_map/ppermute | solution.py:448
  129.1 0.0 collective-permute-done.12.refs_1_
  129.1 0.0 collective-permute-done.14.refs_3_
  129.1 0.0 collective-permute-done.19.refs_5_
  129.1 1.3 collective-permute-done.21.refs_7_
  130.4 8.2 %attend.1 = (bf16[512,1024]{1,0:T(8,128)(2,1)}, bf16[2,512,256]{2,1,0:T(8,128)(2,1)}) custom-call(s32[4]{0:T(128)S(1)} %copy-done.7, s32[16]{0:T(128)S(1)} %copy-done.9, bf16[128,1536]{1,0:T(8,128)(2,1)S(1)} %project.5.refs_0_, bf16[128,1536]{1,0:T(8,128)(2,1)S(1)} %collective-permute-done.12.refs_1_, bf16[128,1536]{1,0:T(8,128)(2,1)S(1)} %collective-permute-done.13.refs_2_, ...), custom_call_target="tpu_custom_call" | custom-call | tf_op jit(solution)/shard_map/attend/pallas_call | solution.py:424
  (17 shorter events, 0.1 us)
Async XLA Ops:
  0.6 4.7 %collective-permute-start = (bf16[512,2048]{1,0:T(8,128)(2,1)}, bf16[512,2048]{1,0:T(8,128)(2,1)S(1)}, u32[]{:S(2)}, u32[]{:S(2)}) collective-permute-start(bf16[512,2048]{1,0:T(8,128)(2,1)} %refs_0_.3), channel_id=1, source_target_pairs={{0,4},{4,0},{8,12},{12,8},{1,5},{5,1},{9,13},{13,9},{2,6},{6,2},{1... | collective-permute-start | bytes 6291464 | tf_op jit(solution)/shard_map/ppermute | solution.py:448
  1.4 1.6 %copy-start.4 = (bf16[512,2048]{1,0:T(8,128)(2,1)S(1)}, bf16[512,2048]{1,0:T(8,128)(2,1)}, u32[]{:S(2)}) copy-start(bf16[512,2048]{1,0:T(8,128)(2,1)} %refs_0_.3) | copy-start | bytes 6291460
  3.0 0.7 copy-start.6
  3.6 4.7 %copy-start.5 = (bf16[512,2048]{1,0:T(8,128)(2,1)S(1)}, bf16[512,2048]{1,0:T(8,128)(2,1)}, u32[]{:S(2)}) copy-start(bf16[512,2048]{1,0:T(8,128)(2,1)} %refs_0_.3) | copy-start | bytes 6291460
  7.0 40.3 %copy-start.10 = (bf16[8192]{0:T(1024)(128)(2,1)S(1)}, bf16[8192]{0:T(1024)(128)(2,1)}, u32[]{:S(2)}) copy-start(bf16[8192]{0:T(1024)(128)(2,1)} %param.10) | copy-start | bytes 49156
  7.1 76.3 %copy-start.7 = (s32[4]{0:T(128)S(1)}, s32[4]{0:T(128)}, u32[]{:S(2)}) copy-start(s32[4]{0:T(128)} %lengths_ref.15) | copy-start | bytes 52
  7.1 76.3 %copy-start.8 = (f32[1,128]{1,0:T(1,128)S(1)}, f32[1,128]{1,0:T(1,128)}, u32[]{:S(2)}) copy-start(f32[1,128]{1,0:T(1,128)} %constant.14.clone.refs_12_.refs_8_.refs_7_) | copy-start | bytes 1540
  7.1 7.6 %collective-permute-start.1 = (bf16[64,2048]{1,0:T(8,128)(2,1)S(1)}, bf16[64,2048]{1,0:T(8,128)(2,1)S(1)}, u32[]{:S(2)}, u32[]{:S(2)}) collective-permute-start(bf16[64,2048]{1,0:T(8,128)(2,1)S(1)} %bitcast.14), channel_id=1, source_target_pairs={{0,8},{4,12},{8,0},{12,4},{1,9},{5,13},{9,1},{13,5},{2,10},{6,14},... | collective-permute-start | bytes 786440 | tf_op jit(solution)/shard_map/ppermute | solution.py:444
  14.7 6.7 %collective-permute-start.2 = (bf16[64,2048]{1,0:T(8,128)(2,1)S(1)}, bf16[64,2048]{1,0:T(8,128)(2,1)S(1)}, u32[]{:S(2)}, u32[]{:S(2)}) collective-permute-start(bf16[64,2048]{1,0:T(8,128)(2,1)S(1)} %bitcast.13), channel_id=1, source_target_pairs={{0,8},{4,12},{8,0},{12,4},{1,9},{5,13},{9,1},{13,5},{2,10},{6,14},... | collective-permute-start | bytes 786440 | tf_op jit(solution)/shard_map/ppermute | solution.py:444
  16.0 8.2 %collective-permute-start.4 = (bf16[64,2048]{1,0:T(8,128)(2,1)S(1)}, bf16[64,2048]{1,0:T(8,128)(2,1)S(1)}, u32[]{:S(2)}, u32[]{:S(2)}) collective-permute-start(bf16[64,2048]{1,0:T(8,128)(2,1)S(1)} %get-tuple-element.33.refs_0_), channel_id=1, source_target_pairs={{1,2},{2,1},{5,6},{6,5},{9,10},{10,9},{13,14},{14,13},{17,18},{18,... | collective-permute-start | bytes 786440 | tf_op jit(solution)/shard_map/ppermute | solution.py:494
  19.2 6.1 %collective-permute-start.3 = (bf16[64,2048]{1,0:T(8,128)(2,1)S(1)}, bf16[64,2048]{1,0:T(8,128)(2,1)S(1)}, u32[]{:S(2)}, u32[]{:S(2)}) collective-permute-start(bf16[64,2048]{1,0:T(8,128)(2,1)S(1)} %get-tuple-element.33.refs_0_), channel_id=1, source_target_pairs={{0,1},{1,0},{2,3},{3,2},{4,5},{5,4},{6,7},{7,6},{8,9},{9,8},{10,11... | collective-permute-start | bytes 786440 | tf_op jit(solution)/shard_map/ppermute | solution.py:494
  25.3 18.8 %collective-permute-start.5 = (bf16[128,2048]{1,0:T(8,128)(2,1)S(1)}, bf16[128,2048]{1,0:T(8,128)(2,1)S(1)}, u32[]{:S(2)}, u32[]{:S(2)}) collective-permute-start(bf16[128,2048]{1,0:T(8,128)(2,1)S(1)} %bitcast.12), channel_id=1, source_target_pairs={{0,8},{4,12},{8,0},{12,4},{1,9},{5,13},{9,1},{13,5},{2,10},{6,14},... | collective-permute-start | bytes 1572872 | tf_op jit(solution)/shard_map/ppermute | solution.py:444
  25.6 10.6 %collective-permute-start.8 = (bf16[64,2048]{1,0:T(8,128)(2,1)S(1)}, bf16[64,2048]{1,0:T(8,128)(2,1)S(1)}, u32[]{:S(2)}, u32[]{:S(2)}) collective-permute-start(bf16[64,2048]{1,0:T(8,128)(2,1)S(1)} %get-tuple-element.33.refs_0_), channel_id=1, source_target_pairs={{0,2},{1,3},{2,0},{3,1},{4,6},{5,7},{6,4},{7,5},{8,10},{9,11},{10,... | collective-permute-start | bytes 786440 | tf_op jit(solution)/shard_map/ppermute | solution.py:494
  25.8 18.3 %collective-permute-start.7 = (bf16[64,2048]{1,0:T(8,128)(2,1)S(1)}, bf16[64,2048]{1,0:T(8,128)(2,1)S(1)}, u32[]{:S(2)}, u32[]{:S(2)}) collective-permute-start(bf16[64,2048]{1,0:T(8,128)(2,1)S(1)} %get-tuple-element.35.refs_4_), channel_id=1, source_target_pairs={{1,2},{2,1},{5,6},{6,5},{9,10},{10,9},{13,14},{14,13},{17,18},{18,... | collective-permute-start | bytes 786440 | tf_op jit(solution)/shard_map/ppermute | solution.py:494
  29.0 15.1 %collective-permute-start.6 = (bf16[64,2048]{1,0:T(8,128)(2,1)S(1)}, bf16[64,2048]{1,0:T(8,128)(2,1)S(1)}, u32[]{:S(2)}, u32[]{:S(2)}) collective-permute-start(bf16[64,2048]{1,0:T(8,128)(2,1)S(1)} %get-tuple-element.35.refs_4_), channel_id=1, source_target_pairs={{0,1},{1,0},{2,3},{3,2},{4,5},{5,4},{6,7},{7,6},{8,9},{9,8},{10,11... | collective-permute-start | bytes 786440 | tf_op jit(solution)/shard_map/ppermute | solution.py:494
  44.2 37.8 %collective-permute-start.15 = (bf16[128,2048]{1,0:T(8,128)(2,1)S(1)}, bf16[128,2048]{1,0:T(8,128)(2,1)S(1)}, u32[]{:S(2)}, u32[]{:S(2)}) collective-permute-start(bf16[128,2048]{1,0:T(8,128)(2,1)S(1)} %get-tuple-element.43.refs_0_), channel_id=1, source_target_pairs={{0,2},{1,3},{2,0},{3,1},{4,6},{5,7},{6,4},{7,5},{8,10},{9,11},{10,... | collective-permute-start | bytes 1572872 | tf_op jit(solution)/shard_map/ppermute | solution.py:494
  45.0 32.3 %collective-permute-start.10 = (bf16[64,2048]{1,0:T(8,128)(2,1)S(1)}, bf16[64,2048]{1,0:T(8,128)(2,1)S(1)}, u32[]{:S(2)}, u32[]{:S(2)}) collective-permute-start(bf16[64,2048]{1,0:T(8,128)(2,1)S(1)} %get-tuple-element.35.refs_4_), channel_id=1, source_target_pairs={{0,2},{1,3},{2,0},{3,1},{4,6},{5,7},{6,4},{7,5},{8,10},{9,11},{10,... | collective-permute-start | bytes 786440 | tf_op jit(solution)/shard_map/ppermute | solution.py:494
  47.3 56.0 %collective-permute-start.18 = (bf16[128,2048]{1,0:T(8,128)(2,1)S(1)}, bf16[128,2048]{1,0:T(8,128)(2,1)S(1)}, u32[]{:S(2)}, u32[]{:S(2)}) collective-permute-start(bf16[128,2048]{1,0:T(8,128)(2,1)S(1)} %get-tuple-element.43.refs_0_), channel_id=1, source_target_pairs={{1,2},{2,1},{5,6},{6,5},{9,10},{10,9},{13,14},{14,13},{17,18},{18,... | collective-permute-start | bytes 1572872 | tf_op jit(solution)/shard_map/ppermute | solution.py:494
  49.4 53.9 %collective-permute-start.17 = (bf16[128,2048]{1,0:T(8,128)(2,1)S(1)}, bf16[128,2048]{1,0:T(8,128)(2,1)S(1)}, u32[]{:S(2)}, u32[]{:S(2)}) collective-permute-start(bf16[128,2048]{1,0:T(8,128)(2,1)S(1)} %get-tuple-element.43.refs_0_), channel_id=1, source_target_pairs={{0,1},{1,0},{2,3},{3,2},{4,5},{5,4},{6,7},{7,6},{8,9},{9,8},{10,11... | collective-permute-start | bytes 1572872 | tf_op jit(solution)/shard_map/ppermute | solution.py:494
  77.3 21.9 %collective-permute-start.11 = (bf16[64,2048]{1,0:T(8,128)(2,1)S(1)}, bf16[64,2048]{1,0:T(8,128)(2,1)S(1)}, u32[]{:S(2)}, u32[]{:S(2)}) collective-permute-start(bf16[64,2048]{1,0:T(8,128)(2,1)S(1)} %collective-permute-done.10.refs_7_), channel_id=1, source_target_pairs={{2,3},{1,0},{6,7},{5,4},{10,11},{9,8},{14,15},{13,12},{18,19},{17,... | collective-permute-start | bytes 786440 | tf_op jit(solution)/shard_map/ppermute | solution.py:499
  80.7 18.5 %collective-permute-start.9 = (bf16[64,2048]{1,0:T(8,128)(2,1)S(1)}, bf16[64,2048]{1,0:T(8,128)(2,1)S(1)}, u32[]{:S(2)}, u32[]{:S(2)}) collective-permute-start(bf16[64,2048]{1,0:T(8,128)(2,1)S(1)} %get-tuple-element.36.refs_3_), channel_id=1, source_target_pairs={{2,3},{1,0},{6,7},{5,4},{10,11},{9,8},{14,15},{13,12},{18,19},{17,... | collective-permute-start | bytes 786440 | tf_op jit(solution)/shard_map/ppermute | solution.py:499
  82.0 32.0 %collective-permute-start.16 = (bf16[128,2048]{1,0:T(8,128)(2,1)S(1)}, bf16[128,2048]{1,0:T(8,128)(2,1)S(1)}, u32[]{:S(2)}, u32[]{:S(2)}) collective-permute-start(bf16[128,2048]{1,0:T(8,128)(2,1)S(1)} %collective-permute-done.15.refs_3_), channel_id=1, source_target_pairs={{2,3},{1,0},{6,7},{5,4},{10,11},{9,8},{14,15},{13,12},{18,19},{17,... | collective-permute-start | bytes 1572872 | tf_op jit(solution)/shard_map/ppermute | solution.py:499
  83.4 2.2 %copy-start = (bf16[8192,256]{1,0:T(8,128)(2,1)S(1)}, bf16[8192,256]{1,0:T(8,128)(2,1)}, u32[]{:S(2)}) copy-start(bf16[8192,256]{1,0:T(8,128)(2,1)} %refs_3_.3) | copy-start | bytes 12582916
  85.6 2.2 %copy-start.2 = (bf16[8192,256]{1,0:T(8,128)(2,1)S(1)}, bf16[8192,256]{1,0:T(8,128)(2,1)}, u32[]{:S(2)}) copy-start(bf16[8192,256]{1,0:T(8,128)(2,1)} %refs_4_.3) | copy-start | bytes 12582916
  87.7 11.5 %copy-start.1 = (bf16[8192,256]{1,0:T(8,128)(2,1)S(1)}, bf16[8192,256]{1,0:T(8,128)(2,1)}, u32[]{:S(2)}) copy-start(bf16[8192,256]{1,0:T(8,128)(2,1)} %refs_3_.3) | copy-start | bytes 12582916
  87.7 11.5 %copy-start.3 = (bf16[8192,256]{1,0:T(8,128)(2,1)S(1)}, bf16[8192,256]{1,0:T(8,128)(2,1)}, u32[]{:S(2)}) copy-start(bf16[8192,256]{1,0:T(8,128)(2,1)} %refs_4_.3) | copy-start | bytes 12582916
  102.0 19.8 %collective-permute-start.13 = (bf16[128,1536]{1,0:T(8,128)(2,1)S(1)}, bf16[128,1536]{1,0:T(8,128)(2,1)S(1)}, u32[]{:S(2)}, u32[]{:S(2)}) collective-permute-start(bf16[128,1536]{1,0:T(8,128)(2,1)S(1)} %project.5.refs_0_), channel_id=1, source_target_pairs={{0,8},{4,12},{8,0},{12,4},{1,9},{5,13},{9,1},{13,5},{2,10},{6,14},... | collective-permute-start | bytes 1179656 | tf_op jit(solution)/shard_map/ppermute | solution.py:444
  114.1 16.4 %copy-start.9 = (s32[16]{0:T(128)S(1)}, s32[16]{0:T(128)}, u32[]{:S(2)}) copy-start(s32[16]{0:T(128)} %plan_ref.1) | copy-start | bytes 196
  116.8 6.7 %collective-permute-start.20 = (bf16[128,1536]{1,0:T(8,128)(2,1)S(1)}, bf16[128,1536]{1,0:T(8,128)(2,1)S(1)}, u32[]{:S(2)}, u32[]{:S(2)}) collective-permute-start(bf16[128,1536]{1,0:T(8,128)(2,1)S(1)} %project.7.refs_4_), channel_id=1, source_target_pairs={{0,8},{4,12},{8,0},{12,4},{1,9},{5,13},{9,1},{13,5},{2,10},{6,14},... | collective-permute-start | bytes 1179656 | tf_op jit(solution)/shard_map/ppermute | solution.py:444
  117.1 12.0 %collective-permute-start.12 = (bf16[128,1536]{1,0:T(8,128)(2,1)S(1)}, bf16[128,1536]{1,0:T(8,128)(2,1)S(1)}, u32[]{:S(2)}, u32[]{:S(2)}) collective-permute-start(bf16[128,1536]{1,0:T(8,128)(2,1)S(1)} %project.5.refs_0_), channel_id=1, source_target_pairs={{0,4},{4,0},{8,12},{12,8},{1,5},{5,1},{9,13},{13,9},{2,6},{6,2},{1... | collective-permute-start | bytes 1179656 | tf_op jit(solution)/shard_map/ppermute | solution.py:448
  121.8 7.3 %collective-permute-start.14 = (bf16[128,1536]{1,0:T(8,128)(2,1)S(1)}, bf16[128,1536]{1,0:T(8,128)(2,1)S(1)}, u32[]{:S(2)}, u32[]{:S(2)}) collective-permute-start(bf16[128,1536]{1,0:T(8,128)(2,1)S(1)} %collective-permute-done.13.refs_2_), channel_id=1, source_target_pairs={{0,4},{4,0},{8,12},{12,8},{1,5},{5,1},{9,13},{13,9},{2,6},{6,2},{1... | collective-permute-start | bytes 1179656 | tf_op jit(solution)/shard_map/ppermute | solution.py:448
  121.8 7.3 %collective-permute-start.19 = (bf16[128,1536]{1,0:T(8,128)(2,1)S(1)}, bf16[128,1536]{1,0:T(8,128)(2,1)S(1)}, u32[]{:S(2)}, u32[]{:S(2)}) collective-permute-start(bf16[128,1536]{1,0:T(8,128)(2,1)S(1)} %project.7.refs_4_), channel_id=1, source_target_pairs={{0,4},{4,0},{8,12},{12,8},{1,5},{5,1},{9,13},{13,9},{2,6},{6,2},{1... | collective-permute-start | bytes 1179656 | tf_op jit(solution)/shard_map/ppermute | solution.py:448
  123.5 6.9 %collective-permute-start.21 = (bf16[128,1536]{1,0:T(8,128)(2,1)S(1)}, bf16[128,1536]{1,0:T(8,128)(2,1)S(1)}, u32[]{:S(2)}, u32[]{:S(2)}) collective-permute-start(bf16[128,1536]{1,0:T(8,128)(2,1)S(1)} %collective-permute-done.20.refs_6_), channel_id=1, source_target_pairs={{0,4},{4,0},{8,12},{12,8},{1,5},{5,1},{9,13},{13,9},{2,6},{6,2},{1... | collective-permute-start | bytes 1179656 | tf_op jit(solution)/shard_map/ppermute | solution.py:448
